TPU v7x, 128 devices: a whole 4x4x4 slice. The times are simulated.
128 devices in a mesh: fsdp: 16 (over y, x), batch: 8 (over z, core).
Axes of the slice: x: 4, y: 4, z: 4, core: 2. Of those that a mesh axis runs over, the one named last changes fastest.
Arguments:
- inputs: float32 [32768, 1024], P(('fsdp', 'batch')), may hold values from -6 to 6
- cotangent: float32 [32768, 1024], P(('fsdp', 'batch'))
- segment_ids: int32 [32768], P(('fsdp', 'batch')), may hold values from 0 to 4, as said below
- routed: int32 [16, 256], P('fsdp'), may hold values from 0 to 2047, as said below
- qkv_master: float32 [2, 1024, 3072], P(None, ('fsdp', 'batch')), may hold values from -0.1875 to 0.1875
- out_master: float32 [2, 1024, 1024], P(None, ('fsdp', 'batch')), may hold values from -3 to 3
- up_master: float32 [2, 4096, 1024], P(None, ('fsdp', 'batch')), may hold values from -0.1875 to 0.1875
- down_master: float32 [2, 4096, 1024], P(None, ('fsdp', 'batch')), may hold values from -0.09375 to 0.09375
- qkv_moment: float32 [2, 1024, 3072], P(None, ('fsdp', 'batch'))
- out_moment: float32 [2, 1024, 1024], P(None, ('fsdp', 'batch'))
- up_moment: float32 [2, 4096, 1024], P(None, ('fsdp', 'batch'))
- down_moment: float32 [2, 4096, 1024], P(None, ('fsdp', 'batch'))
- router: float32 [1024], replicated, may hold values from -0.1875 to 0.1875
- router_first: float32 [1024], replicated, may hold values from -2560 to 2560
- router_second: float32 [1024], replicated, may hold values from 880803.8 to 3523215.2
Outputs:
- mixed: float32 [32768, 1024], P(('fsdp', 'batch'))
- grad_inputs: float32 [32768, 1024], P(('fsdp', 'batch'))
- new_qkv_moment: float32 [2, 1024, 3072], P(None, ('fsdp', 'batch'))
- new_out_moment: float32 [2, 1024, 1024], P(None, ('fsdp', 'batch'))
- new_up_moment: float32 [2, 4096, 1024], P(None, ('fsdp', 'batch'))
- new_down_moment: float32 [2, 4096, 1024], P(None, ('fsdp', 'batch'))
- new_qkv_master: float32 [2, 1024, 3072], P(None, ('fsdp', 'batch'))
- new_out_master: float32 [2, 1024, 1024], P(None, ('fsdp', 'batch'))
- new_up_master: float32 [2, 4096, 1024], P(None, ('fsdp', 'batch'))
- new_down_master: float32 [2, 4096, 1024], P(None, ('fsdp', 'batch'))
- qkv_copy: bfloat16 [2, 1024, 3072], P(None, ('fsdp', 'batch'))
- out_copy: bfloat16 [2, 1024, 1024], P(None, ('fsdp', 'batch'))
- up_copy: bfloat16 [2, 4096, 1024], P(None, ('fsdp', 'batch'))
- down_copy: bfloat16 [2, 4096, 1024], P(None, ('fsdp', 'batch'))
- new_router: float32 [1024], replicated
- new_router_first: float32 [1024], replicated
- new_router_second: float32 [1024], replicated
Inputs may be any that keep to these rules, and one draw needn't show every extreme that they name: `segment_ids`: within each sequence of 2048 positions the numbers never fall, and one segment covers positions 128 to 1919. `routed`: each row holds 256 distinct positions of its sequence in rising order, among them 0 and 2047.
All inputs are finite; a program needn't handle non-finite values.
Results may differ from a plain program's by a relative error of at most 0.017.
The roundings to bfloat16 on the way count: a program that leaves them out, or rounds other values in their place, can miss the bound.
Values may be sent and summed in bfloat16 or wider, within the bound.
No kernel may reach another device: no remote copies, remote signals or barrier semaphores. Data moves between devices by JAX's collectives and lax.ppermute only.
A program may use at most 384 MiB of HBM per device.

v0:
```python
import math

import jax
import jax.numpy as jnp
from jax import lax
from jax.sharding import PartitionSpec as P

D = 1024
HEADS = 16
HDIM = 64
FF = 4096
NS_ITERS = 2
STEP = 8


EPSILON = 1e-05
SCORE_SCALE = 0.125
NEGATIVE = -1e30
MOMENTUM = 0.95
WEIGHT_DECAY = 0.01
STEP_RATES = (0.15, 1.0, 0.15, 0.15)
NEWTON_A = 3.4445
NEWTON_B = -4.775
NEWTON_C = 2.0315
NEWTON_EPSILON = 1e-07
ADAM_RATE = 0.03
FIRST_DECAY = 0.9
SECOND_DECAY = 0.95
ADAM_EPSILON = 1e-08
HIGHEST = lax.Precision.HIGHEST


def rms_norm(values):
    return values * lax.rsqrt(jnp.mean(values * values, axis=-1, keepdims=True) + EPSILON)


def gelu_tanh(values):
    return jax.nn.gelu(values, approximate=True)


def norm_back(values, grad_normed):
    pull_back = jax.vjp(rms_norm, values)[1]
    return pull_back(grad_normed)[0]


def fetch_weights(masters, layer_index):
    return (
        lax.all_gather(
            masters[0][layer_index].astype(jnp.bfloat16), ("fsdp", "batch"), axis=0, tiled=True
        ),
        lax.all_gather(
            masters[1][layer_index].astype(jnp.bfloat16), ("fsdp", "batch"), axis=0, tiled=True
        ),
        lax.all_gather(
            masters[2][layer_index].astype(jnp.bfloat16), ("fsdp", "batch"), axis=0, tiled=True
        ),
        lax.all_gather(
            masters[3][layer_index].astype(jnp.bfloat16), ("fsdp", "batch"), axis=0, tiled=True
        ),
    )


def reduce_grads(grads):
    return (
        lax.psum_scatter(grads[0], ("fsdp", "batch"), scatter_dimension=0, tiled=True),
        lax.psum_scatter(grads[1], ("fsdp", "batch"), scatter_dimension=0, tiled=True),
        lax.psum_scatter(grads[2], ("fsdp", "batch"), scatter_dimension=0, tiled=True),
        lax.psum_scatter(grads[3], ("fsdp", "batch"), scatter_dimension=0, tiled=True),
    )


def sum_wide(gram_list, extra):
    wide_up, wide_down, summed_extra = lax.psum(
        (gram_list[1], gram_list[2], extra), ("fsdp", "batch")
    )
    return (wide_up, wide_down, summed_extra)


def sum_by_batch(gram_list, extra):
    heads_sum = lax.psum(gram_list[0], "batch")
    wide_up, wide_down, summed_extra = sum_wide(gram_list, extra)
    return ([heads_sum, wide_up, wide_down], summed_extra)


def mask_pairs(raw_scores, query_pos, query_seg, key_pos, key_seg):
    allowed = (key_pos[None, :] <= query_pos[:, None]) & (key_seg[None, :] == query_seg[:, None])
    return jnp.where(allowed[None], raw_scores, NEGATIVE)


def attention_forward(normed, weight_qkv, weight_out, query_pos, query_seg):
    row_count = normed.shape[0]
    projected = jnp.dot(normed, weight_qkv, preferred_element_type=jnp.float32).astype(jnp.bfloat16)
    keys_all, values_all, key_seg = (
        lax.all_gather(projected[:, D : 2 * D], "batch", axis=0, tiled=True),
        lax.all_gather(projected[:, 2 * D :], "batch", axis=0, tiled=True),
        lax.all_gather(query_seg.astype(jnp.bfloat16), "batch", axis=0, tiled=True),
    )
    queries = projected[:, :D].reshape(row_count, HEADS, HDIM)
    keys_heads = keys_all.reshape(-1, HEADS, HDIM)
    values_heads = values_all.reshape(-1, HEADS, HDIM)
    key_seg = key_seg.astype(jnp.float32)
    raw_scores = (
        jnp.einsum("qhd,khd->hqk", queries, keys_heads, preferred_element_type=jnp.float32)
        * SCORE_SCALE
    )
    scores = mask_pairs(raw_scores, query_pos, query_seg, jnp.arange(raw_scores.shape[2]), key_seg)
    row_top = jnp.max(scores, axis=2, keepdims=True)
    exponent = jnp.exp(scores - row_top)
    row_total = jnp.sum(exponent, axis=2, keepdims=True)
    attention_probs = (exponent / row_total).astype(jnp.bfloat16)
    mixed_heads = jnp.einsum(
        "hqk,khd->qhd", attention_probs, values_heads, preferred_element_type=jnp.float32
    )
    mixed_low = mixed_heads.reshape(row_count, D).astype(jnp.bfloat16)
    branch = jnp.einsum("td,od->to", mixed_low, weight_out, preferred_element_type=jnp.float32)
    stored = (projected, keys_heads, values_heads, key_seg, row_top + jnp.log(row_total), mixed_low)
    return (branch, stored)


def attention_backward(normed, weight_qkv, weight_out, query_pos, query_seg, stored, grad_branch):
    projected, keys_heads, values_heads, key_seg, log_total, mixed_low = stored
    row_count = normed.shape[0]
    grad_low = grad_branch.astype(jnp.bfloat16)
    grad_out_weight = jnp.einsum(
        "to,td->od", grad_low, mixed_low, preferred_element_type=jnp.float32
    )
    grad_flat = jnp.einsum(
        "to,od->td", grad_low, weight_out, preferred_element_type=jnp.float32
    ).astype(jnp.bfloat16)
    grad_mixed = grad_flat.reshape(row_count, HEADS, HDIM)
    queries = projected[:, :D].reshape(row_count, HEADS, HDIM)
    raw_scores = (
        jnp.einsum("qhd,khd->hqk", queries, keys_heads, preferred_element_type=jnp.float32)
        * SCORE_SCALE
    )
    scores = mask_pairs(raw_scores, query_pos, query_seg, jnp.arange(raw_scores.shape[2]), key_seg)
    attention_probs = jnp.exp(scores - log_total)
    grad_probs = jnp.einsum(
        "qhd,khd->hqk", grad_mixed, values_heads, preferred_element_type=jnp.float32
    )
    inner_sum = jnp.sum(attention_probs * grad_probs, axis=2, keepdims=True)
    grad_scores = (attention_probs * (grad_probs - inner_sum)).astype(jnp.bfloat16) * SCORE_SCALE
    grad_queries = jnp.einsum(
        "hqk,khd->qhd", grad_scores, keys_heads, preferred_element_type=jnp.float32
    ).reshape(row_count, D)
    probs_low = attention_probs.astype(jnp.bfloat16)
    grad_keys = jnp.einsum(
        "hqk,qhd->khd", grad_scores, queries, preferred_element_type=jnp.float32
    ).reshape(row_count * lax.axis_size("batch"), D)
    grad_values = jnp.einsum(
        "hqk,qhd->khd", probs_low, grad_mixed, preferred_element_type=jnp.float32
    ).reshape(row_count * lax.axis_size("batch"), D)
    key_grads = lax.psum_scatter(
        jnp.concatenate([grad_keys, grad_values], axis=1), "batch", scatter_dimension=0, tiled=True
    )
    grad_projected = jnp.concatenate([grad_queries, key_grads], axis=1).astype(jnp.bfloat16)
    grad_qkv_weight = jnp.einsum(
        "td,tc->dc", normed, grad_projected, preferred_element_type=jnp.float32
    )
    grad_normed = jnp.einsum(
        "tc,dc->td", grad_projected, weight_qkv, preferred_element_type=jnp.float32
    )
    return (grad_normed, grad_qkv_weight, grad_out_weight)


def feed_forward(normed, weight_up, weight_down):
    hidden = jnp.einsum("td,fd->tf", normed, weight_up, preferred_element_type=jnp.float32)
    active = gelu_tanh(hidden).astype(jnp.bfloat16)
    branch = jnp.dot(active, weight_down, preferred_element_type=jnp.float32)
    return (branch, (hidden, active))


def feed_backward(normed, weight_up, weight_down, stored, grad_branch):
    hidden, active = stored
    grad_low = grad_branch.astype(jnp.bfloat16)
    grad_down = jnp.einsum("tf,td->fd", active, grad_low, preferred_element_type=jnp.float32)
    grad_active = jnp.einsum("td,fd->tf", grad_low, weight_down, preferred_element_type=jnp.float32)
    pull_back = jax.vjp(gelu_tanh, hidden)[1]
    grad_hidden = pull_back(grad_active)[0].astype(jnp.bfloat16)
    grad_up = jnp.einsum("tf,td->fd", grad_hidden, normed, preferred_element_type=jnp.float32)
    grad_normed = jnp.dot(grad_hidden, weight_up, preferred_element_type=jnp.float32)
    return (grad_normed, grad_up, grad_down)


def block_forward(inputs, normed, weights, query_pos, query_seg):
    normed_low = normed.astype(jnp.bfloat16)
    attended, attn_state = attention_forward(
        normed_low, weights[0], weights[1], query_pos, query_seg
    )
    middle = inputs + attended
    normed_two = rms_norm(middle).astype(jnp.bfloat16)
    fed_branch, feed_state = feed_forward(normed_two, weights[2], weights[3])
    return (attended, middle, fed_branch, (normed_low, attn_state, normed_two, feed_state))


def block_backward(
    weights, query_pos, query_seg, middle, stored, grad_middle, grad_fed, grad_extra
):
    normed_low, attn_state, normed_two, feed_state = stored
    grad_two, grad_up, grad_down = feed_backward(
        normed_two, weights[2], weights[3], feed_state, grad_fed
    )
    grad_mid = grad_middle + norm_back(middle, grad_two)
    grad_normed, grad_qkv, grad_out = attention_backward(
        normed_low, weights[0], weights[1], query_pos, query_seg, attn_state, grad_mid + grad_extra
    )
    return (grad_mid, grad_normed, (grad_qkv, grad_out, grad_up, grad_down))


def group_heads(qkv_part, out_part):
    layer_count, row_count = (qkv_part.shape[0], qkv_part.shape[1])
    joined = jnp.concatenate(
        [
            qkv_part.reshape(layer_count, row_count, 3 * HEADS, HDIM),
            out_part.reshape(layer_count, row_count, HEADS, HDIM),
        ],
        axis=2,
    )
    return jnp.transpose(joined, (1, 0, 2, 3)).reshape(row_count, layer_count * 4 * HEADS, HDIM)


def split_heads(grouped, layer_count):
    row_count = grouped.shape[0]
    blocks = jnp.transpose(grouped.reshape(row_count, layer_count, 4 * HEADS, HDIM), (1, 0, 2, 3))
    return (
        blocks[:, :, : 3 * HEADS].reshape(layer_count, row_count, 3 * D),
        blocks[:, :, 3 * HEADS :].reshape(layer_count, row_count, D),
    )


def newton_step(matrix, gram_sum):
    product = jnp.einsum("rgb,gbc->rgc", matrix, gram_sum, precision=HIGHEST)
    return (
        NEWTON_A * matrix
        + NEWTON_B * product
        + NEWTON_C * jnp.einsum("rgb,gbc->rgc", product, gram_sum, precision=HIGHEST)
    )


def newton(grouped, extra, sum_grams):
    total_extra = extra
    for iteration in range(NS_ITERS):
        local_grams = [
            jnp.einsum("rgb,rgc->gbc", matrix, matrix, precision=HIGHEST) for matrix in grouped
        ]
        carried = extra if iteration == 0 else jnp.zeros_like(extra)
        gram_sums, summed_extra = sum_grams(local_grams, carried)
        if iteration == 0:
            total_extra = summed_extra
            norm_scales = [
                jnp.sqrt(jnp.trace(gram_sum, axis1=1, axis2=2)) + NEWTON_EPSILON
                for gram_sum in gram_sums
            ]
            grouped = [
                matrix / norm_scale[None, :, None]
                for matrix, norm_scale in zip(grouped, norm_scales)
            ]
            gram_sums = [
                gram_sum / (norm_scale * norm_scale)[:, None, None]
                for gram_sum, norm_scale in zip(gram_sums, norm_scales)
            ]
        grouped = [newton_step(matrix, gram_sum) for matrix, gram_sum in zip(grouped, gram_sums)]
    return (grouped, total_extra)


def body(
    inputs,
    cotangent,
    segment_ids,
    routed,
    qkv_master,
    out_master,
    up_master,
    down_master,
    qkv_moment,
    out_moment,
    up_moment,
    down_moment,
    router,
    router_first,
    router_second,
):
    masters = (qkv_master, out_master, up_master, down_master)
    moments = (qkv_moment, out_moment, up_moment, down_moment)
    widths = (HDIM, HDIM, D, D)
    full_rows = (D, D, FF, FF)
    token_count = inputs.shape[0]
    slot_count = routed.shape[1] // lax.axis_size("batch")
    batch_index = lax.axis_index("batch")
    token_pos = batch_index * token_count + jnp.arange(token_count)
    slot_pos = batch_index * slot_count + jnp.arange(slot_count)
    segment = segment_ids.astype(jnp.float32)
    local_index = routed[0] - batch_index * token_count
    is_mine = (local_index >= 0) & (local_index < token_count)
    safe_index = jnp.clip(local_index, 0, token_count - 1)
    dense_weights = fetch_weights(masters, 0)
    attended, middle, fed_branch, unused_state = block_forward(
        inputs, rms_norm(inputs), dense_weights, token_pos, segment
    )
    hidden = middle + fed_branch
    send_rows = jnp.where(is_mine[:, None], jnp.take(hidden, safe_index, axis=0), 0.0)
    send_segment = jnp.where(is_mine, jnp.take(segment, safe_index), 0.0)
    send_grads = jnp.where(is_mine[:, None], jnp.take(cotangent, safe_index, axis=0), 0.0)
    slot_rows, slot_segment, slot_grads = (
        lax.psum_scatter(send_rows, "batch", scatter_dimension=0, tiled=True),
        lax.psum_scatter(send_segment, "batch", scatter_dimension=0, tiled=True),
        lax.psum_scatter(send_grads, "batch", scatter_dimension=0, tiled=True),
    )
    routed_weights = fetch_weights(masters, 1)
    slot_normed = rms_norm(slot_rows)
    gate_values = jnp.dot(slot_normed, router, precision=HIGHEST)
    routed_attended, routed_middle, routed_fed, routed_state = block_forward(
        slot_rows, slot_normed, routed_weights, slot_pos, slot_segment
    )
    routed_branch = routed_attended + routed_fed
    update_rows = lax.all_gather(gate_values[:, None] * routed_branch, "batch", axis=0, tiled=True)
    mixed = hidden.at[safe_index].add(jnp.where(is_mine[:, None], update_rows, 0.0))
    gate_grads = jnp.sum(slot_grads * routed_branch, axis=1)
    branch_grads = gate_values[:, None] * slot_grads
    routed_mid_grads, routed_normed_grads, routed_weight_grads = block_backward(
        routed_weights,
        slot_pos,
        slot_segment,
        routed_middle,
        routed_state,
        jnp.zeros_like(branch_grads),
        branch_grads,
        branch_grads,
    )
    router_grad = jnp.dot(gate_grads, slot_normed, precision=HIGHEST)
    slot_input_grads = routed_mid_grads + norm_back(
        slot_rows, routed_normed_grads + gate_grads[:, None] * router[None, :]
    )
    returned = lax.all_gather(slot_input_grads, "batch", axis=0, tiled=True)
    hidden_grads = cotangent.at[safe_index].add(jnp.where(is_mine[:, None], returned, 0.0))
    routed_shards = reduce_grads(routed_weight_grads)
    routed_moments = [
        MOMENTUM * moments[index_type][1:2] + routed_shards[index_type][None]
        for index_type in range(4)
    ]
    back_weights = fetch_weights(masters, 0)
    attended, middle, fed_branch, dense_state = block_forward(
        inputs, rms_norm(inputs), back_weights, token_pos, segment
    )
    dense_mid_grads, dense_normed_grads, dense_weight_grads = block_backward(
        back_weights,
        token_pos,
        segment,
        middle,
        dense_state,
        hidden_grads,
        hidden_grads,
        jnp.zeros_like(hidden_grads),
    )
    grad_inputs = dense_mid_grads + norm_back(inputs, dense_normed_grads)
    dense_shards = reduce_grads(dense_weight_grads)
    dense_moments = [
        MOMENTUM * moments[index_type][0:1] + dense_shards[index_type][None]
        for index_type in range(4)
    ]
    new_moments = [
        jnp.concatenate([dense_moments[index_type], routed_moments[index_type]], axis=0)
        for index_type in range(4)
    ]
    layer_count = new_moments[0].shape[0]
    heads_moment = group_heads(new_moments[0], new_moments[1])
    wide_up = jnp.transpose(new_moments[2], (1, 0, 2))
    wide_down = jnp.transpose(new_moments[3], (1, 0, 2))
    owned = lax.all_to_all(heads_moment, "fsdp", split_axis=1, concat_axis=0, tiled=True)
    results, router_total = newton([owned, wide_up, wide_down], router_grad, sum_by_batch)
    heads_ortho = lax.all_to_all(results[0], "fsdp", split_axis=0, concat_axis=1, tiled=True)
    qkv_ortho, out_ortho = split_heads(heads_ortho, layer_count)
    orthos = [
        qkv_ortho,
        out_ortho,
        jnp.transpose(results[1], (1, 0, 2)),
        jnp.transpose(results[2], (1, 0, 2)),
    ]
    new_masters = []
    for index_type in range(4):
        rate = STEP_RATES[index_type]
        factor = 0.2 * math.sqrt(max(full_rows[index_type], widths[index_type]))
        new_masters.append(
            masters[index_type] * (1.0 - rate * WEIGHT_DECAY) - rate * factor * orthos[index_type]
        )
    first_new = FIRST_DECAY * router_first + (1.0 - FIRST_DECAY) * router_total
    second_new = SECOND_DECAY * router_second + (1.0 - SECOND_DECAY) * router_total * router_total
    corrected_first = first_new / (1.0 - FIRST_DECAY**STEP)
    corrected_second = second_new / (1.0 - SECOND_DECAY**STEP)
    router_new = router * (1.0 - ADAM_RATE * WEIGHT_DECAY) - ADAM_RATE * corrected_first / (
        jnp.sqrt(corrected_second) + ADAM_EPSILON
    )
    return (
        mixed,
        grad_inputs,
        new_moments[0],
        new_moments[1],
        new_moments[2],
        new_moments[3],
        new_masters[0],
        new_masters[1],
        new_masters[2],
        new_masters[3],
        new_masters[0].astype(jnp.bfloat16),
        new_masters[1].astype(jnp.bfloat16),
        new_masters[2].astype(jnp.bfloat16),
        new_masters[3].astype(jnp.bfloat16),
        router_new,
        first_new,
        second_new,
    )


def solution(mesh):
    placed = (
        P(("fsdp", "batch"), None),
        P(("fsdp", "batch"), None),
        P(("fsdp", "batch")),
        P("fsdp", None),
        P(None, ("fsdp", "batch"), None),
        P(None, ("fsdp", "batch"), None),
        P(None, ("fsdp", "batch"), None),
        P(None, ("fsdp", "batch"), None),
        P(None, ("fsdp", "batch"), None),
        P(None, ("fsdp", "batch"), None),
        P(None, ("fsdp", "batch"), None),
        P(None, ("fsdp", "batch"), None),
        P(),
        P(),
        P(),
    )
    return jax.shard_map(
        body,
        mesh=mesh,
        in_specs=placed,
        out_specs=(
            P(("fsdp", "batch"), None),
            P(("fsdp", "batch"), None),
            P(None, ("fsdp", "batch"), None),
            P(None, ("fsdp", "batch"), None),
            P(None, ("fsdp", "batch"), None),
            P(None, ("fsdp", "batch"), None),
            P(None, ("fsdp", "batch"), None),
            P(None, ("fsdp", "batch"), None),
            P(None, ("fsdp", "batch"), None),
            P(None, ("fsdp", "batch"), None),
            P(None, ("fsdp", "batch"), None),
            P(None, ("fsdp", "batch"), None),
            P(None, ("fsdp", "batch"), None),
            P(None, ("fsdp", "batch"), None),
            P(),
            P(),
            P(),
        ),
        check_vma=False,
    )
```

profile of v0, /device:TPU:1, one launch (start us, length us, event | category | flops | bytes accessed | tf_op | source)
XLA Modules:
  0.0 5924.4 jit_solution(15292321745106573196)
XLA Ops:
  12.1 71.3 %all-gather.30.cloned.1.call-done = bf16[1,1024,3072]{2,1,0:T(8,128)(2,1)} async-done(((bf16[1,8,3072]{2,1,0:T(8,128)(2,1)}), bf16[1,1024,3072]{2,1,0:T(8,128)(2,1)}) %all-gather.30.cloned.1.call-update) | async-done | bytes 6291472 | tf_op jit(solution)/shard_map/all_gather | solution.py:48
  126.2 27.4 all-gather.22.cloned.1.call-done
  160.1 16.2 fusion.226
  189.9 16.2 fusion.92
  206.1 16.2 all-gather.32.cloned.1.call-done
  225.0 68.3 %all-gather.34.cloned.1.call-done = bf16[1,4096,1024]{2,1,0:T(8,128)(2,1)} async-done(((bf16[1,32,1024]{2,1,0:T(8,128)(2,1)}), bf16[1,4096,1024]{2,1,0:T(8,128)(2,1)}) %all-gather.34.cloned.1.call-update) | async-done | bytes 8388624 | tf_op jit(solution)/shard_map/all_gather | solution.py:54
  301.1 63.3 %all-gather.36.cloned.1.call-done = bf16[1,4096,1024]{2,1,0:T(8,128)(2,1)} async-done(((bf16[1,32,1024]{2,1,0:T(8,128)(2,1)}), bf16[1,4096,1024]{2,1,0:T(8,128)(2,1)}) %all-gather.36.cloned.1.call-update) | async-done | bytes 8388624 | tf_op jit(solution)/shard_map/all_gather | solution.py:57
  408.5 68.9 %all-gather.38.cloned.1.call-done = bf16[1,1024,3072]{2,1,0:T(8,128)(2,1)} async-done(((bf16[1,8,3072]{2,1,0:T(8,128)(2,1)}), bf16[1,1024,3072]{2,1,0:T(8,128)(2,1)}) %all-gather.38.cloned.1.call-update) | async-done | bytes 6291472 | tf_op jit(solution)/shard_map/all_gather | solution.py:48
  494.8 14.7 all_gather.63
  516.9 27.2 all-gather.40.cloned.1.call-done
  548.6 66.6 %all-gather.42.cloned.1.call-done = bf16[1,4096,1024]{2,1,0:T(8,128)(2,1)} async-done(((bf16[1,32,1024]{2,1,0:T(8,128)(2,1)}), bf16[1,4096,1024]{2,1,0:T(8,128)(2,1)}) %all-gather.42.cloned.1.call-update) | async-done | bytes 8388624 | tf_op jit(solution)/shard_map/all_gather | solution.py:54
  621.1 65.3 %all-gather.44.cloned.1.call-done = bf16[1,4096,1024]{2,1,0:T(8,128)(2,1)} async-done(((bf16[1,32,1024]{2,1,0:T(8,128)(2,1)}), bf16[1,4096,1024]{2,1,0:T(8,128)(2,1)}) %all-gather.44.cloned.1.call-update) | async-done | bytes 8388624 | tf_op jit(solution)/shard_map/all_gather | solution.py:57
  686.4 29.1 reduce-scatter.17.cloned.1.call-done
  754.8 26.6 reduce-scatter.37.cloned.1.call-done
  798.0 17.5 all-gather.28.cloned.1.call-done
  870.5 15.5 fusion.230
  886.0 46.4 fusion.12
  932.4 17.0 fusion.7
  961.4 515.8 %reduce-scatter.35.cloned.1.call-done = f32[32,1024]{1,0:T(8,128)} async-done(((f32[4096,1024]{1,0:T(8,128)}), f32[32,1024]{1,0:T(8,128)}) %reduce-scatter.35.cloned.1.call-update) | async-done | bytes 131088 | tf_op jit(solution)/shard_map/reduce_scatter | solution.py:68
  1477.3 662.9 %reduce-scatter.33.cloned.1.call-done = f32[32,1024]{1,0:T(8,128)} async-done(((f32[4096,1024]{1,0:T(8,128)}), f32[32,1024]{1,0:T(8,128)}) %reduce-scatter.33.cloned.1.call-update) | async-done | bytes 131088 | tf_op jit(solution)/shard_map/reduce_scatter | solution.py:68
  2141.2 661.8 %reduce-scatter.31.cloned.1.call-done = f32[32,1024]{1,0:T(8,128)} async-done(((f32[4096,1024]{1,0:T(8,128)}), f32[32,1024]{1,0:T(8,128)}) %reduce-scatter.31.cloned.1.call-update) | async-done | bytes 131088 | tf_op jit(solution)/shard_map/reduce_scatter | solution.py:67
  2803.0 662.9 %reduce-scatter.29.cloned.1.call-done = f32[32,1024]{1,0:T(8,128)} async-done(((f32[4096,1024]{1,0:T(8,128)}), f32[32,1024]{1,0:T(8,128)}) %reduce-scatter.29.cloned.1.call-update) | async-done | bytes 131088 | tf_op jit(solution)/shard_map/reduce_scatter | solution.py:67
  3498.7 48.2 fusion.87
  3570.3 212.6 %all-reduce.15.cloned.1.call-done = (f32[2,1024,1024]{2,1,0:T(8,128)}, f32[2,1024,1024]{2,1,0:T(8,128)}) async-done(((f32[2,1024,1024]{2,1,0:T(8,128)}, f32[2,1024,1024]{2,1,0:T(8,128)}), (f32[2,1024,1024]{2,1,0:T(8,128)}, f32[2,1024,1024]{2,1,0:T(8,128)})) %all-reduce.15.cloned.1.call-update) | async-done | bytes 16777232 | tf_op jit(solution)/shard_map/psum | solution.py:73
  3835.9 65.2 %psum.55 = f32[1024]{0:T(1024)S(1)} all-reduce(f32[1024]{0:T(1024)} %bitcast.318), channel_id=1, replica_groups=mesh['fsdp'=16,'batch'=8] {'fsdp','batch'}, use_global_device_ids=true, to_apply=%region_39.41 | all-reduce | flops 1024 | bytes 8192 | tf_op jit(solution)/shard_map/psum | solution.py:73
  3906.4 541.1 %reduce-scatter.27.cloned.1.call-done = f32[8,1024]{1,0:T(8,128)} async-done(((f32[1024,1024]{1,0:T(8,128)}), f32[8,1024]{1,0:T(8,128)}) %reduce-scatter.27.cloned.1.call-update) | async-done | bytes 32784 | tf_op jit(solution)/shard_map/reduce_scatter | solution.py:66
  4447.5 640.4 %reduce-scatter.25.cloned.1.call-done = f32[8,1024]{1,0:T(8,128)} async-done(((f32[1024,1024]{1,0:T(8,128)}), f32[8,1024]{1,0:T(8,128)}) %reduce-scatter.25.cloned.1.call-update) | async-done | bytes 32784 | tf_op jit(solution)/shard_map/reduce_scatter | solution.py:66
  5099.0 214.9 %reduce-scatter.23.cloned.1.call-done = f32[8,3072]{1,0:T(8,128)} async-done(((f32[1024,3072]{1,0:T(8,128)}), f32[8,3072]{1,0:T(8,128)}) %reduce-scatter.23.cloned.1.call-update) | async-done | bytes 98320 | tf_op jit(solution)/shard_map/reduce_scatter | solution.py:65
  5313.9 225.0 %reduce-scatter.21.cloned.1.call-done = f32[8,3072]{1,0:T(8,128)} async-done(((f32[1024,3072]{1,0:T(8,128)}), f32[8,3072]{1,0:T(8,128)}) %reduce-scatter.21.cloned.1.call-update) | async-done | bytes 98320 | tf_op jit(solution)/shard_map/reduce_scatter | solution.py:65
  5547.8 214.1 %all-reduce.13.cloned.1.call-done = (f32[2,1024,1024]{2,1,0:T(8,128)}, f32[2,1024,1024]{2,1,0:T(8,128)}) async-done(((f32[2,1024,1024]{2,1,0:T(8,128)}, f32[2,1024,1024]{2,1,0:T(8,128)}), (f32[2,1024,1024]{2,1,0:T(8,128)}, f32[2,1024,1024]{2,1,0:T(8,128)})) %all-reduce.13.cloned.1.call-update) | async-done | bytes 16777232 | tf_op jit(solution)/shard_map/psum | solution.py:73
  5781.5 48.3 all-reduce.9.cloned.1.call-done
  5842.9 51.8 all-reduce.11.cloned.1.call-done
  (405 shorter events, 468.4 us)
Async XLA Ops:
  7.2 76.3 %all-gather.30.cloned.1.call-start = ((), (), s32[]{:S(2)}) async-start(), calls=%async_computation.31 | async-start | bytes 6340608 | tf_op jit(solution)/shard_map/all_gather | solution.py:48
  10.1 109.6 %all-gather.24.cloned.1.call-start = ((), (), s32[]{:S(2)}) async-start(), calls=%async_computation.15 | async-start | bytes 4718592 | tf_op jit(solution)/shard_map/all_gather | solution.py:94
  89.6 64.0 %all-gather.22.cloned.1.call-start = ((), (), s32[]{:S(2)}) async-start(), calls=%async_computation.14 | async-start | bytes 4718592 | tf_op jit(solution)/shard_map/all_gather | solution.py:95
  90.3 132.0 %all-gather.32.cloned.1.call-start = ((), (), s32[]{:S(2)}) async-start(), calls=%async_computation.32 | async-start | bytes 2113536 | tf_op jit(solution)/shard_map/all_gather | solution.py:51
  91.0 202.3 %all-gather.34.cloned.1.call-start = ((), (), s32[]{:S(2)}) async-start(), calls=%async_computation.33 | async-start | bytes 8454144 | tf_op jit(solution)/shard_map/all_gather | solution.py:54
  91.8 272.6 %all-gather.36.cloned.1.call-start = ((), (), s32[]{:S(2)}) async-start(), calls=%async_computation.34 | async-start | bytes 8454144 | tf_op jit(solution)/shard_map/all_gather | solution.py:57
  92.5 314.9 %reduce-scatter.15.cloned.1.call-start = ((), (), s32[]{:S(2)}) async-start(), calls=%async_computation.16 | async-start | bytes 1179648 | tf_op jit(solution)/shard_map/reduce_scatter | solution.py:305
  377.1 100.4 %all-gather.38.cloned.1.call-start = ((), (), s32[]{:S(2)}) async-start(), calls=%async_computation.35 | async-start | bytes 6340608 | tf_op jit(solution)/shard_map/all_gather | solution.py:48
  377.8 166.4 %all-gather.40.cloned.1.call-start = ((), (), s32[]{:S(2)}) async-start(), calls=%async_computation.36 | async-start | bytes 2113536 | tf_op jit(solution)/shard_map/all_gather | solution.py:51
  378.6 236.6 %all-gather.42.cloned.1.call-start = ((), (), s32[]{:S(2)}) async-start(), calls=%async_computation.37 | async-start | bytes 8454144 | tf_op jit(solution)/shard_map/all_gather | solution.py:54
  379.1 307.3 %all-gather.44.cloned.1.call-start = ((), (), s32[]{:S(2)}) async-start(), calls=%async_computation.38 | async-start | bytes 8454144 | tf_op jit(solution)/shard_map/all_gather | solution.py:57
  379.9 335.6 %reduce-scatter.17.cloned.1.call-start = ((), (), s32[]{:S(2)}) async-start(), calls=%async_computation.18 | async-start | bytes 1179648 | tf_op jit(solution)/shard_map/reduce_scatter | solution.py:307
  407.3 374.0 %reduce-scatter.37.cloned.1.call-start = ((), (), s32[]{:S(2)}) async-start(), calls=%async_computation.39 | async-start | bytes 2359296 | tf_op jit(solution)/shard_map/reduce_scatter | solution.py:153
  748.8 66.6 %all-gather.28.cloned.1.call-start = ((), (), s32[]{:S(2)}) async-start(), calls=%async_computation.19 | async-start | bytes 1179648 | tf_op jit(solution)/shard_map/all_gather | solution.py:334
  789.6 687.7 %reduce-scatter.35.cloned.1.call-start = ((), (), s32[]{:S(2)}) async-start(), calls=%async_computation.28 | async-start | bytes 16908288 | tf_op jit(solution)/shard_map/reduce_scatter | solution.py:68
  797.9 1342.2 %reduce-scatter.33.cloned.1.call-start = ((), (), s32[]{:S(2)}) async-start(), calls=%async_computation.27 | async-start | bytes 16908288 | tf_op jit(solution)/shard_map/reduce_scatter | solution.py:68
  830.1 1973.0 %reduce-scatter.31.cloned.1.call-start = ((), (), s32[]{:S(2)}) async-start(), calls=%async_computation.26 | async-start | bytes 16908288 | tf_op jit(solution)/shard_map/reduce_scatter | solution.py:67
  839.2 2626.7 %reduce-scatter.29.cloned.1.call-start = ((), (), s32[]{:S(2)}) async-start(), calls=%async_computation.25 | async-start | bytes 16908288 | tf_op jit(solution)/shard_map/reduce_scatter | solution.py:67
  860.7 2699.6 %reduce-scatter.19.cloned.1.call-start = ((), (), s32[]{:S(2)}) async-start(), calls=%async_computation.20 | async-start | bytes 18874368 | tf_op jit(solution)/shard_map/reduce_scatter | solution.py:153
  961.2 2504.8 %copy-start.40 = (f32[2,32,1024]{2,1,0:T(8,128)S(1)}, f32[2,32,1024]{2,1,0:T(8,128)}, u32[]{:S(2)}) copy-start(f32[2,32,1024]{2,1,0:T(8,128)} %param.27) | copy-start | bytes 786436
  961.2 2821.7 %all-reduce.15.cloned.1.call-start = ((), (), s32[]{:S(2)}) async-start(), calls=%async_computation.41 | async-start | bytes 33554432 | tf_op jit(solution)/shard_map/psum | solution.py:73
  2141.2 1670.9 %copy-start.17 = (f32[2,32,1024]{2,1,0:T(8,128)}, f32[2,32,1024]{2,1,0:T(8,128)S(1)}, u32[]{:S(2)}) copy-start(f32[2,32,1024]{2,1,0:T(8,128)S(1)} %pad_maximum_fusion.6) | copy-start | bytes 786436
  3485.0 417.5 %all-gather.26.cloned.1.call-start = ((), (), s32[]{:S(2)}) async-start(), calls=%async_computation.17 | async-start | bytes 1179648 | tf_op jit(solution)/shard_map/all_gather | solution.py:316
  3485.7 961.7 %reduce-scatter.27.cloned.1.call-start = ((), (), s32[]{:S(2)}) async-start(), calls=%async_computation.24 | async-start | bytes 4227072 | tf_op jit(solution)/shard_map/reduce_scatter | solution.py:66
  3488.6 1599.3 %reduce-scatter.25.cloned.1.call-start = ((), (), s32[]{:S(2)}) async-start(), calls=%async_computation.23 | async-start | bytes 4227072 | tf_op jit(solution)/shard_map/reduce_scatter | solution.py:66
  3491.4 1822.5 %reduce-scatter.23.cloned.1.call-start = ((), (), s32[]{:S(2)}) async-start(), calls=%async_computation.22 | async-start | bytes 12681216 | tf_op jit(solution)/shard_map/reduce_scatter | solution.py:65
  3498.1 2040.8 %reduce-scatter.21.cloned.1.call-start = ((), (), s32[]{:S(2)}) async-start(), calls=%async_computation.21 | async-start | bytes 12681216 | tf_op jit(solution)/shard_map/reduce_scatter | solution.py:65
  3569.5 2192.3 %all-reduce.13.cloned.1.call-start = ((), (), s32[]{:S(2)}) async-start(), calls=%async_computation.40 | async-start | bytes 33554432 | tf_op jit(solution)/shard_map/psum | solution.py:73
  5543.5 226.2 %all-to-all-start = ((f32[16,1,4096]{2,1,0:T(1,128)}), f32[16,1,4096]{2,1,0:T(1,128)S(1)}, u32[]{:S(2)}, u32[]{:S(2)}) async-start(f32[16,1,4096]{2,1,0:T(1,128)} %reshape.479), calls=%async_computation.11 | async-start | bytes 524288 | tf_op jit(solution)/shard_map/all_to_all | solution.py:369
  5547.7 282.0 %all-reduce.9.cloned.1.call-start = ((), (), s32[]{:S(2)}) async-start(), calls=%async_computation.29 | async-start | bytes 524288 | tf_op jit(solution)/shard_map/psum | solution.py:80
  5773.3 121.5 %all-reduce.11.cloned.1.call-start = ((), (), s32[]{:S(2)}) async-start(), calls=%async_computation.30 | async-start | bytes 524288 | tf_op jit(solution)/shard_map/psum | solution.py:80
  5899.1 14.9 all-to-all-start.1
  (87 other events, 7901.3 us)
Sparse Core Ops, SparseCore 0:
  11.6 71.8 all-gather.29
  89.7 29.9 all-gather.23
  121.4 32.1 all-gather.21
  157.1 65.1 all-gather.31
  225.7 67.5 all-gather.33
  296.7 67.6 all-gather.35
  377.2 26.3 reduce-scatter.14
  407.1 70.3 all-gather.37
  481.2 62.9 all-gather.39
  547.6 67.5 all-gather.41
  618.7 67.6 all-gather.43
  689.2 26.2 reduce-scatter.16
  749.0 32.3 reduce-scatter.36
  789.7 25.7 all-gather.27
  817.7 659.5 reduce-scatter.34
  1479.5 660.6 reduce-scatter.32
  2142.4 660.6 reduce-scatter.30
  2805.3 660.6 reduce-scatter.28
  3468.4 91.8 reduce-scatter.18
  3565.8 216.9 all-reduce.14
  3785.3 22.3 all-gather.25
  3810.1 637.3 reduce-scatter.26
  4449.8 637.9 reduce-scatter.24
  5093.4 220.4 reduce-scatter.22
  5319.7 219.1 reduce-scatter.20
  5545.4 216.3 all-reduce.12
  5773.4 56.2 all-reduce.8
  5835.7 59.0 all-reduce.10
where the time goes:
time: 5940 us; the launch traced here: 5920 us
  waiting for transfers between devices  5230 us (88%)
  matrix products  413 us (7%)
  blocking collectives  127 us (2%)
  other arithmetic  74.7 us (1%)
    reduce_scatter x2, waiting for transfers between devices, reduce_grads(): lax.psum_scatter(grads[2], ('fsdp', 'batch'), scatter_dimension=0, tiled=...  1320 us
    reduce_scatter x2, waiting for transfers between devices, reduce_grads(): lax.psum_scatter(grads[1], ('fsdp', 'batch'), scatter_dimension=0, tiled=...  1180 us
    reduce_scatter x2, waiting for transfers between devices, reduce_grads(): lax.psum_scatter(grads[3], ('fsdp', 'batch'), scatter_dimension=0, tiled=...  1180 us
    reduce_scatter x2, waiting for transfers between devices, reduce_grads(): lax.psum_scatter(grads[0], ('fsdp', 'batch'), scatter_dimension=0, tiled=...  440 us
    psum x2, waiting for transfers between devices, sum_wide(): lax.psum((gram_list[1], gram_list[2], extra), ('fsdp', 'batch'))  427 us
    all_gather x2, waiting for transfers between devices, fetch_weights(): lax.all_gather(masters[0][layer_index].astype(jnp.bfloat16), ('fsdp', 'ba...  140 us
    all_gather x2, waiting for transfers between devices, fetch_weights(): lax.all_gather(masters[2][layer_index].astype(jnp.bfloat16), ('fsdp', 'ba...  135 us
    all_gather x2, waiting for transfers between devices, fetch_weights(): lax.all_gather(masters[3][layer_index].astype(jnp.bfloat16), ('fsdp', 'ba...  129 us
  transfers between devices with their start and end apart: 30, of which 26 were waited for; matrix products, arithmetic and copies ran while one was open for 8% of the time, Pallas kernels for 0%

commit v1 on v0

v1 whole, which is shorter than its diff:
```python
import math

import jax
import jax.numpy as jnp
from jax import lax
from jax.sharding import Mesh
from jax.sharding import PartitionSpec as P

D = 1024
HEADS = 16
HDIM = 64
FF = 4096
STEP = 8
N_FSDP = 16
N_BATCH = 8
LOCAL_HEADS = HEADS // N_BATCH
LOCAL_WIDTH = LOCAL_HEADS * HDIM
K_ROUTE = 256

EPSILON = 1e-05
SCORE_SCALE = 0.125
NEGATIVE = -1e30
MOMENTUM = 0.95
WEIGHT_DECAY = 0.01
STEP_RATES = (0.15, 1.0, 0.15, 0.15)
NEWTON_A = 3.4445
NEWTON_B = -4.775
NEWTON_C = 2.0315
NEWTON_EPSILON = 1e-07
ADAM_RATE = 0.03
FIRST_DECAY = 0.9
SECOND_DECAY = 0.95
ADAM_EPSILON = 1e-08
HIGHEST = lax.Precision.HIGHEST
HIGH = lax.Precision.HIGH
F32 = jnp.float32
BF16 = jnp.bfloat16

FSDP = ("y", "x")
BATCH = ("z", "c")
EVERY = ("y", "x", "z", "c")


def rms_norm(values):
    return values * lax.rsqrt(jnp.mean(values * values, axis=-1, keepdims=True) + EPSILON)


def gelu_tanh(values):
    return jax.nn.gelu(values, approximate=True)


def norm_back(values, grad_normed):
    pull_back = jax.vjp(rms_norm, values)[1]
    return pull_back(grad_normed)[0]


def dot_f32(pattern, left, right):
    return jnp.einsum(pattern, left, right, preferred_element_type=F32)


def gather_batch(values):
    return lax.all_gather(values, BATCH, axis=0, tiled=True)


def scatter_batch(values):
    return lax.psum_scatter(values, BATCH, scatter_dimension=0, tiled=True)


def head_shards(masters):
    joined = jnp.concatenate([masters[0].astype(BF16), masters[1].astype(BF16)], axis=2)
    parts = joined.reshape(2, 8, 4, N_BATCH, LOCAL_WIDTH)
    parts = jnp.transpose(parts, (3, 0, 1, 2, 4)).reshape(N_BATCH, 2, 8, 4 * LOCAL_WIDTH)
    moved = lax.all_to_all(parts, BATCH, split_axis=0, concat_axis=0, tiled=True)
    return jnp.transpose(moved, (1, 0, 2, 3)).reshape(2, 64, 4 * LOCAL_WIDTH)


def attend(projected, positions, segments):
    rows = projected.shape[0]
    queries = projected[:, :LOCAL_WIDTH].reshape(rows, LOCAL_HEADS, HDIM)
    keys = projected[:, LOCAL_WIDTH : 2 * LOCAL_WIDTH].reshape(rows, LOCAL_HEADS, HDIM)
    values = projected[:, 2 * LOCAL_WIDTH :].reshape(rows, LOCAL_HEADS, HDIM)
    allowed = (positions[None, :] <= positions[:, None]) & (segments[None, :] == segments[:, None])
    scores = dot_f32("qhd,khd->hqk", queries, keys) * SCORE_SCALE
    scores = jnp.where(allowed[None], scores, NEGATIVE)
    row_top = jnp.max(scores, axis=2, keepdims=True)
    exponent = jnp.exp(scores - row_top)
    row_total = jnp.sum(exponent, axis=2, keepdims=True)
    probs = (exponent / row_total).astype(BF16)
    mixed = dot_f32("hqk,khd->qhd", probs, values).reshape(rows, LOCAL_WIDTH).astype(BF16)
    return mixed, row_top + jnp.log(row_total)


def attend_back(projected, positions, segments, log_total, grad_mixed):
    rows = projected.shape[0]
    queries = projected[:, :LOCAL_WIDTH].reshape(rows, LOCAL_HEADS, HDIM)
    keys = projected[:, LOCAL_WIDTH : 2 * LOCAL_WIDTH].reshape(rows, LOCAL_HEADS, HDIM)
    values = projected[:, 2 * LOCAL_WIDTH :].reshape(rows, LOCAL_HEADS, HDIM)
    grads = grad_mixed.reshape(rows, LOCAL_HEADS, HDIM)
    allowed = (positions[None, :] <= positions[:, None]) & (segments[None, :] == segments[:, None])
    scores = dot_f32("qhd,khd->hqk", queries, keys) * SCORE_SCALE
    probs = jnp.exp(jnp.where(allowed[None], scores, NEGATIVE) - log_total)
    grad_probs = dot_f32("qhd,khd->hqk", grads, values)
    inner = jnp.sum(probs * grad_probs, axis=2, keepdims=True)
    grad_scores = (probs * (grad_probs - inner)).astype(BF16) * SCORE_SCALE
    grad_q = dot_f32("hqk,khd->qhd", grad_scores, keys).reshape(rows, LOCAL_WIDTH)
    grad_k = dot_f32("hqk,qhd->khd", grad_scores, queries).reshape(rows, LOCAL_WIDTH)
    grad_v = dot_f32("hqk,qhd->khd", probs.astype(BF16), grads).reshape(rows, LOCAL_WIDTH)
    return jnp.concatenate([grad_q, grad_k, grad_v], axis=1).astype(BF16)


def qkv_forward(normed_all, weight_heads):
    return dot_f32("td,dc->tc", normed_all, weight_heads[:, : 3 * LOCAL_WIDTH]).astype(BF16)


def out_forward(mixed, weight_heads):
    return dot_f32("td,od->to", mixed, weight_heads[:, 3 * LOCAL_WIDTH :])


def feed_forward(normed_all, weight_up, weight_down):
    hidden = dot_f32("td,fd->tf", normed_all, weight_up)
    active = gelu_tanh(hidden).astype(BF16)
    return dot_f32("tf,fd->td", active, weight_down), hidden, active


def feed_backward(normed_all, weight_up, weight_down, hidden, active, grad_low):
    grad_down = dot_f32("tf,td->fd", active, grad_low)
    grad_active = dot_f32("td,fd->tf", grad_low, weight_down)
    pull_back = jax.vjp(gelu_tanh, hidden)[1]
    grad_hidden = pull_back(grad_active)[0].astype(BF16)
    grad_up = dot_f32("tf,td->fd", grad_hidden, normed_all)
    grad_normed = dot_f32("tf,fd->td", grad_hidden, weight_up)
    return grad_normed, grad_up, grad_down


def attention_grads(normed_all, weight_heads, mixed, projected, positions, segments, log_total, grad_low):
    grad_out = dot_f32("to,td->od", grad_low, mixed)
    grad_mixed = dot_f32("to,od->td", grad_low, weight_heads[:, 3 * LOCAL_WIDTH :]).astype(BF16)
    grad_projected = attend_back(projected, positions, segments, log_total, grad_mixed)
    grad_qkv = dot_f32("td,tc->dc", normed_all, grad_projected)
    grad_normed = dot_f32("tc,dc->td", grad_projected, weight_heads[:, : 3 * LOCAL_WIDTH])
    return grad_normed, jnp.concatenate([grad_qkv, grad_out], axis=1)


def polynomial(rows, gram):
    once = jnp.einsum("rb,bc->rc", rows, gram, precision=HIGH)
    twice = jnp.einsum("rb,bc->rc", once, gram, precision=HIGH)
    return NEWTON_A * rows + NEWTON_B * once + NEWTON_C * twice


def newton_two(rows, gram):
    scale = jnp.sqrt(jnp.trace(gram)) + NEWTON_EPSILON
    rows = rows / scale
    gram = gram / (scale * scale)

    def second_gram(values):
        inner = polynomial(values, gram)
        return polynomial(jnp.einsum("rb,bc->rc", inner, gram, precision=HIGH), gram)

    first = polynomial(rows, gram)
    once = second_gram(first)
    twice = second_gram(once)
    return NEWTON_A * first + NEWTON_B * once + NEWTON_C * twice


def newton_heads(block):
    for iteration in range(2):
        gram = jnp.einsum("rb,rc->bc", block, block, precision=HIGHEST)
        if iteration == 0:
            scale = jnp.sqrt(jnp.trace(gram)) + NEWTON_EPSILON
            block = block / scale
            gram = gram / (scale * scale)
        product = jnp.einsum("rb,bc->rc", block, gram, precision=HIGHEST)
        block = (
            NEWTON_A * block
            + NEWTON_B * product
            + NEWTON_C * jnp.einsum("rb,bc->rc", product, gram, precision=HIGHEST)
        )
    return block


def body(
    inputs,
    cotangent,
    segment_ids,
    routed,
    qkv_master,
    out_master,
    up_master,
    down_master,
    qkv_moment,
    out_moment,
    up_moment,
    down_moment,
    router,
    router_first,
    router_second,
):
    masters = (qkv_master, out_master, up_master, down_master)
    token_count = inputs.shape[0]
    batch_index = lax.axis_index(BATCH)
    core_index = lax.axis_index("c")
    sequence_pos = jnp.arange(token_count * N_BATCH)
    slot_pos = jnp.arange(K_ROUTE)
    segment = segment_ids.astype(F32)
    segments_all = gather_batch(segment_ids)
    local_index = routed[0] - batch_index * token_count
    is_mine = (local_index >= 0) & (local_index < token_count)
    pick = (local_index[:, None] == jnp.arange(token_count)[None, :]).astype(F32)
    slot_grads = lax.psum(jnp.einsum("st,td->sd", pick, cotangent, precision=HIGHEST), BATCH)
    slot_segments = segments_all[routed[0]]

    heads_local = head_shards(masters)
    heads_dense = lax.all_gather(heads_local[0], FSDP, axis=0, tiled=True)
    up_dense = lax.all_gather(up_master[0].astype(BF16), FSDP, axis=0, tiled=True)
    down_dense = lax.all_gather(down_master[0].astype(BF16), FSDP, axis=0, tiled=True)
    heads_routed = lax.all_gather(heads_local[1], FSDP, axis=0, tiled=True)
    up_routed = lax.all_gather(up_master[1].astype(BF16), FSDP, axis=0, tiled=True)
    down_routed = lax.all_gather(down_master[1].astype(BF16), FSDP, axis=0, tiled=True)

    moments_heads = jnp.concatenate([qkv_moment, out_moment], axis=2).reshape(
        2, 8, 4, N_BATCH, LOCAL_HEADS, HDIM
    )
    moments_heads = jnp.transpose(moments_heads, (0, 2, 4, 3, 1, 5)).reshape(128, 8, HDIM)
    moment_block = lax.all_to_all(
        moments_heads, EVERY, split_axis=0, concat_axis=0, tiled=True
    ).reshape(D, HDIM)

    normed_low = gather_batch(rms_norm(inputs).astype(BF16))
    projected = qkv_forward(normed_low, heads_dense)
    mixed_low, log_total = attend(projected, sequence_pos, segments_all)
    middle = inputs + scatter_batch(out_forward(mixed_low, heads_dense))
    normed_two = gather_batch(rms_norm(middle).astype(BF16))
    fed_part, feed_hidden, feed_active = feed_forward(normed_two, up_dense, down_dense)
    hidden = middle + scatter_batch(fed_part)

    slot_rows = lax.psum(jnp.einsum("st,td->sd", pick, hidden, precision=HIGHEST), BATCH)
    slot_normed = rms_norm(slot_rows)
    slot_low = slot_normed.astype(BF16)
    gate_values = jnp.dot(slot_normed, router, precision=HIGHEST)
    r_projected = qkv_forward(slot_low, heads_routed)
    r_mixed, r_log_total = attend(r_projected, slot_pos, slot_segments)
    r_attended = lax.psum(out_forward(r_mixed, heads_routed), BATCH)
    r_middle = slot_rows + r_attended
    r_two = rms_norm(r_middle).astype(BF16)
    r_fed_part, r_hidden, r_active = feed_forward(r_two, up_routed, down_routed)
    routed_branch = r_attended + lax.psum(r_fed_part, BATCH)
    update_rows = gate_values[:, None] * routed_branch
    mixed = hidden + jnp.einsum("st,sd->td", pick, update_rows, precision=HIGHEST)

    gate_grads = jnp.sum(slot_grads * routed_branch, axis=1)
    branch_grads = gate_values[:, None] * slot_grads
    r_grad_two, r_grad_up, r_grad_down = feed_backward(
        r_two, up_routed, down_routed, r_hidden, r_active, branch_grads.astype(BF16)
    )
    r_grad_mid = norm_back(r_middle, lax.psum(r_grad_two, BATCH))
    r_grad_normed, r_grad_heads = attention_grads(
        slot_low,
        heads_routed,
        r_mixed,
        r_projected,
        slot_pos,
        slot_segments,
        r_log_total,
        (r_grad_mid + branch_grads).astype(BF16),
    )
    r_grad_normed = lax.psum(r_grad_normed, BATCH)
    own_slots = slot_pos // (K_ROUTE // N_BATCH) == batch_index
    router_grad = jnp.dot(jnp.where(own_slots, gate_grads, 0.0), slot_normed, precision=HIGHEST)
    router_total = lax.psum(router_grad, EVERY)
    slot_input_grads = r_grad_mid + norm_back(
        slot_rows, r_grad_normed + gate_grads[:, None] * router[None, :]
    )
    hidden_grads = cotangent + jnp.einsum("st,sd->td", pick, slot_input_grads, precision=HIGHEST)

    dense_low = gather_batch(hidden_grads.astype(BF16))
    grad_two, grad_up, grad_down = feed_backward(
        normed_two, up_dense, down_dense, feed_hidden, feed_active, dense_low
    )
    grad_mid = hidden_grads + norm_back(middle, scatter_batch(grad_two))
    grad_normed, grad_heads = attention_grads(
        normed_low,
        heads_dense,
        mixed_low,
        projected,
        sequence_pos,
        segments_all,
        log_total,
        gather_batch(grad_mid.astype(BF16)),
    )
    grad_inputs = grad_mid + norm_back(inputs, scatter_batch(grad_normed))

    wide_grads = jnp.stack(
        [
            lax.psum_scatter(grads, FSDP, scatter_dimension=0, tiled=True)
            for grads in (grad_up, r_grad_up, grad_down, r_grad_down)
        ]
    )
    new_up_moment = MOMENTUM * up_moment + wide_grads[:2]
    new_down_moment = MOMENTUM * down_moment + wide_grads[2:]
    wide_own = jnp.concatenate([new_up_moment, new_down_moment], axis=0)
    wide_rows = lax.all_to_all(wide_own, "z", split_axis=0, concat_axis=0, tiled=True).reshape(128, D)
    wide_gram = lax.psum(
        jnp.einsum("rb,rc->bc", wide_rows, wide_rows, precision=HIGHEST), ("y", "x", "c")
    )
    wide_ortho = newton_two(wide_rows, wide_gram).reshape(4, 32, D)
    wide_ortho = lax.all_to_all(wide_ortho, "z", split_axis=0, concat_axis=0, tiled=True)

    def blocks_of(grads):
        return jnp.transpose(grads.reshape(D, 8, HDIM), (1, 0, 2))

    block_grads = jnp.concatenate([blocks_of(grad_heads), blocks_of(r_grad_heads)], axis=0)
    block_grad = lax.psum_scatter(
        block_grads.reshape(16, D * HDIM // 128, 128), FSDP, scatter_dimension=0, tiled=True
    ).reshape(D, HDIM)
    new_block = MOMENTUM * moment_block + block_grad
    ortho_block = newton_heads(new_block)
    returned = jnp.concatenate([new_block, ortho_block], axis=1).reshape(128, 8, 2 * HDIM)
    returned = lax.all_to_all(returned, EVERY, split_axis=0, concat_axis=0, tiled=True)
    returned = returned.reshape(2, 4, LOCAL_HEADS, N_BATCH, 8, 2, HDIM)
    returned = jnp.transpose(returned, (5, 0, 4, 1, 3, 2, 6)).reshape(2, 2, 8, 4 * D)
    new_moments = (returned[0, :, :, : 3 * D], returned[0, :, :, 3 * D :], new_up_moment, new_down_moment)
    orthos = (returned[1, :, :, : 3 * D], returned[1, :, :, 3 * D :], wide_ortho[:2], wide_ortho[2:])

    widths = (HDIM, HDIM, D, D)
    full_rows = (D, D, FF, FF)
    new_masters = []
    for index_type in range(4):
        rate = STEP_RATES[index_type]
        factor = 0.2 * math.sqrt(max(full_rows[index_type], widths[index_type]))
        new_masters.append(
            masters[index_type] * (1.0 - rate * WEIGHT_DECAY) - rate * factor * orthos[index_type]
        )
    first_new = FIRST_DECAY * router_first + (1.0 - FIRST_DECAY) * router_total
    second_new = SECOND_DECAY * router_second + (1.0 - SECOND_DECAY) * router_total * router_total
    corrected_first = first_new / (1.0 - FIRST_DECAY**STEP)
    corrected_second = second_new / (1.0 - SECOND_DECAY**STEP)
    router_new = router * (1.0 - ADAM_RATE * WEIGHT_DECAY) - ADAM_RATE * corrected_first / (
        jnp.sqrt(corrected_second) + ADAM_EPSILON
    )
    return (
        (mixed, grad_inputs)
        + new_moments
        + tuple(new_masters)
        + tuple(master.astype(BF16) for master in new_masters)
        + (router_new, first_new, second_new)
    )


def solution(mesh):
    fine = Mesh(mesh.devices.reshape(4, 4, 4, 2), EVERY)
    tokens = P(EVERY, None)
    weights = P(None, EVERY, None)
    return jax.shard_map(
        body,
        mesh=fine,
        in_specs=(tokens, tokens, P(EVERY), P(FSDP, None)) + (weights,) * 8 + (P(),) * 3,
        out_specs=(tokens, tokens) + (weights,) * 12 + (P(),) * 3,
        check_vma=False,
    )
```

time: 5940 us -> 1600 us (0.27)
  waiting for transfers between devices: 5230 us -> 1030 us
  matrix products: 413 us -> 296 us
    reduce_scatter x12 -> x8, waiting for transfers between devices: 4190 us -> 431 us  [the longest x4 297 us: body(): lax.psum_scatter(grads, FSDP, scatter_dimension=0, tiled=True)]
    psum x4 -> x5, waiting for transfers between devices: 527 us -> 243 us  [the longest x1 65.5 us: body(): routed_branch = r_attended + lax.psum(r_fed_part, BATCH)]
    all_gather x12 -> x10, waiting for transfers between devices: 506 us -> 349 us  [the longest x4 121 us: gather_batch(): return lax.all_gather(values, BATCH, axis=0, tiled=True)]
    dot_general x55 -> x60, matrix products: 412 us -> 295 us  [the longest x36 255 us: dot_f32(): return jnp.einsum(pattern, left, right, preferred_element_type=F32)]
  transfers between devices with their start and end apart: 30 -> 27, of which waited for: 26 -> 23; matrix products, arithmetic and copies ran while one was open for 8% -> 18% of each run, Pallas kernels for 0% -> 0%
where the time goes in v1:
time: 1600 us; the launch traced here: 1590 us
  waiting for transfers between devices  1030 us (64%)
  matrix products  296 us (18%)
  blocking collectives  109 us (7%)
  other arithmetic  78.5 us (5%)
  local copies, waits for them, and re-layouts  41.7 us (3%)
  starting transfers between devices  18.6 us (1%)
  between operations  17.6 us (1%)
    reduce_scatter x4, waiting for transfers between devices, body(): lax.psum_scatter(grads, FSDP, scatter_dimension=0, tiled=True)  297 us
    dot_general x36, matrix products, dot_f32(): return jnp.einsum(pattern, left, right, preferred_element_type=F32)  255 us
    reduce_scatter x4, waiting for transfers between devices, scatter_batch(): return lax.psum_scatter(values, BATCH, scatter_dimension=0, tiled=True)  134 us
    all_gather x4, waiting for transfers between devices, gather_batch(): return lax.all_gather(values, BATCH, axis=0, tiled=True)  121 us
    psum x1, blocking collectives, body(): router_total = lax.psum(router_grad, EVERY)  68.3 us
    psum x1, waiting for transfers between devices, body(): routed_branch = r_attended + lax.psum(r_fed_part, BATCH)  65.5 us
    psum x1, waiting for transfers between devices, body(): r_attended = lax.psum(out_forward(r_mixed, heads_routed), BATCH)  62.7 us
    psum x1, waiting for transfers between devices, body(): r_grad_mid = norm_back(r_middle, lax.psum(r_grad_two, BATCH))  58.2 us
  transfers between devices with their start and end apart: 27, of which 23 were waited for; matrix products, arithmetic and copies ran while one was open for 18% of the time, Pallas kernels for 0%

profile of v1, /device:TPU:1, one launch (start us, length us, event | category | flops | bytes accessed | tf_op | source)
XLA Modules:
  0.0 1589.5 jit_solution(1597643782489251936)
XLA Ops:
  9.1 11.9 all_to_all.25
  25.4 9.6 all-gather.4
  40.5 22.2 %all-gather.18.cloned.1.call-done = bf16[1024,512]{1,0:T(8,128)(2,1)} async-done(((bf16[64,512]{1,0:T(8,128)(2,1)}), bf16[1024,512]{1,0:T(8,128)(2,1)}) %all-gather.18.cloned.1.call-update) | async-done | bytes 1048592 | tf_op jit(solution)/shard_map/all_gather | solution.py:213
  62.7 35.8 %all-gather.16.cloned.1.call-done = bf16[2048,1024]{1,0:T(8,128)(2,1)} async-done(((bf16[256,1024]{1,0:T(8,128)(2,1)}), bf16[2048,1024]{1,0:T(8,128)(2,1)}) %all-gather.16.cloned.1.call-update) | async-done | bytes 4194320 | tf_op jit(solution)/shard_map/all_gather | solution.py:62
  103.1 14.5 fusion.4
  117.6 14.6 fusion.3
  132.2 16.0 %fusion.51 = bf16[2,64,2048]{2,1,0:T(8,128)(2,1)S(1)} fusion(bf16[2048,2,64]{0,2,1:T(8,128)(2,1)S(1)} %bitcast.203, f32[2,2048,2048]{1,2,0:T(8,128)} %get-tuple-element.55, f32[2,2048]{1,0:T(2,128)S(1)} %fusion.3, f32[2,2048]{1,0:T(2,128)S(1)} %get-tuple-element.54, pred[2048,2048]{0,1:T(8,128)(4,1)} %fusion.13), kind=kOutput, calls=%fused_computation.46 | convolution fusion | flops 1115947008 | bytes 38830080 | tf_op jit(solution)/shard_map/hqk,khd->qhd/dot_general | solution.py:58
  155.9 49.6 %reduce-scatter.12.cloned.1.call-done = f32[256,1024]{1,0:T(8,128)} async-done(((f32[2048,1024]{1,0:T(8,128)}), f32[256,1024]{1,0:T(8,128)}) %reduce-scatter.12.cloned.1.call-update) | async-done | bytes 1048592 | tf_op jit(solution)/shard_map/reduce_scatter | solution.py:66
  208.7 40.7 %all-gather.28.cloned.1.call-done = bf16[1,512,1024]{2,1,0:T(8,128)(2,1)} async-done(((bf16[1,32,1024]{2,1,0:T(8,128)(2,1)}), bf16[1,512,1024]{2,1,0:T(8,128)(2,1)}) %all-gather.28.cloned.1.call-update) | async-done | bytes 1048592 | tf_op jit(solution)/shard_map/all_gather | solution.py:214
  249.4 35.6 %all-gather.20.cloned.1.call-done = bf16[2048,1024]{1,0:T(8,128)(2,1)} async-done(((bf16[256,1024]{1,0:T(8,128)(2,1)}), bf16[2048,1024]{1,0:T(8,128)(2,1)}) %all-gather.20.cloned.1.call-update) | async-done | bytes 4194320 | tf_op jit(solution)/shard_map/all_gather | solution.py:62
  291.9 36.2 %all-gather.30.cloned.1.call-done = bf16[1,512,1024]{2,1,0:T(8,128)(2,1)} async-done(((bf16[1,32,1024]{2,1,0:T(8,128)(2,1)}), bf16[1,512,1024]{2,1,0:T(8,128)(2,1)}) %all-gather.30.cloned.1.call-update) | async-done | bytes 1048592 | tf_op jit(solution)/shard_map/all_gather | solution.py:215
  337.3 52.1 %reduce-scatter.14.cloned.1.call-done = f32[256,1024]{1,0:T(8,128)} async-done(((f32[2048,1024]{1,0:T(8,128)}), f32[256,1024]{1,0:T(8,128)}) %reduce-scatter.14.cloned.1.call-update) | async-done | bytes 1048592 | tf_op jit(solution)/shard_map/reduce_scatter | solution.py:66
  397.8 56.7 %all-reduce.9.cloned.1.call-done = f32[256,1024]{1,0:T(8,128)} async-done(((f32[256,1024]{1,0:T(8,128)}), f32[256,1024]{1,0:T(8,128)}) %all-reduce.9.cloned.1.call-update) | async-done | bytes 1048592 | tf_op jit(solution)/shard_map/psum | solution.py:236
  455.8 43.7 %all-gather.22.cloned.1.call-done = bf16[1024,512]{1,0:T(8,128)(2,1)} async-done(((bf16[64,512]{1,0:T(8,128)(2,1)}), bf16[1024,512]{1,0:T(8,128)(2,1)}) %all-gather.22.cloned.1.call-update) | async-done | bytes 1048592 | tf_op jit(solution)/shard_map/all_gather | solution.py:216
  507.9 62.7 %all-reduce.17.cloned.1.call-done = (f32[256,1024]{1,0:T(8,128)}, f32[256,1024]{1,0:T(8,128)}) async-done(((f32[256,1024]{1,0:T(8,128)}, f32[256,1024]{1,0:T(8,128)}), (f32[256,1024]{1,0:T(8,128)}, f32[256,1024]{1,0:T(8,128)})) %all-reduce.17.cloned.1.call-update) | async-done | bytes 2097168 | tf_op jit(solution)/shard_map/psum | solution.py:242
  572.1 43.8 %all-gather.32.cloned.1.call-done = bf16[1,512,1024]{2,1,0:T(8,128)(2,1)} async-done(((bf16[1,32,1024]{2,1,0:T(8,128)(2,1)}), bf16[1,512,1024]{2,1,0:T(8,128)(2,1)}) %all-gather.32.cloned.1.call-update) | async-done | bytes 1048592 | tf_op jit(solution)/shard_map/all_gather | solution.py:217
  618.5 41.9 %all-gather.34.cloned.1.call-done = bf16[1,512,1024]{2,1,0:T(8,128)(2,1)} async-done(((bf16[1,32,1024]{2,1,0:T(8,128)(2,1)}), bf16[1,512,1024]{2,1,0:T(8,128)(2,1)}) %all-gather.34.cloned.1.call-update) | async-done | bytes 1048592 | tf_op jit(solution)/shard_map/all_gather | solution.py:218
  667.6 58.2 %all-reduce.11.cloned.1.call-done = f32[256,1024]{1,0:T(8,128)} async-done(((f32[256,1024]{1,0:T(8,128)}), f32[256,1024]{1,0:T(8,128)}) %all-reduce.11.cloned.1.call-update) | async-done | bytes 1048592 | tf_op jit(solution)/shard_map/psum | solution.py:255
  740.0 65.5 %all-reduce.15.cloned.1.call-done = (f32[256,1024]{1,0:T(8,128)}, f32[256,1024]{1,0:T(8,128)}) async-done(((f32[256,1024]{1,0:T(8,128)}, f32[256,1024]{1,0:T(8,128)}), (f32[256,1024]{1,0:T(8,128)}, f32[256,1024]{1,0:T(8,128)})) %all-reduce.15.cloned.1.call-update) | async-done | bytes 2097168 | tf_op jit(solution)/shard_map/psum | solution.py:246
  813.1 34.2 %all-gather.24.cloned.1.call-done = bf16[2048,1024]{1,0:T(8,128)(2,1)} async-done(((bf16[256,1024]{1,0:T(8,128)(2,1)}), bf16[2048,1024]{1,0:T(8,128)(2,1)}) %all-gather.24.cloned.1.call-update) | async-done | bytes 4194320 | tf_op jit(solution)/shard_map/all_gather | solution.py:62
  882.5 31.9 %reduce-scatter.16.cloned.1.call-done = f32[256,1024]{1,0:T(8,128)} async-done(((f32[2048,1024]{1,0:T(8,128)}), f32[256,1024]{1,0:T(8,128)}) %reduce-scatter.16.cloned.1.call-update) | async-done | bytes 1048592 | tf_op jit(solution)/shard_map/reduce_scatter | solution.py:66
  923.1 67.2 %reduce-scatter.22.cloned.1.call-done = f32[32,1024]{1,0:T(8,128)} async-done(((f32[512,1024]{1,0:T(8,128)}), f32[32,1024]{1,0:T(8,128)}) %reduce-scatter.22.cloned.1.call-update) | async-done | bytes 131088 | tf_op jit(solution)/shard_map/reduce_scatter | solution.py:294
  990.3 77.1 %reduce-scatter.20.cloned.1.call-done = f32[32,1024]{1,0:T(8,128)} async-done(((f32[512,1024]{1,0:T(8,128)}), f32[32,1024]{1,0:T(8,128)}) %reduce-scatter.20.cloned.1.call-update) | async-done | bytes 131088 | tf_op jit(solution)/shard_map/reduce_scatter | solution.py:294
  1068.4 75.8 %reduce-scatter.26.cloned.1.call-done = f32[32,1024]{1,0:T(8,128)} async-done(((f32[512,1024]{1,0:T(8,128)}), f32[32,1024]{1,0:T(8,128)}) %reduce-scatter.26.cloned.1.call-update) | async-done | bytes 131088 | tf_op jit(solution)/shard_map/reduce_scatter | solution.py:294
  1144.2 77.2 %reduce-scatter.24.cloned.1.call-done = f32[32,1024]{1,0:T(8,128)} async-done(((f32[512,1024]{1,0:T(8,128)}), f32[32,1024]{1,0:T(8,128)}) %reduce-scatter.24.cloned.1.call-update) | async-done | bytes 131088 | tf_op jit(solution)/shard_map/reduce_scatter | solution.py:294
  1242.1 15.3 all-gather.26.cloned.1.call-done
  1261.3 15.8 fusion.38
  1277.1 13.7 fusion.205
  1290.8 46.1 %fusion.41 = bf16[2,64,2048]{2,1,0:T(8,128)(2,1)S(1)} fusion(bf16[2048,2,64]{0,2,1:T(8,128)(2,1)S(1)} %bitcast.223, f32[2,2048,2048]{1,2,0:T(8,128)} %fusion.205, f32[2,2048,2048]{1,2,0:T(8,128)} %get-tuple-element.55, f32[2,2048]{1,0:T(2,128)S(1)} %copy-done.60, pred[2048,2048]{0,1:T(8,128)(4,1)} %fusion.13), kind=kOutput, calls=%fused_computation.44 | convolution fusion | flops 1191450624 | bytes 72368128 | tf_op jit(solution)/shard_map/hqk,khd->qhd/dot_general | solution.py:58
  1336.9 47.9 %fusion.46 = bf16[2,64,2048]{2,1,0:T(8,128)(2,1)S(1)} fusion(bf16[2048,2,64]{0,2,1:T(8,128)(2,1)S(1)} %bitcast.221, f32[2,2048,2048]{1,2,0:T(8,128)} %fusion.205, f32[2,2048,2048]{1,2,0:T(8,128)} %get-tuple-element.55, f32[2,2048]{1,0:T(2,128)S(1)} %copy-done.60, pred[2048,2048]{0,1:T(8,128)(4,1)} %fusion.13), kind=kOutput, calls=%fused_computation.45 | convolution fusion | flops 1191450624 | bytes 72368128 | tf_op jit(solution)/shard_map/hqk,qhd->khd/dot_general | solution.py:58
  1423.4 19.7 %all_to_all.26 = f32[128,1,512]{2,1,0:T(1,128)} all-to-all(f32[128,1,512]{2,1,0:T(1,128)S(1)} %reshape.412), channel_id=1, replica_groups=mesh['y'=4,'x'=4,'z'=4,'c'=2] {'y','x','z','c'}, dimensions={0} | all-to-all | bytes 524288 | tf_op jit(solution)/shard_map/all_to_all | solution.py:224
  1503.0 68.3 %psum.63 = f32[1024]{0:T(1024)S(1)} all-reduce(f32[1024]{0:T(1024)S(1)} %bitcast.245), channel_id=1, replica_groups=mesh['y'=4,'x'=4,'z'=4,'c'=2] {'y','x','z','c'}, use_global_device_ids=true, to_apply=%region_33.34 | all-reduce | flops 1024 | bytes 8192 | tf_op jit(solution)/shard_map/psum | solution.py:269
  (358 shorter events, 270.4 us)
Async XLA Ops:
  7.2 55.5 %all-gather.18.cloned.1.call-start = ((), (), s32[]{:S(2)}) async-start(), calls=%async_computation.15 | async-start | bytes 1114112 | tf_op jit(solution)/shard_map/all_gather | solution.py:213
  21.7 76.8 %all-gather.16.cloned.1.call-start = ((), (), s32[]{:S(2)}) async-start(), calls=%async_computation.14 | async-start | bytes 4718592 | tf_op jit(solution)/shard_map/all_gather | solution.py:62
  25.3 180.2 %reduce-scatter.12.cloned.1.call-start = ((), (), s32[]{:S(2)}) async-start(), calls=%async_computation.16 | async-start | bytes 9437184 | tf_op jit(solution)/shard_map/reduce_scatter | solution.py:66
  154.0 95.4 %all-gather.28.cloned.1.call-start = ((), (), s32[]{:S(2)}) async-start(), calls=%async_computation.31 | async-start | bytes 1114112 | tf_op jit(solution)/shard_map/all_gather | solution.py:214
  155.6 129.4 %all-gather.20.cloned.1.call-start = ((), (), s32[]{:S(2)}) async-start(), calls=%async_computation.17 | async-start | bytes 4718592 | tf_op jit(solution)/shard_map/all_gather | solution.py:62
  207.9 120.2 %all-gather.30.cloned.1.call-start = ((), (), s32[]{:S(2)}) async-start(), calls=%async_computation.32 | async-start | bytes 1114112 | tf_op jit(solution)/shard_map/all_gather | solution.py:215
  208.7 180.7 %reduce-scatter.14.cloned.1.call-start = ((), (), s32[]{:S(2)}) async-start(), calls=%async_computation.18 | async-start | bytes 9437184 | tf_op jit(solution)/shard_map/reduce_scatter | solution.py:66
  336.6 117.8 %all-reduce.9.cloned.1.call-start = ((), (), s32[]{:S(2)}) async-start(), calls=%async_computation.19 | async-start | bytes 2097152 | tf_op jit(solution)/shard_map/psum | solution.py:236
  337.3 472.6 %copy-start.56 = (s32[1,256]{1,0:T(1,128)}, s32[1,256]{1,0:T(1,128)S(1)}, u32[]{:S(2)}) copy-start(s32[1,256]{1,0:T(1,128)S(1)} %broadcast_subtract_fusion) | copy-start | bytes 3076
  393.4 106.1 %all-gather.22.cloned.1.call-start = ((), (), s32[]{:S(2)}) async-start(), calls=%async_computation.20 | async-start | bytes 1114112 | tf_op jit(solution)/shard_map/all_gather | solution.py:216
  394.2 176.5 %all-reduce.17.cloned.1.call-start = ((), (), s32[]{:S(2)}) async-start(), calls=%async_computation.37 | async-start | bytes 4194304 | tf_op jit(solution)/shard_map/psum | solution.py:242
  455.8 354.0 %copy-start.54 = (f32[256]{0:T(256)}, f32[256]{0:T(256)S(1)}, u32[]{:S(2)}) copy-start(f32[256]{0:T(256)S(1)} %fusion.157) | copy-start | bytes 3076
  505.6 110.4 %all-gather.32.cloned.1.call-start = ((), (), s32[]{:S(2)}) async-start(), calls=%async_computation.33 | async-start | bytes 1114112 | tf_op jit(solution)/shard_map/all_gather | solution.py:217
  506.3 154.1 %all-gather.34.cloned.1.call-start = ((), (), s32[]{:S(2)}) async-start(), calls=%async_computation.34 | async-start | bytes 1114112 | tf_op jit(solution)/shard_map/all_gather | solution.py:218
  506.9 219.0 %all-reduce.11.cloned.1.call-start = ((), (), s32[]{:S(2)}) async-start(), calls=%async_computation.21 | async-start | bytes 2097152 | tf_op jit(solution)/shard_map/psum | solution.py:255
  664.3 141.1 %all-reduce.15.cloned.1.call-start = ((), (), s32[]{:S(2)}) async-start(), calls=%async_computation.36 | async-start | bytes 4194304 | tf_op jit(solution)/shard_map/psum | solution.py:246
  739.9 107.4 %all-gather.24.cloned.1.call-start = ((), (), s32[]{:S(2)}) async-start(), calls=%async_computation.22 | async-start | bytes 4718592 | tf_op jit(solution)/shard_map/all_gather | solution.py:62
  813.1 101.3 %reduce-scatter.16.cloned.1.call-start = ((), (), s32[]{:S(2)}) async-start(), calls=%async_computation.23 | async-start | bytes 9437184 | tf_op jit(solution)/shard_map/reduce_scatter | solution.py:66
  862.9 127.3 %reduce-scatter.22.cloned.1.call-start = ((), (), s32[]{:S(2)}) async-start(), calls=%async_computation.27 | async-start | bytes 2228224 | tf_op jit(solution)/shard_map/reduce_scatter | solution.py:294
  864.8 202.5 %reduce-scatter.20.cloned.1.call-start = ((), (), s32[]{:S(2)}) async-start(), calls=%async_computation.26 | async-start | bytes 2228224 | tf_op jit(solution)/shard_map/reduce_scatter | solution.py:294
  871.8 272.4 %reduce-scatter.26.cloned.1.call-start = ((), (), s32[]{:S(2)}) async-start(), calls=%async_computation.29 | async-start | bytes 2228224 | tf_op jit(solution)/shard_map/reduce_scatter | solution.py:294
  874.9 346.4 %reduce-scatter.24.cloned.1.call-start = ((), (), s32[]{:S(2)}) async-start(), calls=%async_computation.28 | async-start | bytes 2228224 | tf_op jit(solution)/shard_map/reduce_scatter | solution.py:294
  882.4 375.0 %all-gather.26.cloned.1.call-start = ((), (), s32[]{:S(2)}) async-start(), calls=%async_computation.24 | async-start | bytes 4718592 | tf_op jit(solution)/shard_map/all_gather | solution.py:62
  919.2 302.2 %copy-start.42 = (f32[2,32,1024]{2,1,0:T(8,128)S(1)}, f32[2,32,1024]{2,1,0:T(8,128)}, u32[]{:S(2)}) copy-start(f32[2,32,1024]{2,1,0:T(8,128)} %param.26) | copy-start | bytes 786436
  919.2 308.9 %copy-start.13 = (bf16[256,1024]{1,0:T(8,128)(2,1)S(1)}, bf16[256,1024]{1,0:T(8,128)(2,1)}, u32[]{:S(2)}) copy-start(bf16[256,1024]{1,0:T(8,128)(2,1)} %copy-done.12) | copy-start | bytes 1572868
  919.2 308.9 %copy-start.47 = (bf16[2,64,256]{2,1,0:T(8,128)(2,1)S(1)}, bf16[2,64,256]{2,1,0:T(8,128)(2,1)}, u32[]{:S(2)}) copy-start(bf16[2,64,256]{2,1,0:T(8,128)(2,1)} %copy-done.46) | copy-start | bytes 196612
  1223.9 11.2 all-to-all-start.3
  1228.0 227.0 %all-reduce.13.cloned.1.call-start = ((), (), s32[]{:S(2)}) async-start(), calls=%async_computation.30 | async-start | bytes 8388608 | tf_op jit(solution)/shard_map/psum | solution.py:302
  1241.9 243.3 %reduce-scatter.28.cloned.1.call-start = ((), (), s32[]{:S(2)}) async-start(), calls=%async_computation.35 | async-start | bytes 4456448
  1408.4 169.6 %reduce-scatter.18.cloned.1.call-start = ((), (), s32[]{:S(2)}) async-start(), calls=%async_computation.25 | async-start | bytes 9437184 | tf_op jit(solution)/shard_map/reduce_scatter | solution.py:66
  1481.7 11.6 all-to-all-start.4
  1493.3 79.6 %all-to-all-start.2 = ((f32[128,8,128]{2,1,0:T(8,128)}), f32[128,8,128]{2,1,0:T(8,128)S(1)}, u32[]{:S(2)}, u32[]{:S(2)}) async-start(f32[128,8,128]{2,1,0:T(8,128)} %bitcast.49), calls=%async_computation.6 | async-start | bytes 1048576 | tf_op jit(solution)/shard_map/all_to_all | solution.py:318
  (75 other events, 2318.2 us)
Sparse Core Ops, SparseCore 0:
  21.8 40.8 all-gather.17
  65.0 33.4 all-gather.15
  154.1 51.3 reduce-scatter.11
  208.1 41.2 all-gather.27
  251.5 33.4 all-gather.19
  287.6 40.5 all-gather.29
  336.7 52.6 reduce-scatter.13
  393.6 60.8 all-reduce.8
  457.2 42.3 all-gather.21
  505.7 64.9 all-reduce.16
  573.4 42.4 all-gather.31
  618.5 41.8 all-gather.33
  664.4 61.3 all-reduce.10
  740.0 65.3 all-reduce.14
  813.2 34.0 all-gather.23
  863.1 51.2 reduce-scatter.15
  917.5 72.7 reduce-scatter.21
  993.7 73.5 reduce-scatter.19
  1070.6 73.5 reduce-scatter.25
  1147.7 73.6 reduce-scatter.23
  1223.7 33.6 all-gather.25
  1260.7 110.9 all-reduce.12
  1408.6 76.3 reduce-scatter.27
  1487.3 59.3 reduce-scatter.17

commit v2 on v1

v2 whole, which is shorter than its diff:
```python
import functools
import math

import jax
import jax.numpy as jnp
from jax import lax
from jax.experimental import pallas as pl
from jax.experimental.pallas import tpu as pltpu
from jax.sharding import Mesh
from jax.sharding import PartitionSpec as P

D = 1024
HEADS = 16
HDIM = 64
FF = 4096
STEP = 8
N_FSDP = 16
N_BATCH = 8
LOCAL_HEADS = HEADS // N_BATCH
LOCAL_WIDTH = LOCAL_HEADS * HDIM
K_ROUTE = 256

EPSILON = 1e-05
SCORE_SCALE = 0.125
NEGATIVE = -1e30
MOMENTUM = 0.95
WEIGHT_DECAY = 0.01
STEP_RATES = (0.15, 1.0, 0.15, 0.15)
NEWTON_A = 3.4445
NEWTON_B = -4.775
NEWTON_C = 2.0315
NEWTON_EPSILON = 1e-07
ADAM_RATE = 0.03
FIRST_DECAY = 0.9
SECOND_DECAY = 0.95
ADAM_EPSILON = 1e-08
HIGHEST = lax.Precision.HIGHEST
F32 = jnp.float32
BF16 = jnp.bfloat16

FSDP = ("y", "x")
BATCH = ("z", "c")
EVERY = ("y", "x", "z", "c")


def rms_norm(values):
    return values * lax.rsqrt(jnp.mean(values * values, axis=-1, keepdims=True) + EPSILON)


def gelu_tanh(values):
    return jax.nn.gelu(values, approximate=True)


def norm_back(values, grad_normed):
    pull_back = jax.vjp(rms_norm, values)[1]
    return pull_back(grad_normed)[0]


def dot_f32(pattern, left, right):
    return jnp.einsum(pattern, left, right, preferred_element_type=F32)


def shift(values, axis, step):
    size = 2 if axis == "c" else 4
    return lax.ppermute(values, axis, [(i, (i + step) % size) for i in range(size)])


def pair(values, axis, partner):
    return lax.ppermute(values, axis, [(i, partner(i)) for i in range(4)])


def neighbour_a(i):
    return i ^ 1


def neighbour_b(i):
    return 3 - i


def after(values, *others):
    return lax.optimization_barrier((values,) + others)[0]


def take(values, index):
    return lax.dynamic_index_in_dim(values, index, 0, keepdims=False)


def put(values, piece, index):
    return lax.dynamic_update_index_in_dim(values, piece, index, 0)


def turn(values, step, last=False):
    pairs = []
    for y in range(4):
        for x in range(4):
            for core in range(2):
                along_x = (core == 0) != last
                to_y, to_x = (y, (x + step) % 4) if along_x else ((y + step) % 4, x)
                pairs.append(((y * 4 + x) * 2 + core, (to_y * 4 + to_x) * 2 + core))
    return lax.ppermute(values, ("y", "x", "c"), pairs)


def turn_place(last=False):
    along_x = (lax.axis_index("c") == 0) != last
    return jnp.where(along_x, lax.axis_index("x"), lax.axis_index("y"))


def copy_rows(target, start, source, first, rows):
    step = min(rows, 64)

    @pl.loop(0, rows // step)
    def _(at):
        here = pl.ds(pl.multiple_of(first + at * step, step), step)
        there = pl.ds(pl.multiple_of(start + at * step, step), step)
        target[there, :] = source[here, :].astype(target.dtype)


def place_kernel(piece_count, sub_count, spots, *refs):
    pieces, whole = refs[:piece_count], refs[piece_count]
    rows = pieces[0].shape[0] // sub_count
    for p in range(piece_count):
        for s in range(sub_count):
            start = pl.multiple_of(spots[p * sub_count + s] * rows, rows)
            copy_rows(whole, start, pieces[p], s * rows, rows)


def place(pieces, spots, sub_count=1):
    rows = len(pieces) * pieces[0].shape[0]
    shape = (rows,) + pieces[0].shape[1:]
    size = math.prod(shape) * pieces[0].dtype.itemsize
    return pl.pallas_call(
        functools.partial(place_kernel, len(pieces), sub_count),
        out_shape=jax.ShapeDtypeStruct(shape, pieces[0].dtype),
        in_specs=[IN_SMEM] + [IN_VMEM] * len(pieces),
        out_specs=IN_VMEM,
        compiler_params=pltpu.CompilerParams(vmem_limit_bytes=40 * 2**20),
        cost_estimate=pl.CostEstimate(flops=0, bytes_accessed=2 * size, transcendentals=0),
    )(spots, *pieces)


def split_kernel(rows, spots, up, down, *outs):
    for step in range(4):
        for i in range(4):
            first = pl.multiple_of(spots[4 * step + i] * rows, rows)
            copy_rows(outs[step], 2 * i * rows, up, first, rows)
            copy_rows(outs[step], (2 * i + 1) * rows, down, first, rows)


def split(up, down, spots):
    rows = up.shape[0] // 16
    shape = jax.ShapeDtypeStruct((8 * rows, up.shape[1]), BF16)
    return pl.pallas_call(
        functools.partial(split_kernel, rows),
        out_shape=(shape,) * 4,
        in_specs=[IN_SMEM, IN_VMEM, IN_VMEM],
        out_specs=(IN_VMEM,) * 4,
        compiler_params=pltpu.CompilerParams(vmem_limit_bytes=40 * 2**20),
        cost_estimate=pl.CostEstimate(flops=0, bytes_accessed=3 * up.size * 4, transcendentals=0),
    )(spots, up, down)


IN_VMEM = pl.BlockSpec(memory_space=pltpu.VMEM)
IN_SMEM = pl.BlockSpec(memory_space=pltpu.SMEM)


def in_line(pieces):
    return place(pieces, jnp.arange(len(pieces), dtype=jnp.int32))


def gather_fsdp(values):
    core = lax.axis_index("c")
    mine, far = turn_place(), turn_place(True)
    line = in_line([values] + [turn(values, step) for step in (1, 2, 3)])
    pieces = [line] + [turn(line, step, True) for step in (1, 2, 3)]
    step = jnp.arange(4)
    first, second = (mine - step[None, :]) % 4, (far - step[:, None]) % 4
    spots = jnp.where(core == 0, second * 4 + first, first * 4 + second)
    return place(pieces, spots.reshape(16).astype(jnp.int32), 4)


def turn_parts(parts, last=False):
    me = turn_place(last)
    parts = parts.reshape((4, -1) + parts.shape[1:])
    sent = tuple(take(parts, (me + step) % 4).astype(BF16) for step in (1, 2, 3))
    own = take(parts, me).astype(F32)
    return (own,) + sent, tuple(turn(sent[i], i + 1, last) for i in range(3))


def turn_total(state):
    total = state[0][0].astype(F32)
    for piece in state[1]:
        total = total + piece.astype(F32)
    return total


def scatter_fsdp_first(up, down):
    core = lax.axis_index("c")
    me = turn_place()
    step, other = jnp.arange(4)[:, None], jnp.arange(4)[None, :]
    spot = (me + step) % 4
    spots = jnp.where(core == 0, other * 4 + spot, spot * 4 + other)
    parts = split(up, down, spots.reshape(16).astype(jnp.int32))
    return tuple(parts), tuple(turn(parts[step], step) for step in (1, 2, 3))


def scatter_fsdp_second(state):
    return turn_parts(turn_total(state), True)


def scatter_fsdp_value(state):
    total = turn_total(state)
    return total.reshape(2, -1, total.shape[1])


def turn_first(values):
    return turn_parts(values)


def turn_second(state):
    return turn_parts(turn_total(state), True)


def turn_third(state):
    total = turn_total(state).astype(BF16)
    return (total,), tuple(turn(total, step, True) for step in (1, 2, 3))


def turn_fourth(state):
    spots = (turn_place(True) - jnp.arange(4)) % 4
    line = place([state[0][0], *state[1]], spots.astype(jnp.int32))
    return (line,), tuple(turn(line, step) for step in (1, 2, 3))


def turn_value(state):
    spots = (turn_place() - jnp.arange(4)) % 4
    return place([state[0][0], *state[1]], spots.astype(jnp.int32))


def place_columns_kernel(width, spots, *refs):
    pieces, whole = refs[:-1], refs[-1]
    for p, piece in enumerate(pieces):
        for s in range(piece.shape[1] // width):
            start = pl.multiple_of(spots[p * (piece.shape[1] // width) + s] * width, width)
            whole[:, pl.ds(start, width)] = piece[:, s * width : (s + 1) * width]


def place_columns(pieces, spots):
    rows, width = pieces[0].shape
    return pl.pallas_call(
        functools.partial(place_columns_kernel, LOCAL_WIDTH),
        out_shape=jax.ShapeDtypeStruct((rows, width * len(pieces)), pieces[0].dtype),
        in_specs=[IN_SMEM] + [IN_VMEM] * len(pieces),
        out_specs=IN_VMEM,
        cost_estimate=pl.CostEstimate(flops=0, bytes_accessed=2**20, transcendentals=0),
    )(spots, *pieces)


def take_columns_kernel(width, spots, values, kept, given):
    rows = values.shape[0]
    for step in range(4):
        for i, out in enumerate((kept, given)):
            start = pl.multiple_of(spots[2 * step + i] * width, width)
            out[step * rows : (step + 1) * rows, :] = values[:, pl.ds(start, width)]


def take_columns(values, spots):
    shape = jax.ShapeDtypeStruct((4 * values.shape[0], LOCAL_WIDTH), values.dtype)
    return pl.pallas_call(
        functools.partial(take_columns_kernel, LOCAL_WIDTH),
        out_shape=(shape, shape),
        in_specs=[IN_SMEM, IN_VMEM],
        out_specs=(IN_VMEM, IN_VMEM),
        cost_estimate=pl.CostEstimate(flops=0, bytes_accessed=2**20, transcendentals=0),
    )(spots, values)


def during(state, work):
    sent, comes = state
    done = work(lambda values: after(values, *sent))
    leaves = jax.tree.leaves(done)
    comes = lax.optimization_barrier(tuple(comes) + tuple(leaves))[: len(comes)]
    return (sent, tuple(comes)), done


def gather_near(values):
    return (values,), (shift(values, "z", 1), shift(values, "z", -1))


def gather_far(state):
    (values,), (before, following) = state
    half = values.shape[0] // 2
    across = (shift(before[:half], "z", 1), shift(following[half:], "z", -1))
    return (values, before, following), across


def gather_core(state):
    (values, before, following), (low, high) = state
    half = values.shape[0] // 2
    pieces = [values[:half], values[half:], following[:half], following[half:], low, high]
    mine = in_line(pieces + [before[:half], before[half:]])
    return (mine,), (shift(mine, "c", 1),)


def gather_value(state):
    return in_line([state[0][0], state[1][0]])


def gather_batch(values):
    return gather_value(gather_core(gather_far(gather_near(values))))


def scatter_core(parts):
    rows = parts.shape[0] // 2
    given = parts[rows:].astype(BF16)
    return (parts, given), (shift(given, "c", 1),)


def scatter_far(state):
    (parts, _), (theirs,) = state
    rows = parts.shape[0] // 8
    half = rows // 2

    def mine(step, start, count):
        spot = step * rows + start
        return parts[spot : spot + count] + theirs[spot : spot + count].astype(F32)

    low, high = mine(2, 0, half).astype(BF16), mine(2, half, half).astype(BF16)
    near = (mine(0, 0, rows), mine(1, 0, rows), mine(3, 0, rows))
    return (low, high) + near, (shift(low, "z", 1), shift(high, "z", -1))


def scatter_near(state):
    (_, _, own, up, down), (low, high) = state
    half = low.shape[0]
    up = jnp.concatenate([up[:half] + low.astype(F32), up[half:]], axis=0).astype(BF16)
    down = jnp.concatenate([down[:half], down[half:] + high.astype(F32)], axis=0).astype(BF16)
    return (own, up, down), (shift(up, "z", 1), shift(down, "z", -1))


def scatter_value(state):
    return state[0][0] + state[1][0].astype(F32) + state[1][1].astype(F32)


def column_spots():
    at = jnp.arange(N_BATCH)
    core, place_z = lax.axis_index("c"), lax.axis_index("z")
    return (2 * ((place_z - at // 2) % 4) + (at + core) % 2).astype(jnp.int32)


def columns_core(values):
    return (values,), (shift(values, "c", 1),)


def columns_near(state):
    both = jnp.concatenate([state[0][0], state[1][0]], axis=1)
    return (both,), tuple(shift(both, "z", step) for step in (1, 2, 3))


def columns_value(state):
    return place_columns([state[0][0], *state[1]], column_spots())


def rows_core(values):
    half = values.shape[0] // 2
    given = values[half:]
    return (values, given), (shift(given, "c", 1),)


def rows_near(state):
    values, got = state[0][0], state[1][0]
    rows = values.shape[0] // 8
    pieces = []
    for step in range(4):
        spot = slice(step * rows, (step + 1) * rows)
        pieces.append(jnp.concatenate([values[spot], got[spot]], axis=1))
    return tuple(pieces), tuple(shift(pieces[step], "z", step) for step in (1, 2, 3))


def back_core(values):
    kept, given = take_columns(values, column_spots())
    return (kept, given), (shift(given, "c", 1),)


def back_near(state):
    kept, got = state[0][0], state[1][0]
    rows = kept.shape[0] // 4
    pieces = []
    for step in range(4):
        spot = slice(step * rows, (step + 1) * rows)
        pieces.append(jnp.concatenate([kept[spot], got[spot]], axis=0))
    return tuple(pieces), tuple(shift(pieces[step], "z", -step) for step in (1, 2, 3))


def back_value(state):
    pieces = (state[0][0],) + state[1]
    rows = pieces[0].shape[0] // 2
    return jnp.concatenate([piece[:rows] for piece in pieces] + [piece[rows:] for piece in pieces], axis=0)


def add(left, right):
    return left.astype(F32) + right.astype(F32)


def sum_core(values, kind=BF16):
    core = lax.axis_index("c")
    halves = values.reshape((2, values.shape[0] // 2) + values.shape[1:])
    given = take(halves, 1 - core).astype(kind)
    return (take(halves, core), given), (shift(given, "c", 1),)


def sum_near(state):
    (kept, given), (got,) = state
    kept = add(kept, got).astype(given.dtype)
    quarter = kept.shape[0] // 2
    low, high = kept[:quarter], kept[quarter:]
    return (low, high), (pair(low, "z", neighbour_a), pair(high, "z", neighbour_b))


def sum_next(state):
    (low, high), (from_low, from_high) = state
    low, high = add(low, from_low).astype(low.dtype), add(high, from_high).astype(high.dtype)
    return (low, high), (pair(low, "z", neighbour_b), pair(high, "z", neighbour_a))


def sum_last(state):
    (low, high), (from_low, from_high) = state
    kept = jnp.concatenate([add(low, from_low), add(high, from_high)], axis=0).astype(low.dtype)
    return (kept,), (shift(kept, "c", 1),)


def sum_value(state):
    core = lax.axis_index("c")
    kept, other = state[0][0].astype(F32), state[1][0].astype(F32)
    return jnp.concatenate(
        [jnp.where(core == 0, kept, other), jnp.where(core == 0, other, kept)], axis=0
    )


def head_shards(masters):
    joined = jnp.concatenate([masters[0].astype(BF16), masters[1].astype(BF16)], axis=2)
    parts = joined.reshape(2, 8, 4, N_BATCH, LOCAL_WIDTH)
    parts = jnp.transpose(parts, (3, 0, 1, 2, 4)).reshape(N_BATCH, 2, 8, 4 * LOCAL_WIDTH)
    moved = lax.all_to_all(parts, BATCH, split_axis=0, concat_axis=0, tiled=True)
    return jnp.transpose(moved, (1, 0, 2, 3)).reshape(2, 64, 4 * LOCAL_WIDTH)


BLOCK = 256


def masked_scores(keys, queries, key_block, query_block, key_segs, query_segs):
    scores = lax.dot_general(keys, queries, (((1,), (1,)), ((), ())), preferred_element_type=F32)
    key_pos = key_block * BLOCK + lax.broadcasted_iota(jnp.int32, (BLOCK, BLOCK), 0)
    query_pos = query_block * BLOCK + lax.broadcasted_iota(jnp.int32, (BLOCK, BLOCK), 1)
    allowed = (key_pos <= query_pos) & (key_segs == query_segs)
    return jnp.where(allowed, scores * SCORE_SCALE, NEGATIVE)


def head_columns(part, head):
    start = part * LOCAL_WIDTH + head * HDIM
    return slice(start, start + HDIM)


def attend_kernel(order, qkv, seg_row, seg_col, mixed, mixed_line, logs, keys, values_t, scores):
    block = pl.program_id(0)
    count = pl.num_programs(0)

    @pl.when(block == 0)
    def _():
        @pl.loop(0, count)
        def _(at):
            here = pl.ds(pl.multiple_of(at * BLOCK, BLOCK), BLOCK)
            rows = pl.ds(pl.multiple_of(order[at] * BLOCK, BLOCK), BLOCK)
            keys[here, :] = qkv[rows, LOCAL_WIDTH : 2 * LOCAL_WIDTH]
            values_t[:, here] = qkv[rows, 2 * LOCAL_WIDTH :].T

    here = pl.ds(pl.multiple_of(block * BLOCK, BLOCK), BLOCK)
    rows = pl.ds(pl.multiple_of(order[block] * BLOCK, BLOCK), BLOCK)
    query_segs = seg_row[:, here]
    heads = range(LOCAL_HEADS)
    queries = [qkv[rows, head_columns(0, head)] for head in heads]

    def score_step(at, tops):
        spot = pl.ds(pl.multiple_of(at * BLOCK, BLOCK), BLOCK)
        new = []
        for head in heads:
            found = masked_scores(
                keys[spot, head_columns(0, head)], queries[head], at, block, seg_col[spot, :], query_segs
            )
            scores[head, spot, :] = found
            new.append(jnp.maximum(tops[head], jnp.max(found, axis=0, keepdims=True)))
        return tuple(new)

    lowest = jnp.full((1, BLOCK), NEGATIVE, F32)
    tops = lax.fori_loop(0, block + 1, score_step, (lowest,) * LOCAL_HEADS)

    def exponent_step(at, totals):
        spot = pl.ds(pl.multiple_of(at * BLOCK, BLOCK), BLOCK)
        new = []
        for head in heads:
            exponent = jnp.exp(scores[head, spot, :] - tops[head])
            scores[head, spot, :] = exponent
            new.append(totals[head] + jnp.sum(exponent, axis=0, keepdims=True))
        return tuple(new)

    zero = jnp.zeros((1, BLOCK), F32)
    totals = lax.fori_loop(0, block + 1, exponent_step, (zero,) * LOCAL_HEADS)
    scales = [1.0 / total for total in totals]

    def value_step(at, sums):
        spot = pl.ds(pl.multiple_of(at * BLOCK, BLOCK), BLOCK)
        new = []
        for head in heads:
            probs = (scores[head, spot, :] * scales[head]).astype(BF16)
            new.append(
                sums[head]
                + jnp.dot(values_t[head_columns(0, head), spot], probs, preferred_element_type=F32)
            )
        return tuple(new)

    empty = jnp.zeros((HDIM, BLOCK), F32)
    sums = lax.fori_loop(0, block + 1, value_step, (empty,) * LOCAL_HEADS)
    result = jnp.concatenate(sums, axis=0).T.astype(BF16)
    mixed[rows, :] = result
    mixed_line[here, :] = result
    for head in heads:
        logs[head : head + 1, here] = tops[head] + jnp.log(totals[head])


def attend_back_kernel(
    order, qkv, grads, logs, seg_row, seg_col, out, out_line, keys, keys_t, values, grad_k, grad_v, probs, grad_probs
):
    block = pl.program_id(0)
    count = pl.num_programs(0)

    @pl.when(block == 0)
    def _():
        grad_k[...] = jnp.zeros_like(grad_k)
        grad_v[...] = jnp.zeros_like(grad_v)

        @pl.loop(0, count)
        def _(at):
            here = pl.ds(pl.multiple_of(at * BLOCK, BLOCK), BLOCK)
            rows = pl.ds(pl.multiple_of(order[at] * BLOCK, BLOCK), BLOCK)
            found = qkv[rows, LOCAL_WIDTH : 2 * LOCAL_WIDTH]
            keys[here, :] = found
            keys_t[:, here] = found.T
            values[here, :] = qkv[rows, 2 * LOCAL_WIDTH :]

    here = pl.ds(pl.multiple_of(block * BLOCK, BLOCK), BLOCK)
    rows = pl.ds(pl.multiple_of(order[block] * BLOCK, BLOCK), BLOCK)
    query_segs = seg_row[:, here]
    heads = range(LOCAL_HEADS)
    queries = [qkv[rows, head_columns(0, head)] for head in heads]
    grads_here = [grads[rows, head_columns(0, head)] for head in heads]
    logs_here = [logs[head : head + 1, here] for head in heads]

    def score_step(at, inners):
        spot = pl.ds(pl.multiple_of(at * BLOCK, BLOCK), BLOCK)
        new = []
        for head in heads:
            found = masked_scores(
                keys[spot, head_columns(0, head)], queries[head], at, block, seg_col[spot, :], query_segs
            )
            found = jnp.exp(found - logs_here[head])
            reached = lax.dot_general(
                values[spot, head_columns(0, head)],
                grads_here[head],
                (((1,), (1,)), ((), ())),
                preferred_element_type=F32,
            )
            probs[head, spot, :] = found
            grad_probs[head, spot, :] = reached
            new.append(inners[head] + jnp.sum(found * reached, axis=0, keepdims=True))
        return tuple(new)

    zero = jnp.zeros((1, BLOCK), F32)
    inners = lax.fori_loop(0, block + 1, score_step, (zero,) * LOCAL_HEADS)

    def grad_step(at, sums):
        spot = pl.ds(pl.multiple_of(at * BLOCK, BLOCK), BLOCK)
        new = []
        for head in heads:
            found = probs[head, spot, :]
            grad_scores = (found * (grad_probs[head, spot, :] - inners[head])).astype(BF16)
            grad_k[head, spot, :] += jnp.dot(grad_scores, queries[head], preferred_element_type=F32)
            grad_v[head, spot, :] += jnp.dot(
                found.astype(BF16), grads_here[head], preferred_element_type=F32
            )
            new.append(
                sums[head]
                + jnp.dot(keys_t[head_columns(0, head), spot], grad_scores, preferred_element_type=F32)
            )
        return tuple(new)

    empty = jnp.zeros((HDIM, BLOCK), F32)
    sums = lax.fori_loop(0, block + 1, grad_step, (empty,) * LOCAL_HEADS)
    result = (jnp.concatenate(sums, axis=0) * SCORE_SCALE).T.astype(BF16)
    out[rows, :LOCAL_WIDTH] = result
    out_line[here, :LOCAL_WIDTH] = result

    @pl.when(block == count - 1)
    def _():
        @pl.loop(0, count)
        def _(at):
            here = pl.ds(pl.multiple_of(at * BLOCK, BLOCK), BLOCK)
            rows = pl.ds(pl.multiple_of(order[at] * BLOCK, BLOCK), BLOCK)
            for head in heads:
                for part, found in ((1, grad_k[head, here, :] * SCORE_SCALE), (2, grad_v[head, here, :])):
                    out[rows, head_columns(part, head)] = found.astype(BF16)
                    out_line[here, head_columns(part, head)] = found.astype(BF16)


def skip_awaited(kernel, used, count, *refs):
    kernel(*refs[:used], *refs[used + count :])


def attend(projected, order, segments, *awaited):
    rows = projected.shape[0]
    return pl.pallas_call(
        functools.partial(skip_awaited, attend_kernel, 4, len(awaited)),
        grid=(rows // BLOCK,),
        out_shape=(
            jax.ShapeDtypeStruct((rows, LOCAL_WIDTH), BF16),
            jax.ShapeDtypeStruct((rows, LOCAL_WIDTH), BF16),
            jax.ShapeDtypeStruct((LOCAL_HEADS, rows), F32),
        ),
        in_specs=[IN_SMEM] + [IN_VMEM] * 3 + [pl.BlockSpec(memory_space=pl.ANY)] * len(awaited),
        out_specs=(IN_VMEM,) * 3,
        scratch_shapes=[
            pltpu.VMEM((rows, LOCAL_WIDTH), BF16),
            pltpu.VMEM((LOCAL_WIDTH, rows), BF16),
            pltpu.VMEM((LOCAL_HEADS, rows, BLOCK), F32),
        ],
        compiler_params=pltpu.CompilerParams(vmem_limit_bytes=40 * 2**20),
        cost_estimate=pl.CostEstimate(flops=rows, bytes_accessed=rows, transcendentals=0),
    )(order, projected, segments[None, :], segments[:, None], *awaited)


def attend_back(projected, order, segments, log_total, grad_mixed, *awaited):
    rows = projected.shape[0]
    return pl.pallas_call(
        functools.partial(skip_awaited, attend_back_kernel, 6, len(awaited)),
        grid=(rows // BLOCK,),
        out_shape=(jax.ShapeDtypeStruct((rows, 3 * LOCAL_WIDTH), BF16),) * 2,
        in_specs=[IN_SMEM] + [IN_VMEM] * 5 + [pl.BlockSpec(memory_space=pl.ANY)] * len(awaited),
        out_specs=(IN_VMEM,) * 2,
        scratch_shapes=[
            pltpu.VMEM((rows, LOCAL_WIDTH), BF16),
            pltpu.VMEM((LOCAL_WIDTH, rows), BF16),
            pltpu.VMEM((rows, LOCAL_WIDTH), BF16),
            pltpu.VMEM((LOCAL_HEADS, rows, HDIM), F32),
            pltpu.VMEM((LOCAL_HEADS, rows, HDIM), F32),
            pltpu.VMEM((LOCAL_HEADS, rows, BLOCK), F32),
            pltpu.VMEM((LOCAL_HEADS, rows, BLOCK), F32),
        ],
        compiler_params=pltpu.CompilerParams(vmem_limit_bytes=40 * 2**20),
        cost_estimate=pl.CostEstimate(flops=rows, bytes_accessed=rows, transcendentals=0),
    )(order, projected, grad_mixed, log_total, segments[None, :], segments[:, None], *awaited)


def qkv_forward(normed_all, weight_heads):
    return dot_f32("td,dc->tc", normed_all, weight_heads[:, : 3 * LOCAL_WIDTH]).astype(BF16)


def out_forward(mixed, weight_heads):
    return dot_f32("td,od->to", mixed, weight_heads[:, 3 * LOCAL_WIDTH :])


def feed_forward(normed_all, weight_up, weight_down):
    hidden = dot_f32("td,fd->tf", normed_all, weight_up)
    active = gelu_tanh(hidden).astype(BF16)
    return dot_f32("tf,fd->td", active, weight_down), hidden, active


def feed_backward(weight_up, weight_down, hidden, grad_low):
    grad_active = dot_f32("td,fd->tf", grad_low, weight_down)
    grad_hidden = jax.vjp(gelu_tanh, hidden)[1](grad_active)[0].astype(BF16)
    return grad_hidden, dot_f32("tf,fd->td", grad_hidden, weight_up)


def times(rows, gram):
    return jnp.dot(rows.astype(BF16), gram, preferred_element_type=F32)


def newton_two(rows, gram, scale):
    def polynomial(values):
        once = times(values, gram)
        return NEWTON_A * values + NEWTON_B * once + NEWTON_C * times(once, gram)

    first = polynomial(rows / scale)
    once = polynomial(times(polynomial(first), gram))
    twice = polynomial(times(polynomial(once), gram))
    return NEWTON_A * first + NEWTON_B * once + NEWTON_C * twice


def exact(left, right):
    return jnp.dot(left, right, precision=HIGHEST)


def newton_heads(block):
    gram = jnp.einsum("br,cr->bc", block, block, precision=HIGHEST)
    scale = jnp.sqrt(jnp.trace(gram)) + NEWTON_EPSILON
    gram = gram / (scale * scale)
    one = jnp.eye(HDIM, dtype=F32)
    first = NEWTON_A * one + NEWTON_B * gram + NEWTON_C * exact(gram, gram)
    gram = exact(exact(first, gram), first)
    second = NEWTON_A * one + NEWTON_B * gram + NEWTON_C * exact(gram, gram)
    return exact(exact(second, first), block / scale)


def body(
    inputs,
    cotangent,
    segment_ids,
    routed,
    qkv_master,
    out_master,
    up_master,
    down_master,
    qkv_moment,
    out_moment,
    up_moment,
    down_moment,
    router,
    router_first,
    router_second,
):
    masters = (qkv_master, out_master, up_master, down_master)
    token_count = inputs.shape[0]
    core, place_z = lax.axis_index("c"), lax.axis_index("z")
    batch_index = 2 * place_z + core
    all_tokens = jnp.arange(token_count * N_BATCH)

    at = jnp.arange(N_BATCH)
    order = (4 * ((at + core) % 2) + (at // 2 - place_z) % 4).astype(jnp.int32)
    block_of = 2 * ((at % 4 + place_z) % 4) + (at // 4 + core) % 2
    row_pos = (block_of[:, None] * token_count + jnp.arange(token_count)[None, :]).reshape(-1)
    single = jnp.zeros((1,), jnp.int32)

    normed_round = gather_near(rms_norm(inputs).astype(BF16))
    heads_local = head_shards(masters)
    wide_dense = jnp.stack([up_master[0], down_master[0]]).astype(BF16)
    wide_dense = lax.all_gather(wide_dense, FSDP, axis=1, tiled=True)
    up_dense, down_dense = wide_dense[0], wide_dense[1]
    out_low = jnp.concatenate([out_master[0], out_master[1]], axis=1).astype(BF16)
    out_low = lax.all_gather(out_low, EVERY, axis=0, tiled=True)
    out_dense, out_routed = out_low[:, :D], out_low[:, D:]
    wide_routed = jnp.stack([up_master[1], down_master[1]]).astype(BF16)
    wide_routed = lax.all_gather(wide_routed, FSDP, axis=1, tiled=True)
    up_routed, down_routed = wide_routed[0], wide_routed[1]
    heads_dense = gather_fsdp(heads_local[0])
    normed_low = gather_value(gather_core(gather_far(normed_round)))

    chosen = routed[0]
    local_index = chosen - batch_index * token_count
    pick = (local_index[:, None] == jnp.arange(token_count)[None, :]).astype(F32)
    pick_all = (chosen[:, None] == row_pos[None, :]).astype(BF16)
    not_routed = 1.0 - jnp.max(pick, axis=0)[:, None]
    rest_grads = cotangent * not_routed
    segment_blocks = segment_ids.astype(F32)[None, :]
    segment_blocks = jnp.concatenate([segment_blocks, shift(segment_blocks, "c", 1)], axis=0)
    segment_blocks = jnp.concatenate(
        [segment_blocks] + [shift(segment_blocks, "z", step) for step in (1, 2, 3)], axis=0
    )
    segments_all = jnp.sum(
        jnp.where((column_spots()[:, None] == at[None, :])[:, :, None], segment_blocks[:, None, :], 0.0),
        axis=0,
    ).reshape(-1)
    slot_segments = jnp.sum(
        jnp.where(chosen[:, None] == all_tokens[None, :], segments_all[None, :], 0.0), axis=1
    )

    moments_heads = jnp.concatenate([qkv_moment, out_moment], axis=2).reshape(
        2, 8, 4, N_BATCH, LOCAL_HEADS, HDIM
    )
    moments_heads = jnp.transpose(moments_heads, (0, 2, 4, 3, 1, 5)).reshape(128, 8, HDIM)
    moment_block = lax.all_to_all(
        moments_heads, EVERY, split_axis=0, concat_axis=0, tiled=True
    ).reshape(D, HDIM)
    moment_block = jnp.transpose(moment_block)

    def of_slots(values):
        return jnp.einsum("st,td->sd", pick_all, values, preferred_element_type=F32).astype(BF16)

    start_rows = jnp.einsum("st,td->sd", pick, inputs, precision=HIGHEST)
    start_round = sum_near(sum_core(after(start_rows, *normed_round[1]), F32))
    slot_inputs = sum_value(sum_last(sum_next(start_round)))
    heads_routed = gather_fsdp(heads_local[1])
    projected = qkv_forward(normed_low, heads_dense)
    rest_round = gather_near(after(rest_grads.astype(BF16), normed_low))
    mixed_low, mixed_line, log_total = attend(
        projected, order, segments_all, moment_block, heads_routed, slot_inputs, rest_round[0][0]
    )
    mixed_slots = of_slots(mixed_low)

    slot_round = columns_core(mixed_slots)
    slot_round = columns_near(slot_round)
    slot_middle = slot_inputs + dot_f32("td,od->to", columns_value(slot_round), out_dense)
    slot_two = rms_norm(slot_middle).astype(BF16)
    slot_fed, slot_hidden, slot_active = feed_forward(slot_two, up_dense, down_dense)

    fed_round = sum_core(slot_fed)
    mixed_round = rows_core(after(mixed_low, *fed_round[0]))
    fed_round = sum_near(fed_round)
    mixed_round = rows_near(mixed_round)
    fed_round, mixed_rows = during(fed_round, lambda late: columns_value(mixed_round))
    fed_round = sum_next(fed_round)

    def rest_forward(late):
        middle = inputs + dot_f32("td,od->to", late(mixed_rows), out_dense)
        return middle, rms_norm(middle).astype(BF16)

    fed_round, (middle, rest_two_low) = during(fed_round, rest_forward)
    fed_round = sum_last(fed_round)
    two_round = gather_near(after(rest_two_low, *fed_round[0]))
    slot_rows = slot_middle + sum_value(fed_round)

    slot_normed = rms_norm(slot_rows)
    slot_low = slot_normed.astype(BF16)
    r_projected = qkv_forward(slot_low, heads_routed)
    r_mixed, _, r_log_total = attend(r_projected, single, slot_segments)
    r_round = columns_core(r_mixed)
    gate_values = jnp.dot(slot_normed, router, precision=HIGHEST)
    r_round = columns_near(r_round)
    two_round = gather_far((two_round[0], lax.optimization_barrier(two_round[1] + r_round[0])[:2]))
    r_attended = dot_f32("td,od->to", columns_value(r_round), out_routed)
    r_middle = slot_rows + r_attended
    r_two = rms_norm(r_middle).astype(BF16)
    r_fed_part, r_hidden, r_active = feed_forward(r_two, up_routed, down_routed)
    rest_round = gather_far((rest_round[0], lax.optimization_barrier(rest_round[1] + (r_two,))[:2]))

    r_round = sum_core(r_fed_part)
    two_round = gather_core((two_round[0], lax.optimization_barrier(two_round[1] + r_round[0])[:2]))
    r_round = sum_near(r_round)
    r_round, normed_two = during(r_round, lambda late: gather_value(two_round))
    r_round = sum_next(r_round)

    def rest_active(late):
        _, hidden, active = feed_forward(late(normed_two), up_dense, down_dense)
        return hidden, active

    r_round, (feed_hidden, feed_active) = during(r_round, rest_active)
    rest_round = gather_core((rest_round[0], lax.optimization_barrier(rest_round[1] + (feed_active,))[:2]))
    r_round = sum_last(r_round)
    r_round, rest_low = during(r_round, lambda late: gather_value(rest_round))
    routed_branch = r_attended + sum_value(r_round)

    grads_round = sum_near(
        sum_core(after(jnp.einsum("st,td->sd", pick, cotangent, precision=HIGHEST), mixed_low), F32)
    )
    slot_grads = sum_value(sum_last(sum_next(grads_round)))
    branch_grads = gate_values[:, None] * slot_grads
    branch_low = branch_grads.astype(BF16)
    r_grad_hidden, r_grad_two = feed_backward(up_routed, down_routed, r_hidden, branch_low)

    r_round = sum_near(sum_core(r_grad_two))

    def rest_back(late):
        return feed_backward(up_dense, down_dense, feed_hidden, late(rest_low))

    r_round, (rest_hidden, rest_two) = during(r_round, rest_back)
    back_round = scatter_core(rest_two)
    r_round = sum_next(r_round)
    r_round, gate_grads = during(r_round, lambda late: jnp.sum(late(slot_grads) * routed_branch, axis=1))
    back_round = scatter_far((back_round[0], lax.optimization_barrier(back_round[1] + r_round[0])[:1]))
    r_round = sum_last(r_round)
    r_grad_mid = norm_back(r_middle, sum_value(r_round))
    r_grad_low = (r_grad_mid + branch_grads).astype(BF16)

    def out_back(grad_low, weight_heads):
        return dot_f32("to,od->td", grad_low, weight_heads[:, 3 * LOCAL_WIDTH :]).astype(BF16)

    r_grad_projected, _ = attend_back(
        r_projected, single, slot_segments, r_log_total, out_back(r_grad_low, heads_routed)
    )
    r_round = sum_core(dot_f32("tc,dc->td", r_grad_projected, heads_routed[:, : 3 * LOCAL_WIDTH]))
    back_round = scatter_near((back_round[0], lax.optimization_barrier(back_round[1] + r_round[0])[:2]))
    r_round = sum_near(r_round)

    def routed_weights(late):
        return (
            dot_f32("tf,td->fd", late(r_grad_hidden), r_two),
            dot_f32("tf,td->fd", r_active, late(branch_low)),
        )

    r_round, (r_grad_up, r_grad_down) = during(r_round, routed_weights)
    r_round = sum_next(r_round)

    def rest_middle(late):
        rest_mid = rest_grads + norm_back(middle, late(scatter_value(back_round)))
        rest_mid_low = rest_mid.astype(BF16)
        return rest_mid, rest_mid_low, dot_f32("to,od->td", rest_mid_low, out_dense).astype(BF16)

    r_round, (rest_mid, rest_mid_low, rest_mixed) = during(r_round, rest_middle)
    rest_mid_all = lax.all_gather(rest_mid_low, BATCH, axis=0, tiled=True)
    r_round = sum_last(r_round)
    back_round = back_core(after(rest_mixed, *r_round[0]))
    r_grad_normed = sum_value(r_round)
    slot_out_grads = (
        slot_grads
        + r_grad_mid
        + norm_back(slot_rows, r_grad_normed + gate_grads[:, None] * router[None, :])
    )

    slot_out_low = slot_out_grads.astype(BF16)
    slot_grad_hidden, slot_grad_two = feed_backward(up_dense, down_dense, slot_hidden, slot_out_low)
    slot_round = sum_core(slot_grad_two)
    back_round = back_near((back_round[0], lax.optimization_barrier(back_round[1] + slot_round[0])[:1]))
    slot_round = sum_near(slot_round)
    slot_round, rest_up = during(
        slot_round, lambda late: dot_f32("tf,td->fd", late(rest_hidden), normed_two)
    )
    slot_round = sum_next(slot_round)
    slot_round, rest_down = during(
        slot_round, lambda late: dot_f32("tf,td->fd", feed_active, late(rest_low))
    )
    slot_round = sum_last(slot_round)
    slot_mid = slot_out_grads + norm_back(slot_middle, sum_value(slot_round))
    slot_mid_low = slot_mid.astype(BF16)
    slot_mixed = out_back(slot_mid_low, heads_dense)
    grad_mixed = (
        back_value(back_round).astype(F32)
        + jnp.einsum("st,sd->td", pick_all, slot_mixed, preferred_element_type=F32)
    ).astype(BF16)
    grad_up = rest_up + dot_f32("tf,td->fd", slot_grad_hidden, slot_two)
    grad_down = rest_down + dot_f32("tf,td->fd", slot_active, slot_out_low)
    wide_round = scatter_fsdp_first(grad_up, grad_down)
    grad_mixed = after(grad_mixed, *wide_round[0])
    grad_projected, grad_projected_line = attend_back(projected, order, segments_all, log_total, grad_mixed)

    routed_wide = lax.psum_scatter(
        jnp.stack([r_grad_up, r_grad_down]), FSDP, scatter_dimension=1, tiled=True
    )
    wide_round = (
        wide_round[0],
        lax.optimization_barrier(wide_round[1] + (grad_projected, routed_wide))[:3],
    )
    wide_round = scatter_fsdp_second(wide_round)

    def dense_weights(late):
        grads = late(grad_projected)
        grad_qkv = dot_f32("tc,td->cd", grads, normed_low)
        grad_out = dot_f32("td,to->do", mixed_line, rest_mid_all) + dot_f32(
            "td,to->do", mixed_slots, slot_mid_low
        )
        return grad_qkv, grad_out

    wide_round, (grad_qkv, grad_out) = during(wide_round, dense_weights)
    dense_wide = scatter_fsdp_value(wide_round)

    r_grad_qkv = dot_f32("tc,td->cd", r_grad_projected, slot_low)
    r_grad_out = dot_f32("td,to->do", r_mixed, r_grad_low)
    block_parts = jnp.concatenate([grad_qkv, grad_out, r_grad_qkv, r_grad_out], axis=0).astype(BF16)
    router_grad = jnp.dot(gate_grads, slot_normed, precision=HIGHEST)
    router_high = router_grad.astype(BF16)
    router_low = (router_grad - router_high.astype(F32)).astype(BF16)
    router_rows = jnp.concatenate(
        [router_high[None, :], router_low[None, :], jnp.zeros((14, D), BF16)], axis=0
    )
    block_parts = jnp.concatenate(
        [block_parts.reshape(16, HDIM, D), jnp.broadcast_to(router_rows[None], (16, 16, D))], axis=1
    )
    block_grads = lax.all_to_all(block_parts, FSDP, split_axis=0, concat_axis=0, tiled=True)

    new_up_moment = MOMENTUM * up_moment + jnp.stack([dense_wide[0], routed_wide[0]])
    new_down_moment = MOMENTUM * down_moment + jnp.stack([dense_wide[1], routed_wide[1]])
    wide_own = after(jnp.concatenate([new_up_moment, new_down_moment], axis=0), block_parts)
    wide_rows = lax.all_to_all(wide_own, "z", split_axis=0, concat_axis=0, tiled=True).reshape(128, D)
    grad_normed = dot_f32(
        "tc,dc->td", after(grad_projected_line, block_parts), heads_dense[:, : 3 * LOCAL_WIDTH]
    )
    rows_low = wide_rows.astype(BF16)
    rows_both = jnp.concatenate([rows_low, shift(rows_low, "c", 1)], axis=0)
    rows_both = after(rows_both, grad_normed, block_grads)
    grad_normed = lax.psum_scatter(grad_normed, BATCH, scatter_dimension=0, tiled=True)
    own_columns = lax.dynamic_slice_in_dim(rows_both, core * (D // 2), D // 2, 1)
    gram_part = dot_f32("rb,rc->bc", own_columns, rows_both)

    def heads_step(late):
        grads = jnp.sum(late(block_grads).astype(F32), axis=0)
        new_block = MOMENTUM * moment_block + grads[:HDIM]
        ortho_block = newton_heads(new_block)
        returned = jnp.transpose(jnp.concatenate([new_block, ortho_block], axis=0))
        return returned.reshape(128, 8, 2 * HDIM), grads[HDIM] + grads[HDIM + 1]

    def fed_step(late):
        spots = jnp.argsort(order).astype(jnp.int32)
        fed_line = place([late(feed_active)], spots, N_BATCH)
        return dot_f32("tf,fd->td", fed_line, down_dense)

    gram_round = turn_first(gram_part)
    gram_round, (returned, router_total) = during(gram_round, heads_step)
    gram_round = turn_second(gram_round)
    returned = lax.all_to_all(returned, EVERY, split_axis=0, concat_axis=0, tiled=True)
    gram_round = turn_third(gram_round)
    gram_round = turn_fourth(gram_round)
    gram_round, fed_line = during(gram_round, fed_step)
    fed_rows = lax.psum_scatter(after(fed_line, grad_normed), BATCH, scatter_dimension=0, tiled=True)
    gram_half = turn_value(gram_round)
    gram_other = shift(gram_half, "c", 1)
    wide_gram = jnp.concatenate(
        [jnp.where(core == 0, gram_half, gram_other), jnp.where(core == 0, gram_other, gram_half)],
        axis=0,
    )
    wide_scale = jnp.sqrt(jnp.trace(wide_gram.astype(F32))) + NEWTON_EPSILON
    wide_gram = (wide_gram.astype(F32) / (wide_scale * wide_scale)).astype(BF16)
    wide_ortho = newton_two(wide_rows, wide_gram, wide_scale).reshape(4, 32, D)
    wide_ortho = lax.all_to_all(wide_ortho, "z", split_axis=0, concat_axis=0, tiled=True)

    grad_mid = rest_mid + jnp.einsum("st,sd->td", pick, slot_mid, precision=HIGHEST)
    grad_inputs = grad_mid + norm_back(inputs, grad_normed)
    mixed = (
        middle
        + fed_rows
        + jnp.einsum("st,sd->td", pick, gate_values[:, None] * routed_branch, precision=HIGHEST)
    )

    returned = returned.reshape(2, 4, LOCAL_HEADS, N_BATCH, 8, 2, HDIM)
    returned = jnp.transpose(returned, (5, 0, 4, 1, 3, 2, 6)).reshape(2, 2, 8, 4 * D)
    new_moments = (returned[0, :, :, : 3 * D], returned[0, :, :, 3 * D :], new_up_moment, new_down_moment)
    orthos = (returned[1, :, :, : 3 * D], returned[1, :, :, 3 * D :], wide_ortho[:2], wide_ortho[2:])

    widths = (HDIM, HDIM, D, D)
    full_rows = (D, D, FF, FF)
    new_masters = []
    for index_type in range(4):
        rate = STEP_RATES[index_type]
        factor = 0.2 * math.sqrt(max(full_rows[index_type], widths[index_type]))
        new_masters.append(
            masters[index_type] * (1.0 - rate * WEIGHT_DECAY) - rate * factor * orthos[index_type]
        )
    first_new = FIRST_DECAY * router_first + (1.0 - FIRST_DECAY) * router_total
    second_new = SECOND_DECAY * router_second + (1.0 - SECOND_DECAY) * router_total * router_total
    corrected_first = first_new / (1.0 - FIRST_DECAY**STEP)
    corrected_second = second_new / (1.0 - SECOND_DECAY**STEP)
    router_new = router * (1.0 - ADAM_RATE * WEIGHT_DECAY) - ADAM_RATE * corrected_first / (
        jnp.sqrt(corrected_second) + ADAM_EPSILON
    )
    return (
        (mixed, grad_inputs)
        + new_moments
        + tuple(new_masters)
        + tuple(master.astype(BF16) for master in new_masters)
        + (router_new, first_new, second_new)
    )


def solution(mesh):
    fine = Mesh(mesh.devices.reshape(4, 4, 4, 2), EVERY)
    tokens = P(EVERY, None)
    weights = P(None, EVERY, None)
    return jax.shard_map(
        body,
        mesh=fine,
        in_specs=(tokens, tokens, P(EVERY), P(FSDP, None)) + (weights,) * 8 + (P(),) * 3,
        out_specs=(tokens, tokens) + (weights,) * 12 + (P(),) * 3,
        check_vma=False,
    )
```

time: 1600 us -> 664 us (0.41)
  waiting for transfers between devices: 1030 us -> 144 us
  matrix products: 296 us -> 106 us
  starting transfers between devices: 18.6 us -> 184 us
  blocking collectives: 109 us -> 15.2 us
  Pallas kernels: 0 us -> 76.4 us
  other arithmetic: 78.5 us -> 57.6 us
    reduce_scatter x8 -> x3, waiting for transfers between devices: 431 us -> 0.02 us  [the longest x1 0.02 us: body(): lax.psum_scatter(jnp.stack([r_grad_up, r_grad_down]), FSDP, scatter_dimen...]
    all_gather x10 -> x4, waiting for transfers between devices: 349 us -> 0.03 us  [the longest x1 0.02 us: body(): wide_dense = lax.all_gather(wide_dense, FSDP, axis=1, tiled=True)]
    psum x5 -> x0, waiting for transfers between devices: 243 us -> none  [the longest x1 65.5 us: body(): routed_branch = r_attended + lax.psum(r_fed_part, BATCH)]
    dot_general x36 -> x33, matrix products: 255 us -> 77 us  [dot_f32(): return jnp.einsum(pattern, left, right, preferred_element_type=F32)]
    ppermute x0 -> x114, starting transfers between devices: none -> 146 us  [the longest x56 75.8 us: shift(): lax.ppermute(values, axis, [(i, (i + step) % size) for i in range(size)])]
    ppermute x0 -> x114, waiting for transfers between devices: none -> 98.7 us  [the longest x56 52.7 us: shift(): lax.ppermute(values, axis, [(i, (i + step) % size) for i in range(size)])]
    pallas_call x0 -> x22, Pallas kernels: none -> 76.4 us  [the longest x2 29.7 us: attend_back(): pl.pallas_call(functools.partial(skip_awaited, attend_back_kernel, 6, len...]
    psum x1 -> x0, blocking collectives: 68.3 us -> none  [body(): router_total = lax.psum(router_grad, EVERY)]
  transfers between devices with their start and end apart: 27 -> 126, of which waited for: 23 -> 51; matrix products, arithmetic and copies ran while one was open for 18% -> 27% of each run, Pallas kernels for 0% -> 11%
where the time goes in v2:
time: 664 us; the launch traced here: 653 us
  starting transfers between devices  184 us (28%)
  waiting for transfers between devices  144 us (22%)
  matrix products  106 us (16%)
  Pallas kernels  76.4 us (12%)
  other arithmetic  57.6 us (9%)
  local copies, waits for them, and re-layouts  51.4 us (8%)
  between operations  18.7 us (3%)
  blocking collectives  15.2 us (2%)
    dot_general x33, matrix products, dot_f32(): return jnp.einsum(pattern, left, right, preferred_element_type=F32)  77 us
    ppermute x56, starting transfers between devices, shift(): lax.ppermute(values, axis, [(i, (i + step) % size) for i in range(size)])  75.8 us
    ppermute x56, waiting for transfers between devices, shift(): lax.ppermute(values, axis, [(i, (i + step) % size) for i in range(size)])  52.7 us
    ppermute x30, starting transfers between devices, turn(): return lax.ppermute(values, ('y', 'x', 'c'), pairs)  39.5 us
    ppermute x28, waiting for transfers between devices, pair(): return lax.ppermute(values, axis, [(i, partner(i)) for i in range(4)])  32.8 us
    all_to_all x1, waiting for transfers between devices, body(): lax.all_to_all(block_parts, FSDP, split_axis=0, concat_axis=0, tiled=True)  31.2 us
    ppermute x28, starting transfers between devices, pair(): return lax.ppermute(values, axis, [(i, partner(i)) for i in range(4)])  30.6 us
    pallas_call x2, Pallas kernels, attend_back(): pl.pallas_call(functools.partial(skip_awaited, attend_back_kernel, 6, len...  29.7 us
  transfers between devices with their start and end apart: 126, of which 51 were waited for; matrix products, arithmetic and copies ran while one was open for 27% of the time, Pallas kernels for 11%

profile of v2, /device:TPU:1, one launch (start us, length us, event | category | flops | bytes accessed | tf_op | source)
XLA Modules:
  0.0 653.5 jit_solution(13485764639670601593)
XLA Ops:
  12.1 4.7 collective-permute-start
  17.5 5.5 all-to-all-start
  52.6 10.3 %all-to-all-start.1 = ((f32[128,1,512]{2,1,0:T(1,128)}), f32[128,1,512]{2,1,0:T(1,128)}, u32[]{:S(2)}, u32[]{:S(2)}) async-start(f32[128,1,512]{2,1,0:T(1,128)} %reshape.463), calls=%async_computation.1 | async-start | bytes 524288 | tf_op jit(solution)/shard_map/all_to_all | solution.py:777
  113.2 22.6 %shard_map.284 = (bf16[2048,128]{1,0:T(8,128)(2,1)S(1)}, bf16[2048,128]{1,0:T(8,128)(2,1)S(1)}, f32[2,2048]{1,0:T(2,128)S(1)}) custom-call(s32[8]{0:T(128)S(1)} %fusion.202.refs_0_, bf16[2048,384]{1,0:T(8,128)(2,1)S(1)} %convolution_convert_fusion.refs_1_, f32[1,2048]{1,0:T(1,128)S(1)} %bitcast.265, f32[2048,1]{1,0:T(8,128)S(1)} %bitcast.261, ...), custom_call_target="tpu_custom_call" | custom-call | flops 2048 | bytes 2048 | tf_op jit(solution)/shard_map/pallas_call | solution.py:619
  145.7 3.8 collective-permute-done.29.refs_2_
  151.5 3.7 multiply_reduce_fusion.9
  169.4 4.1 collective-permute-done.34.refs_3_
  207.6 3.7 multiply_reduce_fusion.6
  215.9 3.8 collective-permute-start.50
  239.8 6.6 %collective-permute-done.60 = f32[64,1024]{1,0:T(8,128)S(1)} collective-permute-done((f32[64,1024]{1,0:T(8,128)S(1)}, f32[64,1024]{1,0:T(8,128)S(1)}, u32[]{:S(2)}, u32[]{:S(2)}) %collective-permute-start.60) | collective-permute-done | bytes 262176 | tf_op jit(solution)/shard_map/ppermute | solution.py:69
  251.8 11.6 %collective-permute-done.53 = bf16[256,1024]{1,0:T(8,128)(2,1)S(1)} collective-permute-done((bf16[256,1024]{1,0:T(8,128)(2,1)S(1)}, bf16[256,1024]{1,0:T(8,128)(2,1)S(1)}, u32[]{:S(2)}, u32[]{:S(2)}) %collective-permute-start.53) | collective-permute-done | bytes 524320 | tf_op jit(solution)/shard_map/ppermute | solution.py:65
  274.6 6.0 multiply_convert_fusion
  295.6 7.7 %fusion.8 = bf16[2048,512]{1,0:T(8,128)(2,1)S(1)} fusion(f32[2048,512]{1,0:T(8,128)} %get-tuple-element.328, bf16[2048,1024]{1,0:T(8,128)(2,1)S(1)} %shard_map.292, bf16[2,512,1024]{2,1,0:T(8,128)(2,1)S(1)} %copy-done.69), kind=kOutput, calls=%fused_computation.13 | convolution fusion | flops 2168455168 | bytes 11534336 | tf_op jit(solution)/shard_map/td,fd->tf/dot_general | solution.py:60
  303.3 5.7 fusion.61
  311.1 4.1 collective-permute-done.67
  327.3 4.0 slice.657
  342.3 3.8 collective-permute-done.79
  350.8 10.9 %collective-permute-done.74 = bf16[64,1024]{1,0:T(8,128)(2,1)S(1)} collective-permute-done((bf16[64,1024]{1,0:T(8,128)(2,1)S(1)}, bf16[64,1024]{1,0:T(8,128)(2,1)S(1)}, u32[]{:S(2)}, u32[]{:S(2)}) %collective-permute-start.74) | collective-permute-done | bytes 131104 | tf_op jit(solution)/shard_map/ppermute | solution.py:69
  389.5 3.8 collective-permute-start.92
  393.5 4.7 fusion.260
  419.6 28.0 %shard_map.296 = (bf16[2048,384]{1,0:T(8,128)(2,1)S(1)}, bf16[2048,384]{1,0:T(8,128)(2,1)S(1)}) custom-call(s32[8]{0:T(128)S(1)} %fusion.202.refs_0_, bf16[2048,384]{1,0:T(8,128)(2,1)S(1)} %copy-done.1, bf16[2048,128]{1,0:T(8,128)(2,1)S(1)} %add_convert_fusion.refs_2_, f32[2,2048]{1,0:T(2,128)S(1)} %get-tuple-element.160.refs_3_, f32[1,2048]{1,0:T(1,128)S(1)} %bitcast.266, ...), custom_call_target="tpu_custom_call" | custom-call | flops 2048 | bytes 2048 | tf_op jit(solution)/shard_map/pallas_call | solution.py:641
  453.8 5.0 fusion.262
  464.2 5.6 fusion.85
  479.3 15.2 %all_to_all.30 = f32[4,32,1024]{2,1,0:T(8,128)S(1)} all-to-all(f32[4,32,1024]{2,1,0:T(8,128)S(1)} %pad_maximum_fusion.12), channel_id=1, replica_groups=mesh['y'=4,'x'=4,'z'=4,'c'=2] {'z'}, dimensions={0} | all-to-all | bytes 1048576 | tf_op jit(solution)/shard_map/all_to_all | solution.py:968
  494.6 5.9 all-to-all-start.3
  504.0 31.2 %all-to-all-done.3 = bf16[16,80,1024]{2,1,0:T(8,128)(2,1)} async-done(((bf16[16,80,1024]{2,1,0:T(8,128)(2,1)}), bf16[16,80,1024]{2,1,0:T(8,128)(2,1)}, u32[]{:S(2)}, u32[]{:S(2)}) %all-to-all-start.3) | async-done | bytes 2621472 | tf_op jit(solution)/shard_map/all_to_all | solution.py:963
  565.5 5.6 fusion.57
  571.2 11.6 %all-to-all-start.4 = ((f32[128,8,128]{2,1,0:T(8,128)}), f32[128,8,128]{2,1,0:T(8,128)S(1)}, u32[]{:S(2)}, u32[]{:S(2)}) async-start(f32[128,8,128]{2,1,0:T(8,128)} %bitcast.66), calls=%async_computation.7 | async-start | bytes 1048576 | tf_op jit(solution)/shard_map/all_to_all | solution.py:994
  588.6 7.8 %all-to-all-done.4 = f32[128,8,128]{2,1,0:T(8,128)S(1)} async-done(((f32[128,8,128]{2,1,0:T(8,128)}), f32[128,8,128]{2,1,0:T(8,128)S(1)}, u32[]{:S(2)}, u32[]{:S(2)}) %all-to-all-start.4) | async-done | bytes 524320 | tf_op jit(solution)/shard_map/all_to_all | solution.py:994
  623.5 4.3 all-to-all-start.5
  630.8 6.3 all-to-all-done.5
  642.7 3.7 convolution_add_fusion.3
  (822 shorter events, 373.5 us)
Async XLA Ops:
  7.2 144.3 %all-gather.5.cloned.1.call-start = ((), (), s32[]{:S(2)}) async-start(), calls=%async_computation.9 | async-start | bytes 4227072 | tf_op jit(solution)/shard_map/all_gather | solution.py:746
  17.5 35.0 %all-to-all-start = ((bf16[8,2,8,512]{3,2,1,0:T(8,128)(2,1)}), bf16[8,2,8,512]{3,2,1,0:T(8,128)(2,1)S(1)}, u32[]{:S(2)}, u32[]{:S(2)}) async-start(bf16[8,2,8,512]{3,2,1,0:T(8,128)(2,1)} %bitcast.260), calls=%async_computation | async-start | bytes 262144 | tf_op jit(solution)/shard_map/all_to_all | solution.py:443
  23.0 132.3 %all-gather.7.cloned.1.call-start = ((), (), s32[]{:S(2)}) async-start(), calls=%async_computation.10 | async-start | bytes 2228224 | tf_op jit(solution)/shard_map/all_gather | solution.py:743
  23.6 20.6 %collective-permute-start.11 = (f32[1,256]{1,0:T(1,128)}, f32[1,256]{1,0:T(1,128)}, u32[]{:S(2)}, u32[]{:S(2)}) collective-permute-start(f32[1,256]{1,0:T(1,128)} %bitcast.5), channel_id=1, source_target_pairs={{0,1},{1,0},{2,3},{3,2},{4,5},{5,4},{6,7},{7,6},{8,9},{9,8},{10,11... | collective-permute-start | bytes 3080 | tf_op jit(solution)/shard_map/ppermute | solution.py:65
  43.9 19.0 %collective-permute-start.22 = (f32[64,1024]{1,0:T(8,128)S(1)}, f32[64,1024]{1,0:T(8,128)S(1)}, u32[]{:S(2)}, u32[]{:S(2)}) collective-permute-start(f32[64,1024]{1,0:T(8,128)S(1)} %get-tuple-element.267), channel_id=1, source_target_pairs={{0,2},{2,0},{4,6},{6,4},{1,3},{3,1},{5,7},{7,5},{8,10},{10,8},{12,... | collective-permute-start | bytes 786440 | tf_op jit(solution)/shard_map/ppermute | solution.py:69
  44.0 20.4 %collective-permute-start.24 = (f32[64,1024]{1,0:T(8,128)S(1)}, f32[64,1024]{1,0:T(8,128)S(1)}, u32[]{:S(2)}, u32[]{:S(2)}) collective-permute-start(f32[64,1024]{1,0:T(8,128)S(1)} %get-tuple-element.268), channel_id=1, source_target_pairs={{0,6},{2,4},{4,2},{6,0},{1,7},{3,5},{5,3},{7,1},{8,14},{10,12},{12... | collective-permute-start | bytes 786440 | tf_op jit(solution)/shard_map/ppermute | solution.py:69
  44.8 22.8 %collective-permute-start.12 = (f32[2,256]{1,0:T(2,128)S(1)}, f32[2,256]{1,0:T(2,128)S(1)}, u32[]{:S(2)}, u32[]{:S(2)}) collective-permute-start(f32[2,256]{1,0:T(2,128)S(1)} %pad_maximum_fusion.32), channel_id=1, source_target_pairs={{0,2},{2,4},{4,6},{6,0},{1,3},{3,5},{5,7},{7,1},{8,10},{10,12},{12... | collective-permute-start | bytes 6152 | tf_op jit(solution)/shard_map/ppermute | solution.py:65
  48.1 20.1 %collective-permute-start.13 = (f32[2,256]{1,0:T(2,128)S(1)}, f32[2,256]{1,0:T(2,128)S(1)}, u32[]{:S(2)}, u32[]{:S(2)}) collective-permute-start(f32[2,256]{1,0:T(2,128)S(1)} %pad_maximum_fusion.32), channel_id=1, source_target_pairs={{0,4},{2,6},{4,0},{6,2},{1,5},{3,7},{5,1},{7,3},{8,12},{10,14},{12... | collective-permute-start | bytes 6152 | tf_op jit(solution)/shard_map/ppermute | solution.py:65
  50.7 56.7 %collective-permute-start.4 = (bf16[1024,1024]{1,0:T(8,128)(2,1)}, bf16[1024,1024]{1,0:T(8,128)(2,1)}, u32[]{:S(2)}, u32[]{:S(2)}) collective-permute-start(bf16[1024,1024]{1,0:T(8,128)(2,1)} %shard_map.278.refs_0_), channel_id=1, source_target_pairs={{0,1},{1,0},{2,3},{3,2},{4,5},{5,4},{6,7},{7,6},{8,9},{9,8},{10,11... | collective-permute-start | bytes 6291464 | tf_op jit(solution)/shard_map/ppermute | solution.py:65
  52.6 45.5 %all-to-all-start.1 = ((f32[128,1,512]{2,1,0:T(1,128)}), f32[128,1,512]{2,1,0:T(1,128)}, u32[]{:S(2)}, u32[]{:S(2)}) async-start(f32[128,1,512]{2,1,0:T(1,128)} %reshape.463), calls=%async_computation.1 | async-start | bytes 524288 | tf_op jit(solution)/shard_map/all_to_all | solution.py:777
  62.9 150.5 %all-gather.9.cloned.1.call-start = ((), (), s32[]{:S(2)}) async-start(), calls=%async_computation.11 | async-start | bytes 2228224 | tf_op jit(solution)/shard_map/all_gather | solution.py:749
  64.5 18.5 %collective-permute-start.23 = (f32[64,1024]{1,0:T(8,128)S(1)}, f32[64,1024]{1,0:T(8,128)S(1)}, u32[]{:S(2)}, u32[]{:S(2)}) collective-permute-start(f32[64,1024]{1,0:T(8,128)S(1)} %get-tuple-element.265), channel_id=1, source_target_pairs={{0,6},{2,4},{4,2},{6,0},{1,7},{3,5},{5,3},{7,1},{8,14},{10,12},{12... | collective-permute-start | bytes 786440 | tf_op jit(solution)/shard_map/ppermute | solution.py:69
  89.3 16.9 %collective-permute-start.26 = (f32[128,1024]{1,0:T(8,128)}, f32[128,1024]{1,0:T(8,128)}, u32[]{:S(2)}, u32[]{:S(2)}) collective-permute-start(f32[128,1024]{1,0:T(8,128)} %pad_maximum_fusion.8), channel_id=1, source_target_pairs={{0,1},{1,0},{2,3},{3,2},{4,5},{5,4},{6,7},{7,6},{8,9},{9,8},{10,11... | collective-permute-start | bytes 1572872 | tf_op jit(solution)/shard_map/ppermute | solution.py:65
  145.1 306.1 %reduce-scatter.4.cloned.1.call-start = ((), (), s32[]{:S(2)}) async-start(), calls=%async_computation.12 | async-start | bytes 4456448 | tf_op jit(solution)/shard_map/reduce_scatter | solution.py:931
  200.2 35.3 %collective-permute-start.59 = (f32[64,1024]{1,0:T(8,128)}, f32[64,1024]{1,0:T(8,128)}, u32[]{:S(2)}, u32[]{:S(2)}) collective-permute-start(f32[64,1024]{1,0:T(8,128)} %get-tuple-element.251), channel_id=1, source_target_pairs={{0,2},{2,0},{4,6},{6,4},{1,3},{3,1},{5,7},{7,5},{8,10},{10,8},{12,... | collective-permute-start | bytes 786440 | tf_op jit(solution)/shard_map/ppermute | solution.py:69
  200.9 34.6 %collective-permute-start.61 = (f32[64,1024]{1,0:T(8,128)}, f32[64,1024]{1,0:T(8,128)}, u32[]{:S(2)}, u32[]{:S(2)}) collective-permute-start(f32[64,1024]{1,0:T(8,128)} %get-tuple-element.252), channel_id=1, source_target_pairs={{0,6},{2,4},{4,2},{6,0},{1,7},{3,5},{5,3},{7,1},{8,14},{10,12},{12... | collective-permute-start | bytes 786440 | tf_op jit(solution)/shard_map/ppermute | solution.py:69
  202.6 19.0 %collective-permute-start.40 = (bf16[256,1024]{1,0:T(8,128)(2,1)}, bf16[256,1024]{1,0:T(8,128)(2,1)}, u32[]{:S(2)}, u32[]{:S(2)}) collective-permute-start(bf16[256,1024]{1,0:T(8,128)(2,1)} %multiply_convert_fusion.2), channel_id=1, source_target_pairs={{0,2},{2,4},{4,6},{6,0},{1,3},{3,5},{5,7},{7,1},{8,10},{10,12},{12... | collective-permute-start | bytes 1572872 | tf_op jit(solution)/shard_map/ppermute | solution.py:65
  204.9 17.5 %collective-permute-start.41 = (bf16[256,1024]{1,0:T(8,128)(2,1)}, bf16[256,1024]{1,0:T(8,128)(2,1)}, u32[]{:S(2)}, u32[]{:S(2)}) collective-permute-start(bf16[256,1024]{1,0:T(8,128)(2,1)} %multiply_convert_fusion.2), channel_id=1, source_target_pairs={{0,6},{2,0},{4,2},{6,4},{1,7},{3,1},{5,3},{7,5},{8,14},{10,8},{12,... | collective-permute-start | bytes 1572872 | tf_op jit(solution)/shard_map/ppermute | solution.py:65
  233.7 34.0 %collective-permute-start.49 = (bf16[1024,1024]{1,0:T(8,128)(2,1)S(1)}, bf16[1024,1024]{1,0:T(8,128)(2,1)S(1)}, u32[]{:S(2)}, u32[]{:S(2)}) collective-permute-start(bf16[1024,1024]{1,0:T(8,128)(2,1)S(1)} %shard_map.289.refs_0_), channel_id=1, source_target_pairs={{0,1},{1,0},{2,3},{3,2},{4,5},{5,4},{6,7},{7,6},{8,9},{9,8},{10,11... | collective-permute-start | bytes 6291464 | tf_op jit(solution)/shard_map/ppermute | solution.py:65
  263.4 17.2 %collective-permute-start.55 = (bf16[128,1024]{1,0:T(8,128)(2,1)S(1)}, bf16[128,1024]{1,0:T(8,128)(2,1)S(1)}, u32[]{:S(2)}, u32[]{:S(2)}) collective-permute-start(bf16[128,1024]{1,0:T(8,128)(2,1)S(1)} %get-tuple-element.244.refs_6_), channel_id=1, source_target_pairs={{0,2},{2,4},{4,6},{6,0},{1,3},{3,5},{5,7},{7,1},{8,10},{10,12},{12... | collective-permute-start | bytes 786440 | tf_op jit(solution)/shard_map/ppermute | solution.py:65
  327.2 131.6 %all-gather.11.cloned.1.call-start = ((), (), s32[]{:S(2)}) async-start(), calls=%async_computation.13 | async-start | bytes 4718592 | tf_op jit(solution)/shard_map/all_gather | solution.py:895
  346.2 19.3 %collective-permute-start.81 = (bf16[256,1024]{1,0:T(8,128)(2,1)S(1)}, bf16[256,1024]{1,0:T(8,128)(2,1)S(1)}, u32[]{:S(2)}, u32[]{:S(2)}) collective-permute-start(bf16[256,1024]{1,0:T(8,128)(2,1)S(1)} %pad_maximum_fusion.10), channel_id=1, source_target_pairs={{0,2},{2,4},{4,6},{6,0},{1,3},{3,5},{5,7},{7,1},{8,10},{10,12},{12... | collective-permute-start | bytes 1572872 | tf_op jit(solution)/shard_map/ppermute | solution.py:65
  346.5 18.9 %collective-permute-start.82 = (bf16[256,1024]{1,0:T(8,128)(2,1)S(1)}, bf16[256,1024]{1,0:T(8,128)(2,1)S(1)}, u32[]{:S(2)}, u32[]{:S(2)}) collective-permute-start(bf16[256,1024]{1,0:T(8,128)(2,1)S(1)} %pad_maximum_fusion.11), channel_id=1, source_target_pairs={{0,6},{2,0},{4,2},{6,4},{1,7},{3,1},{5,3},{7,5},{8,14},{10,8},{12,... | collective-permute-start | bytes 1572872 | tf_op jit(solution)/shard_map/ppermute | solution.py:65
  383.3 187.9 %reduce-scatter.6.cloned.1.call-start = ((), (), s32[]{:S(2)}) async-start(), calls=%async_computation.14 | async-start | bytes 9437184 | tf_op jit(solution)/shard_map/reduce_scatter | solution.py:975
  389.3 20.1 %collective-permute-start.93 = (bf16[512,128]{1,0:T(8,128)(2,1)S(1)}, bf16[512,128]{1,0:T(8,128)(2,1)S(1)}, u32[]{:S(2)}, u32[]{:S(2)}) collective-permute-start(bf16[512,128]{1,0:T(8,128)(2,1)S(1)} %pad_maximum_fusion.30), channel_id=1, source_target_pairs={{0,2},{2,4},{4,6},{6,0},{1,3},{3,5},{5,7},{7,1},{8,10},{10,12},{12... | collective-permute-start | bytes 393224 | tf_op jit(solution)/shard_map/ppermute | solution.py:65
  389.5 17.5 %collective-permute-start.92 = (bf16[512,128]{1,0:T(8,128)(2,1)S(1)}, bf16[512,128]{1,0:T(8,128)(2,1)S(1)}, u32[]{:S(2)}, u32[]{:S(2)}) collective-permute-start(bf16[512,128]{1,0:T(8,128)(2,1)S(1)} %pad_maximum_fusion.29), channel_id=1, source_target_pairs={{0,4},{2,6},{4,0},{6,2},{1,5},{3,7},{5,1},{7,3},{8,12},{10,14},{12... | collective-permute-start | bytes 393224 | tf_op jit(solution)/shard_map/ppermute | solution.py:65
  405.8 45.3 %collective-permute-start.87 = (bf16[256,1024]{1,0:T(8,128)(2,1)}, bf16[256,1024]{1,0:T(8,128)(2,1)}, u32[]{:S(2)}, u32[]{:S(2)}) collective-permute-start(bf16[256,1024]{1,0:T(8,128)(2,1)} %get-tuple-element.150), channel_id=1, source_target_pairs={{0,8},{1,33},{8,16},{9,41},{16,24},{17,49},{24,0},{25,57},{32,40},... | collective-permute-start | bytes 1572872 | tf_op jit(solution)/shard_map/ppermute | solution.py:100
  407.0 44.1 %collective-permute-start.88 = (bf16[256,1024]{1,0:T(8,128)(2,1)}, bf16[256,1024]{1,0:T(8,128)(2,1)}, u32[]{:S(2)}, u32[]{:S(2)}) collective-permute-start(bf16[256,1024]{1,0:T(8,128)(2,1)} %get-tuple-element.151), channel_id=1, source_target_pairs={{0,16},{1,65},{8,24},{9,73},{16,0},{17,81},{24,8},{25,89},{32,48},... | collective-permute-start | bytes 1572872 | tf_op jit(solution)/shard_map/ppermute | solution.py:100
  409.4 41.7 %collective-permute-start.89 = (bf16[256,1024]{1,0:T(8,128)(2,1)}, bf16[256,1024]{1,0:T(8,128)(2,1)}, u32[]{:S(2)}, u32[]{:S(2)}) collective-permute-start(bf16[256,1024]{1,0:T(8,128)(2,1)} %get-tuple-element.152), channel_id=1, source_target_pairs={{0,24},{1,97},{8,0},{9,105},{16,8},{17,113},{24,16},{25,121},{32,5... | collective-permute-start | bytes 1572872 | tf_op jit(solution)/shard_map/ppermute | solution.py:100
  494.6 40.6 %all-to-all-start.3 = ((bf16[16,80,1024]{2,1,0:T(8,128)(2,1)}), bf16[16,80,1024]{2,1,0:T(8,128)(2,1)}, u32[]{:S(2)}, u32[]{:S(2)}) async-start(bf16[16,80,1024]{2,1,0:T(8,128)(2,1)} %pad_maximum_fusion.1), calls=%async_computation.4 | async-start | bytes 5242880 | tf_op jit(solution)/shard_map/all_to_all | solution.py:963
  500.5 142.2 %reduce-scatter.8.cloned.1.call-start = ((), (), s32[]{:S(2)}) async-start(), calls=%async_computation.15 | async-start | bytes 9437184 | tf_op jit(solution)/shard_map/reduce_scatter | solution.py:998
  571.2 25.2 %all-to-all-start.4 = ((f32[128,8,128]{2,1,0:T(8,128)}), f32[128,8,128]{2,1,0:T(8,128)S(1)}, u32[]{:S(2)}, u32[]{:S(2)}) async-start(f32[128,8,128]{2,1,0:T(8,128)} %bitcast.66), calls=%async_computation.7 | async-start | bytes 1048576 | tf_op jit(solution)/shard_map/all_to_all | solution.py:994
  (239 other events, 1915.6 us)
Sparse Core Ops, SparseCore 0:
  11.8 73.3 all-gather.4
  87.9 44.0 all-gather.6
  145.2 43.4 all-gather.8
  327.3 75.1 reduce-scatter.3
  404.2 33.5 all-gather.10
  470.0 56.4 reduce-scatter.5
  571.3 60.6 reduce-scatter.7

commit v3 on v2

--- a/solution.py
+++ b/solution.py
@@ -42,6 +42,9 @@
 BATCH = ("z", "c")
 EVERY = ("y", "x", "z", "c")
 
+IN_VMEM = pl.BlockSpec(memory_space=pltpu.VMEM)
+IN_SMEM = pl.BlockSpec(memory_space=pltpu.SMEM)
+
 
 def rms_norm(values):
     return values * lax.rsqrt(jnp.mean(values * values, axis=-1, keepdims=True) + EPSILON)
@@ -106,7 +109,7 @@
 
 
 def copy_rows(target, start, source, first, rows):
-    step = min(rows, 64)
+    step = math.gcd(rows, 64)
 
     @pl.loop(0, rows // step)
     def _(at):
@@ -138,44 +141,49 @@
     )(spots, *pieces)
 
 
-def split_kernel(rows, spots, up, down, *outs):
+def split_kernel(rows, count, spots, *refs):
+    values, outs = refs[:count], refs[count:]
     for step in range(4):
         for i in range(4):
             first = pl.multiple_of(spots[4 * step + i] * rows, rows)
-            copy_rows(outs[step], 2 * i * rows, up, first, rows)
-            copy_rows(outs[step], (2 * i + 1) * rows, down, first, rows)
-
-
-def split(up, down, spots):
-    rows = up.shape[0] // 16
-    shape = jax.ShapeDtypeStruct((8 * rows, up.shape[1]), BF16)
+            for at, source in enumerate(values):
+                copy_rows(outs[step], (count * i + at) * rows, source, first, rows)
+
+
+def split(values, spots):
+    count = len(values)
+    rows = values[0].shape[0] // 16
+    shape = jax.ShapeDtypeStruct((4 * count * rows, values[0].shape[1]), BF16)
     return pl.pallas_call(
-        functools.partial(split_kernel, rows),
+        functools.partial(split_kernel, rows, count),
         out_shape=(shape,) * 4,
-        in_specs=[IN_SMEM, IN_VMEM, IN_VMEM],
+        in_specs=[IN_SMEM] + [IN_VMEM] * count,
         out_specs=(IN_VMEM,) * 4,
         compiler_params=pltpu.CompilerParams(vmem_limit_bytes=40 * 2**20),
-        cost_estimate=pl.CostEstimate(flops=0, bytes_accessed=3 * up.size * 4, transcendentals=0),
-    )(spots, up, down)
-
-
-IN_VMEM = pl.BlockSpec(memory_space=pltpu.VMEM)
-IN_SMEM = pl.BlockSpec(memory_space=pltpu.SMEM)
+        cost_estimate=pl.CostEstimate(flops=0, bytes_accessed=2**22, transcendentals=0),
+    )(spots, *values)
 
 
 def in_line(pieces):
     return place(pieces, jnp.arange(len(pieces), dtype=jnp.int32))
 
 
-def gather_fsdp(values):
+def gather_fsdp_first(values):
+    return (values,), tuple(turn(values, step) for step in (1, 2, 3))
+
+
+def gather_fsdp_second(state):
+    line = in_line([state[0][0], *state[1]])
+    return (line,), tuple(turn(line, step, True) for step in (1, 2, 3))
+
+
+def gather_fsdp_value(state):
     core = lax.axis_index("c")
     mine, far = turn_place(), turn_place(True)
-    line = in_line([values] + [turn(values, step) for step in (1, 2, 3)])
-    pieces = [line] + [turn(line, step, True) for step in (1, 2, 3)]
     step = jnp.arange(4)
     first, second = (mine - step[None, :]) % 4, (far - step[:, None]) % 4
     spots = jnp.where(core == 0, second * 4 + first, first * 4 + second)
-    return place(pieces, spots.reshape(16).astype(jnp.int32), 4)
+    return place([state[0][0], *state[1]], spots.reshape(16).astype(jnp.int32), 4)
 
 
 def turn_parts(parts, last=False):
@@ -193,13 +201,13 @@
     return total
 
 
-def scatter_fsdp_first(up, down):
+def scatter_fsdp_first(*values):
     core = lax.axis_index("c")
     me = turn_place()
     step, other = jnp.arange(4)[:, None], jnp.arange(4)[None, :]
     spot = (me + step) % 4
     spots = jnp.where(core == 0, other * 4 + spot, spot * 4 + other)
-    parts = split(up, down, spots.reshape(16).astype(jnp.int32))
+    parts = split(values, spots.reshape(16).astype(jnp.int32))
     return tuple(parts), tuple(turn(parts[step], step) for step in (1, 2, 3))
 
 
@@ -207,9 +215,15 @@
     return turn_parts(turn_total(state), True)
 
 
-def scatter_fsdp_value(state):
-    total = turn_total(state)
-    return total.reshape(2, -1, total.shape[1])
+def exchange_near(values):
+    place_z = lax.axis_index("z")
+    pieces = tuple(take(values, (place_z + step) % 4) for step in range(4))
+    return pieces, tuple(shift(pieces[step], "z", step) for step in (1, 2, 3))
+
+
+def exchange_value(state):
+    spots = (lax.axis_index("z") - jnp.arange(4)) % 4
+    return place([state[0][0], *state[1]], spots.astype(jnp.int32))
 
 
 def turn_first(values):
@@ -236,23 +250,25 @@
     return place([state[0][0], *state[1]], spots.astype(jnp.int32))
 
 
-def place_columns_kernel(width, spots, *refs):
-    pieces, whole = refs[:-1], refs[-1]
+def place_columns_kernel(width, count, spots, *refs):
+    pieces, whole = refs[:count], refs[-1]
     for p, piece in enumerate(pieces):
         for s in range(piece.shape[1] // width):
             start = pl.multiple_of(spots[p * (piece.shape[1] // width) + s] * width, width)
             whole[:, pl.ds(start, width)] = piece[:, s * width : (s + 1) * width]
 
 
-def place_columns(pieces, spots):
+def place_columns(pieces, spots, *awaited):
     rows, width = pieces[0].shape
     return pl.pallas_call(
-        functools.partial(place_columns_kernel, LOCAL_WIDTH),
+        functools.partial(place_columns_kernel, LOCAL_WIDTH, len(pieces)),
         out_shape=jax.ShapeDtypeStruct((rows, width * len(pieces)), pieces[0].dtype),
-        in_specs=[IN_SMEM] + [IN_VMEM] * len(pieces),
+        in_specs=[IN_SMEM]
+        + [IN_VMEM] * len(pieces)
+        + [pl.BlockSpec(memory_space=pl.ANY)] * len(awaited),
         out_specs=IN_VMEM,
         cost_estimate=pl.CostEstimate(flops=0, bytes_accessed=2**20, transcendentals=0),
-    )(spots, *pieces)
+    )(spots, *pieces, *awaited)
 
 
 def take_columns_kernel(width, spots, values, kept, given):
@@ -305,40 +321,8 @@
     return in_line([state[0][0], state[1][0]])
 
 
-def gather_batch(values):
-    return gather_value(gather_core(gather_far(gather_near(values))))
-
-
-def scatter_core(parts):
-    rows = parts.shape[0] // 2
-    given = parts[rows:].astype(BF16)
-    return (parts, given), (shift(given, "c", 1),)
-
-
-def scatter_far(state):
-    (parts, _), (theirs,) = state
-    rows = parts.shape[0] // 8
-    half = rows // 2
-
-    def mine(step, start, count):
-        spot = step * rows + start
-        return parts[spot : spot + count] + theirs[spot : spot + count].astype(F32)
-
-    low, high = mine(2, 0, half).astype(BF16), mine(2, half, half).astype(BF16)
-    near = (mine(0, 0, rows), mine(1, 0, rows), mine(3, 0, rows))
-    return (low, high) + near, (shift(low, "z", 1), shift(high, "z", -1))
-
-
-def scatter_near(state):
-    (_, _, own, up, down), (low, high) = state
-    half = low.shape[0]
-    up = jnp.concatenate([up[:half] + low.astype(F32), up[half:]], axis=0).astype(BF16)
-    down = jnp.concatenate([down[:half], down[half:] + high.astype(F32)], axis=0).astype(BF16)
-    return (own, up, down), (shift(up, "z", 1), shift(down, "z", -1))
-
-
-def scatter_value(state):
-    return state[0][0] + state[1][0].astype(F32) + state[1][1].astype(F32)
+def gather_line(state, spots):
+    return place([state[0][0], state[1][0]], spots, 4)
 
 
 def column_spots():
@@ -356,8 +340,8 @@
     return (both,), tuple(shift(both, "z", step) for step in (1, 2, 3))
 
 
-def columns_value(state):
-    return place_columns([state[0][0], *state[1]], column_spots())
+def columns_value(state, *awaited):
+    return place_columns([state[0][0], *state[1]], column_spots(), *awaited)
 
 
 def rows_core(values):
@@ -392,9 +376,9 @@
 
 
 def back_value(state):
-    pieces = (state[0][0],) + state[1]
-    rows = pieces[0].shape[0] // 2
-    return jnp.concatenate([piece[:rows] for piece in pieces] + [piece[rows:] for piece in pieces], axis=0)
+    pieces = [state[0][0], *state[1]]
+    spots = jnp.arange(4)[:, None] + 4 * jnp.arange(2)[None, :]
+    return place(pieces, spots.reshape(8).astype(jnp.int32), 2)
 
 
 def add(left, right):
@@ -436,12 +420,17 @@
     )
 
 
-def head_shards(masters):
+def head_shards(masters, segment_ids):
     joined = jnp.concatenate([masters[0].astype(BF16), masters[1].astype(BF16)], axis=2)
     parts = joined.reshape(2, 8, 4, N_BATCH, LOCAL_WIDTH)
-    parts = jnp.transpose(parts, (3, 0, 1, 2, 4)).reshape(N_BATCH, 2, 8, 4 * LOCAL_WIDTH)
+    parts = jnp.transpose(parts, (3, 0, 1, 2, 4)).reshape(N_BATCH, 16, 4 * LOCAL_WIDTH)
+    numbers = jnp.concatenate([segment_ids, segment_ids]).astype(BF16)
+    numbers = jnp.broadcast_to(numbers[None, None, :], parts.shape)
+    parts = jnp.concatenate([parts, numbers], axis=1)
     moved = lax.all_to_all(parts, BATCH, split_axis=0, concat_axis=0, tiled=True)
-    return jnp.transpose(moved, (1, 0, 2, 3)).reshape(2, 64, 4 * LOCAL_WIDTH)
+    heads = moved[:, :16].reshape(N_BATCH, 2, 8, 4 * LOCAL_WIDTH)
+    heads = jnp.transpose(heads, (1, 0, 2, 3)).reshape(2, 64, 4 * LOCAL_WIDTH)
+    return heads, moved[:, 16, : segment_ids.shape[0]].reshape(-1).astype(F32)
 
 
 BLOCK = 256
@@ -735,21 +724,32 @@
     order = (4 * ((at + core) % 2) + (at // 2 - place_z) % 4).astype(jnp.int32)
     block_of = 2 * ((at % 4 + place_z) % 4) + (at // 4 + core) % 2
     row_pos = (block_of[:, None] * token_count + jnp.arange(token_count)[None, :]).reshape(-1)
+    block_of = block_of.astype(jnp.int32)
     single = jnp.zeros((1,), jnp.int32)
 
     normed_round = gather_near(rms_norm(inputs).astype(BF16))
-    heads_local = head_shards(masters)
-    wide_dense = jnp.stack([up_master[0], down_master[0]]).astype(BF16)
+    heads_local, segments_all = head_shards(masters, segment_ids)
+    tied = lax.optimization_barrier((heads_local, *normed_round[1]))
+    heads_local, normed_round = tied[0], (normed_round[0], tied[1:])
+    heads_pair = jnp.concatenate([heads_local[1, :32], heads_local[1, 32:]], axis=1)
+    wide_dense = jnp.stack([up_master[0].astype(BF16), down_master[0].astype(BF16), heads_pair])
     wide_dense = lax.all_gather(wide_dense, FSDP, axis=1, tiled=True)
     up_dense, down_dense = wide_dense[0], wide_dense[1]
+    heads_pair = wide_dense[2].reshape(N_FSDP, 32, 2, 4 * LOCAL_WIDTH)
+    heads_routed = jnp.transpose(heads_pair, (0, 2, 1, 3)).reshape(D, 4 * LOCAL_WIDTH)
+    heads_round = gather_fsdp_first(heads_local[0])
+    normed_round = gather_far(normed_round)
+    tied = lax.optimization_barrier((*heads_round[1], *normed_round[1]))
     out_low = jnp.concatenate([out_master[0], out_master[1]], axis=1).astype(BF16)
     out_low = lax.all_gather(out_low, EVERY, axis=0, tiled=True)
     out_dense, out_routed = out_low[:, :D], out_low[:, D:]
     wide_routed = jnp.stack([up_master[1], down_master[1]]).astype(BF16)
     wide_routed = lax.all_gather(wide_routed, FSDP, axis=1, tiled=True)
     up_routed, down_routed = wide_routed[0], wide_routed[1]
-    heads_dense = gather_fsdp(heads_local[0])
-    normed_low = gather_value(gather_core(gather_far(normed_round)))
+    heads_round = gather_fsdp_second((heads_round[0], tied[:3]))
+    normed_round = gather_core((normed_round[0], tied[3:]))
+    heads_dense = gather_fsdp_value(heads_round)
+    normed_low = gather_value(normed_round)
 
     chosen = routed[0]
     local_index = chosen - batch_index * token_count
@@ -757,45 +757,48 @@
     pick_all = (chosen[:, None] == row_pos[None, :]).astype(BF16)
     not_routed = 1.0 - jnp.max(pick, axis=0)[:, None]
     rest_grads = cotangent * not_routed
-    segment_blocks = segment_ids.astype(F32)[None, :]
-    segment_blocks = jnp.concatenate([segment_blocks, shift(segment_blocks, "c", 1)], axis=0)
-    segment_blocks = jnp.concatenate(
-        [segment_blocks] + [shift(segment_blocks, "z", step) for step in (1, 2, 3)], axis=0
-    )
-    segments_all = jnp.sum(
-        jnp.where((column_spots()[:, None] == at[None, :])[:, :, None], segment_blocks[:, None, :], 0.0),
-        axis=0,
-    ).reshape(-1)
     slot_segments = jnp.sum(
         jnp.where(chosen[:, None] == all_tokens[None, :], segments_all[None, :], 0.0), axis=1
     )
 
     moments_heads = jnp.concatenate([qkv_moment, out_moment], axis=2).reshape(
-        2, 8, 4, N_BATCH, LOCAL_HEADS, HDIM
-    )
-    moments_heads = jnp.transpose(moments_heads, (0, 2, 4, 3, 1, 5)).reshape(128, 8, HDIM)
+        2, 8, 4, N_BATCH, LOCAL_WIDTH
+    )
+    moments_heads = jnp.transpose(moments_heads, (0, 2, 3, 1, 4))[:, :, None]
+    moments_heads = jnp.broadcast_to(moments_heads, (2, 4, LOCAL_HEADS, N_BATCH, 8, LOCAL_WIDTH))
     moment_block = lax.all_to_all(
-        moments_heads, EVERY, split_axis=0, concat_axis=0, tiled=True
-    ).reshape(D, HDIM)
-    moment_block = jnp.transpose(moment_block)
+        moments_heads.reshape(128, 8, LOCAL_WIDTH), EVERY, split_axis=0, concat_axis=0, tiled=True
+    ).reshape(D, LOCAL_WIDTH)
+    moment_block = lax.dynamic_slice_in_dim(
+        jnp.transpose(moment_block), lax.axis_index("x") % 2 * HDIM, HDIM, 0
+    )
 
     def of_slots(values):
         return jnp.einsum("st,td->sd", pick_all, values, preferred_element_type=F32).astype(BF16)
 
-    start_rows = jnp.einsum("st,td->sd", pick, inputs, precision=HIGHEST)
-    start_round = sum_near(sum_core(after(start_rows, *normed_round[1]), F32))
-    slot_inputs = sum_value(sum_last(sum_next(start_round)))
-    heads_routed = gather_fsdp(heads_local[1])
+    start_rows = jnp.einsum(
+        "st,td->sd", pick, jnp.concatenate([inputs, cotangent], axis=1), precision=HIGHEST
+    )
+    start_round = sum_near(sum_core(after(start_rows, heads_dense), F32))
     projected = qkv_forward(normed_low, heads_dense)
-    rest_round = gather_near(after(rest_grads.astype(BF16), normed_low))
     mixed_low, mixed_line, log_total = attend(
-        projected, order, segments_all, moment_block, heads_routed, slot_inputs, rest_round[0][0]
+        projected, order, segments_all, *start_round[0]
     )
     mixed_slots = of_slots(mixed_low)
 
     slot_round = columns_core(mixed_slots)
+    start_round = sum_next(
+        (start_round[0], lax.optimization_barrier(start_round[1] + (mixed_slots,))[:2])
+    )
     slot_round = columns_near(slot_round)
-    slot_middle = slot_inputs + dot_f32("td,od->to", columns_value(slot_round), out_dense)
+    start_round = sum_last(
+        (start_round[0], lax.optimization_barrier(start_round[1] + slot_round[0])[:2])
+    )
+    slot_inputs = sum_value(start_round)
+    slot_inputs, slot_grads = slot_inputs[:, :D], slot_inputs[:, D:]
+    slot_middle = slot_inputs + dot_f32(
+        "td,od->to", columns_value(slot_round), out_dense
+    )
     slot_two = rms_norm(slot_middle).astype(BF16)
     slot_fed, slot_hidden, slot_active = feed_forward(slot_two, up_dense, down_dense)
 
@@ -803,7 +806,7 @@
     mixed_round = rows_core(after(mixed_low, *fed_round[0]))
     fed_round = sum_near(fed_round)
     mixed_round = rows_near(mixed_round)
-    fed_round, mixed_rows = during(fed_round, lambda late: columns_value(mixed_round))
+    fed_round, mixed_rows = during(fed_round, lambda late: columns_value(mixed_round, moment_block))
     fed_round = sum_next(fed_round)
 
     def rest_forward(late):
@@ -812,7 +815,10 @@
 
     fed_round, (middle, rest_two_low) = during(fed_round, rest_forward)
     fed_round = sum_last(fed_round)
-    two_round = gather_near(after(rest_two_low, *fed_round[0]))
+    normed_two = lax.all_gather(rest_two_low, BATCH, axis=0, tiled=True)
+    rest_low = lax.all_gather(
+        after(rest_grads.astype(BF16), rest_two_low), BATCH, axis=0, tiled=True
+    )
     slot_rows = slot_middle + sum_value(fed_round)
 
     slot_normed = rms_norm(slot_rows)
@@ -822,33 +828,21 @@
     r_round = columns_core(r_mixed)
     gate_values = jnp.dot(slot_normed, router, precision=HIGHEST)
     r_round = columns_near(r_round)
-    two_round = gather_far((two_round[0], lax.optimization_barrier(two_round[1] + r_round[0])[:2]))
     r_attended = dot_f32("td,od->to", columns_value(r_round), out_routed)
     r_middle = slot_rows + r_attended
     r_two = rms_norm(r_middle).astype(BF16)
     r_fed_part, r_hidden, r_active = feed_forward(r_two, up_routed, down_routed)
-    rest_round = gather_far((rest_round[0], lax.optimization_barrier(rest_round[1] + (r_two,))[:2]))
-
-    r_round = sum_core(r_fed_part)
-    two_round = gather_core((two_round[0], lax.optimization_barrier(two_round[1] + r_round[0])[:2]))
-    r_round = sum_near(r_round)
-    r_round, normed_two = during(r_round, lambda late: gather_value(two_round))
-    r_round = sum_next(r_round)
+
+    r_round = sum_near(sum_core(r_fed_part))
 
     def rest_active(late):
         _, hidden, active = feed_forward(late(normed_two), up_dense, down_dense)
         return hidden, active
 
     r_round, (feed_hidden, feed_active) = during(r_round, rest_active)
-    rest_round = gather_core((rest_round[0], lax.optimization_barrier(rest_round[1] + (feed_active,))[:2]))
-    r_round = sum_last(r_round)
-    r_round, rest_low = during(r_round, lambda late: gather_value(rest_round))
+    r_round = sum_last(sum_next(r_round))
     routed_branch = r_attended + sum_value(r_round)
 
-    grads_round = sum_near(
-        sum_core(after(jnp.einsum("st,td->sd", pick, cotangent, precision=HIGHEST), mixed_low), F32)
-    )
-    slot_grads = sum_value(sum_last(sum_next(grads_round)))
     branch_grads = gate_values[:, None] * slot_grads
     branch_low = branch_grads.astype(BF16)
     r_grad_hidden, r_grad_two = feed_backward(up_routed, down_routed, r_hidden, branch_low)
@@ -856,45 +850,42 @@
     r_round = sum_near(sum_core(r_grad_two))
 
     def rest_back(late):
-        return feed_backward(up_dense, down_dense, feed_hidden, late(rest_low))
-
-    r_round, (rest_hidden, rest_two) = during(r_round, rest_back)
-    back_round = scatter_core(rest_two)
+        grad_active = dot_f32("td,fd->tf", late(rest_low), down_dense)
+        return jax.vjp(gelu_tanh, feed_hidden)[1](grad_active)[0].astype(BF16)
+
+    r_round, rest_hidden = during(r_round, rest_back)
     r_round = sum_next(r_round)
-    r_round, gate_grads = during(r_round, lambda late: jnp.sum(late(slot_grads) * routed_branch, axis=1))
-    back_round = scatter_far((back_round[0], lax.optimization_barrier(back_round[1] + r_round[0])[:1]))
+    r_round, rest_two = during(r_round, lambda late: dot_f32("tf,fd->td", late(rest_hidden), up_dense))
+    rest_two = lax.psum_scatter(rest_two.astype(BF16), BATCH, scatter_dimension=0, tiled=True)
     r_round = sum_last(r_round)
-    r_grad_mid = norm_back(r_middle, sum_value(r_round))
-    r_grad_low = (r_grad_mid + branch_grads).astype(BF16)
-
-    def out_back(grad_low, weight_heads):
-        return dot_f32("to,od->td", grad_low, weight_heads[:, 3 * LOCAL_WIDTH :]).astype(BF16)
-
-    r_grad_projected, _ = attend_back(
-        r_projected, single, slot_segments, r_log_total, out_back(r_grad_low, heads_routed)
-    )
-    r_round = sum_core(dot_f32("tc,dc->td", r_grad_projected, heads_routed[:, : 3 * LOCAL_WIDTH]))
-    back_round = scatter_near((back_round[0], lax.optimization_barrier(back_round[1] + r_round[0])[:2]))
-    r_round = sum_near(r_round)
 
     def routed_weights(late):
         return (
             dot_f32("tf,td->fd", late(r_grad_hidden), r_two),
             dot_f32("tf,td->fd", r_active, late(branch_low)),
+            jnp.sum(slot_grads * routed_branch, axis=1),
         )
 
-    r_round, (r_grad_up, r_grad_down) = during(r_round, routed_weights)
+    r_round, (r_grad_up, r_grad_down, gate_grads) = during(r_round, routed_weights)
+    r_grad_mid = norm_back(r_middle, sum_value(r_round))
+    r_grad_low = (r_grad_mid + branch_grads).astype(BF16)
+
+    def out_back(grad_low, weight_heads):
+        return dot_f32("to,od->td", grad_low, weight_heads[:, 3 * LOCAL_WIDTH :]).astype(BF16)
+
+    r_grad_projected, _ = attend_back(
+        r_projected, single, slot_segments, r_log_total, out_back(r_grad_low, heads_routed)
+    )
+    r_round = sum_core(dot_f32("tc,dc->td", r_grad_projected, heads_routed[:, : 3 * LOCAL_WIDTH]))
+    r_round = sum_near(r_round)
+    r_round, rest_up = during(
+        r_round, lambda late: dot_f32("tf,td->fd", late(rest_hidden), normed_two)
+    )
     r_round = sum_next(r_round)
-
-    def rest_middle(late):
-        rest_mid = rest_grads + norm_back(middle, late(scatter_value(back_round)))
-        rest_mid_low = rest_mid.astype(BF16)
-        return rest_mid, rest_mid_low, dot_f32("to,od->td", rest_mid_low, out_dense).astype(BF16)
-
-    r_round, (rest_mid, rest_mid_low, rest_mixed) = during(r_round, rest_middle)
-    rest_mid_all = lax.all_gather(rest_mid_low, BATCH, axis=0, tiled=True)
+    r_round, rest_down = during(
+        r_round, lambda late: dot_f32("tf,td->fd", feed_active, late(rest_low))
+    )
     r_round = sum_last(r_round)
-    back_round = back_core(after(rest_mixed, *r_round[0]))
     r_grad_normed = sum_value(r_round)
     slot_out_grads = (
         slot_grads
@@ -904,36 +895,43 @@
 
     slot_out_low = slot_out_grads.astype(BF16)
     slot_grad_hidden, slot_grad_two = feed_backward(up_dense, down_dense, slot_hidden, slot_out_low)
-    slot_round = sum_core(slot_grad_two)
-    back_round = back_near((back_round[0], lax.optimization_barrier(back_round[1] + slot_round[0])[:1]))
-    slot_round = sum_near(slot_round)
-    slot_round, rest_up = during(
-        slot_round, lambda late: dot_f32("tf,td->fd", late(rest_hidden), normed_two)
-    )
+    slot_round = sum_near(sum_core(slot_grad_two))
+    def routed_heads(late):
+        return (
+            dot_f32("tc,td->cd", late(r_grad_projected), slot_low),
+            dot_f32("td,to->do", r_mixed, late(r_grad_low)),
+        )
+
+    slot_round, (r_grad_qkv, r_grad_out) = during(slot_round, routed_heads)
     slot_round = sum_next(slot_round)
-    slot_round, rest_down = during(
-        slot_round, lambda late: dot_f32("tf,td->fd", feed_active, late(rest_low))
+    slot_round, fed_line = during(
+        slot_round, lambda late: dot_f32("tf,fd->td", late(feed_active), down_dense)
     )
     slot_round = sum_last(slot_round)
     slot_mid = slot_out_grads + norm_back(slot_middle, sum_value(slot_round))
     slot_mid_low = slot_mid.astype(BF16)
     slot_mixed = out_back(slot_mid_low, heads_dense)
+    grad_up = rest_up + dot_f32("tf,td->fd", slot_grad_hidden, slot_two)
+    grad_down = rest_down + dot_f32("tf,td->fd", slot_active, slot_out_low)
+    wide_round = scatter_fsdp_first(grad_up, r_grad_up, grad_down, r_grad_down)
+
+    rest_two = after(rest_two, *wide_round[0], slot_mixed)
+    rest_mid = rest_grads + norm_back(middle, rest_two.astype(F32))
+    rest_mid_low = rest_mid.astype(BF16)
+    rest_mixed = dot_f32("to,od->td", rest_mid_low, out_dense).astype(BF16)
+    rest_mid_all = lax.all_gather(rest_mid_low, BATCH, axis=0, tiled=True)
+    rest_mixed = back_value(back_near(back_core(rest_mixed)))
     grad_mixed = (
-        back_value(back_round).astype(F32)
+        rest_mixed.astype(F32)
         + jnp.einsum("st,sd->td", pick_all, slot_mixed, preferred_element_type=F32)
     ).astype(BF16)
-    grad_up = rest_up + dot_f32("tf,td->fd", slot_grad_hidden, slot_two)
-    grad_down = rest_down + dot_f32("tf,td->fd", slot_active, slot_out_low)
-    wide_round = scatter_fsdp_first(grad_up, grad_down)
     grad_mixed = after(grad_mixed, *wide_round[0])
+    fed_rows = lax.psum_scatter(after(fed_line, grad_mixed), BATCH, scatter_dimension=0, tiled=True)
     grad_projected, grad_projected_line = attend_back(projected, order, segments_all, log_total, grad_mixed)
 
-    routed_wide = lax.psum_scatter(
-        jnp.stack([r_grad_up, r_grad_down]), FSDP, scatter_dimension=1, tiled=True
-    )
     wide_round = (
         wide_round[0],
-        lax.optimization_barrier(wide_round[1] + (grad_projected, routed_wide))[:3],
+        lax.optimization_barrier(wide_round[1] + (grad_projected,))[:3],
     )
     wide_round = scatter_fsdp_second(wide_round)
 
@@ -946,10 +944,7 @@
         return grad_qkv, grad_out
 
     wide_round, (grad_qkv, grad_out) = during(wide_round, dense_weights)
-    dense_wide = scatter_fsdp_value(wide_round)
-
-    r_grad_qkv = dot_f32("tc,td->cd", r_grad_projected, slot_low)
-    r_grad_out = dot_f32("td,to->do", r_mixed, r_grad_low)
+
     block_parts = jnp.concatenate([grad_qkv, grad_out, r_grad_qkv, r_grad_out], axis=0).astype(BF16)
     router_grad = jnp.dot(gate_grads, slot_normed, precision=HIGHEST)
     router_high = router_grad.astype(BF16)
@@ -960,42 +955,47 @@
     block_parts = jnp.concatenate(
         [block_parts.reshape(16, HDIM, D), jnp.broadcast_to(router_rows[None], (16, 16, D))], axis=1
     )
-    block_grads = lax.all_to_all(block_parts, FSDP, split_axis=0, concat_axis=0, tiled=True)
-
-    new_up_moment = MOMENTUM * up_moment + jnp.stack([dense_wide[0], routed_wide[0]])
-    new_down_moment = MOMENTUM * down_moment + jnp.stack([dense_wide[1], routed_wide[1]])
-    wide_own = after(jnp.concatenate([new_up_moment, new_down_moment], axis=0), block_parts)
-    wide_rows = lax.all_to_all(wide_own, "z", split_axis=0, concat_axis=0, tiled=True).reshape(128, D)
-    grad_normed = dot_f32(
-        "tc,dc->td", after(grad_projected_line, block_parts), heads_dense[:, : 3 * LOCAL_WIDTH]
-    )
+    heads_round = scatter_fsdp_first(block_parts.reshape(-1, D))
+
+    wide_grads = turn_total(wide_round).reshape(4, 32, D)
+    new_up_moment = MOMENTUM * up_moment + wide_grads[:2]
+    new_down_moment = MOMENTUM * down_moment + wide_grads[2:]
+    wide_own = after(jnp.concatenate([new_up_moment, new_down_moment], axis=0), *heads_round[0])
+    wide_round = exchange_near(wide_own)
+    wide_round, grad_normed = during(
+        wide_round,
+        lambda late: dot_f32("tc,dc->td", late(grad_projected_line), heads_dense[:, : 3 * LOCAL_WIDTH]),
+    )
+    wide_rows = exchange_value(wide_round)
     rows_low = wide_rows.astype(BF16)
     rows_both = jnp.concatenate([rows_low, shift(rows_low, "c", 1)], axis=0)
-    rows_both = after(rows_both, grad_normed, block_grads)
-    grad_normed = lax.psum_scatter(grad_normed, BATCH, scatter_dimension=0, tiled=True)
+    heads_round = (heads_round[0], lax.optimization_barrier(heads_round[1] + (rows_both,))[:3])
+    heads_round = turn_parts(turn_total(heads_round), True)
+    rows_both = after(rows_both, *heads_round[0])
+    grad_normed = lax.psum_scatter(
+        after(grad_normed, rows_both), BATCH, scatter_dimension=0, tiled=True
+    )
     own_columns = lax.dynamic_slice_in_dim(rows_both, core * (D // 2), D // 2, 1)
     gram_part = dot_f32("rb,rc->bc", own_columns, rows_both)
 
     def heads_step(late):
-        grads = jnp.sum(late(block_grads).astype(F32), axis=0)
-        new_block = MOMENTUM * moment_block + grads[:HDIM]
+        grads = turn_total(heads_round)
+        new_block = MOMENTUM * moment_block + late(grads)[:HDIM]
         ortho_block = newton_heads(new_block)
         returned = jnp.transpose(jnp.concatenate([new_block, ortho_block], axis=0))
         return returned.reshape(128, 8, 2 * HDIM), grads[HDIM] + grads[HDIM + 1]
 
-    def fed_step(late):
-        spots = jnp.argsort(order).astype(jnp.int32)
-        fed_line = place([late(feed_active)], spots, N_BATCH)
-        return dot_f32("tf,fd->td", fed_line, down_dense)
-
-    gram_round = turn_first(gram_part)
+    gram_round = turn_second(turn_first(gram_part))
     gram_round, (returned, router_total) = during(gram_round, heads_step)
-    gram_round = turn_second(gram_round)
+    gram_round = turn_third(gram_round)
     returned = lax.all_to_all(returned, EVERY, split_axis=0, concat_axis=0, tiled=True)
-    gram_round = turn_third(gram_round)
     gram_round = turn_fourth(gram_round)
-    gram_round, fed_line = during(gram_round, fed_step)
-    fed_rows = lax.psum_scatter(after(fed_line, grad_normed), BATCH, scatter_dimension=0, tiled=True)
+    gram_round, mixed = during(
+        gram_round,
+        lambda late: middle
+        + late(fed_rows)
+        + jnp.einsum("st,sd->td", pick, gate_values[:, None] * routed_branch, precision=HIGHEST),
+    )
     gram_half = turn_value(gram_round)
     gram_other = shift(gram_half, "c", 1)
     wide_gram = jnp.concatenate(
@@ -1005,15 +1005,15 @@
     wide_scale = jnp.sqrt(jnp.trace(wide_gram.astype(F32))) + NEWTON_EPSILON
     wide_gram = (wide_gram.astype(F32) / (wide_scale * wide_scale)).astype(BF16)
     wide_ortho = newton_two(wide_rows, wide_gram, wide_scale).reshape(4, 32, D)
-    wide_ortho = lax.all_to_all(wide_ortho, "z", split_axis=0, concat_axis=0, tiled=True)
-
-    grad_mid = rest_mid + jnp.einsum("st,sd->td", pick, slot_mid, precision=HIGHEST)
-    grad_inputs = grad_mid + norm_back(inputs, grad_normed)
-    mixed = (
-        middle
-        + fed_rows
-        + jnp.einsum("st,sd->td", pick, gate_values[:, None] * routed_branch, precision=HIGHEST)
-    )
+    wide_round = exchange_near(wide_ortho)
+
+    def token_step(late):
+        grad_mid = rest_mid + jnp.einsum("st,sd->td", pick, slot_mid, precision=HIGHEST)
+        grad_inputs = grad_mid + norm_back(inputs, late(grad_normed))
+        return grad_inputs
+
+    wide_round, grad_inputs = during(wide_round, token_step)
+    wide_ortho = exchange_value(wide_round).reshape(4, 32, D)
 
     returned = returned.reshape(2, 4, LOCAL_HEADS, N_BATCH, 8, 2, HDIM)
     returned = jnp.transpose(returned, (5, 0, 4, 1, 3, 2, 6)).reshape(2, 2, 8, 4 * D)

time: 664 us -> 589 us (0.89)
  starting transfers between devices: 184 us -> 145 us
  waiting for transfers between devices: 144 us -> 117 us
  blocking collectives: 15.2 us -> 0 us
  matrix products: 106 us -> 119 us
    all_to_all x3 -> x1, waiting for transfers between devices: 37.4 us -> 3.26 us  [body(): lax.all_to_all(moments_heads.reshape(128, 8, LOCAL_WIDTH), EVERY, split_a...]
    ppermute x56 -> x41, starting transfers between devices: 75.8 us -> 57.8 us  [shift(): lax.ppermute(values, axis, [(i, (i + step) % size) for i in range(size)])]
    all_to_all x1 -> x0, blocking collectives: 15.2 us -> none  [body(): lax.all_to_all(wide_own, 'z', split_axis=0, concat_axis=0, tiled=True)]
    all_to_all x3 -> x1, starting transfers between devices: 20.5 us -> 5.33 us  [body(): lax.all_to_all(moments_heads.reshape(128, 8, LOCAL_WIDTH), EVERY, split_a...]
    dot_general x33 -> x34, matrix products: 77 us -> 90.5 us  [dot_f32(): return jnp.einsum(pattern, left, right, preferred_element_type=F32)]
    ppermute x30, waiting for transfers between devices: 13.2 us -> 24.7 us  [turn(): return lax.ppermute(values, ('y', 'x', 'c'), pairs)]
    all_to_all x1, waiting for transfers between devices: 0.01 us -> 9.28 us  [head_shards(): lax.all_to_all(parts, BATCH, split_axis=0, concat_axis=0, tiled=True)]
    all_to_all x1, waiting for transfers between devices: 7.78 us -> 0.01 us  [body(): lax.all_to_all(returned, EVERY, split_axis=0, concat_axis=0, tiled=True)]
  transfers between devices with their start and end apart: 126 -> 107, of which waited for: 51 -> 50; matrix products, arithmetic and copies ran while one was open for 27% -> 34% of each run, Pallas kernels for 11% -> 12%
where the time goes in v3:
time: 589 us; the launch traced here: 578 us
  starting transfers between devices  145 us (25%)
  matrix products  119 us (20%)
  waiting for transfers between devices  117 us (20%)
  Pallas kernels  72.2 us (12%)
  other arithmetic  61.4 us (10%)
  local copies, waits for them, and re-layouts  45.1 us (8%)
  between operations  18.7 us (3%)
    dot_general x34, matrix products, dot_f32(): return jnp.einsum(pattern, left, right, preferred_element_type=F32)  90.5 us
    ppermute x41, starting transfers between devices, shift(): lax.ppermute(values, axis, [(i, (i + step) % size) for i in range(size)])  57.8 us
    ppermute x41, waiting for transfers between devices, shift(): lax.ppermute(values, axis, [(i, (i + step) % size) for i in range(size)])  47.9 us
    ppermute x30, starting transfers between devices, turn(): return lax.ppermute(values, ('y', 'x', 'c'), pairs)  32.7 us
    pallas_call x2, Pallas kernels, attend_back(): pl.pallas_call(functools.partial(skip_awaited, attend_back_kernel, 6, len...  29.7 us
    ppermute x24, starting transfers between devices, pair(): return lax.ppermute(values, axis, [(i, partner(i)) for i in range(4)])  26.3 us
    ppermute x24, waiting for transfers between devices, pair(): return lax.ppermute(values, axis, [(i, partner(i)) for i in range(4)])  25.4 us
    ppermute x30, waiting for transfers between devices, turn(): return lax.ppermute(values, ('y', 'x', 'c'), pairs)  24.7 us
  transfers between devices with their start and end apart: 107, of which 50 were waited for; matrix products, arithmetic and copies ran while one was open for 34% of the time, Pallas kernels for 12%

profile of v3, /device:TPU:1, one launch (start us, length us, event | category | flops | bytes accessed | tf_op | source)
XLA Modules:
  0.0 578.5 jit_solution(5471795812266074693)
XLA Ops:
  17.2 4.3 all-to-all-start
  22.9 9.3 %all-to-all-done = bf16[8,32,512]{2,1,0:T(8,128)(2,1)S(1)} async-done(((bf16[8,32,512]{2,1,0:T(8,128)(2,1)}), bf16[8,32,512]{2,1,0:T(8,128)(2,1)S(1)}, u32[]{:S(2)}, u32[]{:S(2)}) %all-to-all-start) | async-done | bytes 262176 | tf_op jit(solution)/shard_map/all_to_all | solution.py:430
  41.2 3.4 collective-permute-done.3.refs_2_
  56.2 3.4 collective-permute-start.7
  77.2 22.6 %shard_map.282 = (bf16[2048,128]{1,0:T(8,128)(2,1)S(1)}, bf16[2048,128]{1,0:T(8,128)(2,1)S(1)}, f32[2,2048]{1,0:T(2,128)S(1)}) custom-call(s32[8]{0:T(128)S(1)} %fusion.199.refs_0_, bf16[2048,384]{1,0:T(8,128)(2,1)S(1)} %convolution_convert_fusion.refs_1_, f32[1,2048]{1,0:T(1,128)S(1)} %bitcast.282, f32[2048,1]{1,0:T(8,128)S(1)} %copy.61.refs_3_.refs_5_, ...), custom_call_target="tpu_custom_call" | custom-call | flops 2048 | bytes 2048 | tf_op jit(solution)/shard_map/pallas_call | solution.py:608
  104.4 10.3 %collective-permute-done.14 = f32[64,2048]{1,0:T(8,128)S(1)} collective-permute-done((f32[64,2048]{1,0:T(8,128)S(1)}, f32[64,2048]{1,0:T(8,128)S(1)}, u32[]{:S(2)}, u32[]{:S(2)}) %collective-permute-start.14) | collective-permute-done | bytes 524320 | tf_op jit(solution)/shard_map/ppermute | solution.py:72
  125.2 3.5 collective-permute-done.18.refs_1_
  144.0 5.3 all-to-all-start.1
  177.6 3.3 collective-permute-done.29
  197.3 5.0 collective-permute-done.34.refs_3_
  205.6 3.5 collective-permute-done.32.refs_1_
  211.8 3.5 multiply_reduce_fusion.5
  224.9 8.5 %multiply_convert_fusion = (bf16[2048,512]{1,0:T(8,128)(2,1)}, f32[2048,512]{1,0:T(8,128)}) fusion(bf16[2048,1024]{1,0:T(8,128)(2,1)} %all-gather.11.cloned.1.call-done, bf16[3,512,1024]{2,1,0:T(8,128)(2,1)} %all-gather.9.cloned.1.call-done), kind=kOutput, calls=%fused_computation.14 | convolution fusion | flops 2156920832 | bytes 11534336 | tf_op jit(solution)/shard_map/td,fd->tf/dot_general | solution.py:63
  235.2 6.6 %collective-permute-done.44 = bf16[64,1024]{1,0:T(8,128)(2,1)S(1)} collective-permute-done((bf16[64,1024]{1,0:T(8,128)(2,1)S(1)}, bf16[64,1024]{1,0:T(8,128)(2,1)S(1)}, u32[]{:S(2)}, u32[]{:S(2)}) %collective-permute-start.44) | collective-permute-done | bytes 131104 | tf_op jit(solution)/shard_map/ppermute | solution.py:72
  253.6 6.7 %all-gather.15.cloned.1.call-done = bf16[2048,1024]{1,0:T(8,128)(2,1)} async-done(((bf16[256,1024]{1,0:T(8,128)(2,1)}), bf16[2048,1024]{1,0:T(8,128)(2,1)}) %all-gather.15.cloned.1.call-update) | async-done | bytes 4194320 | tf_op jit(solution)/shard_map/all_gather | solution.py:819
  260.3 8.6 %fusion.8 = bf16[2048,512]{1,0:T(8,128)(2,1)S(1)} fusion(f32[2048,512]{1,0:T(8,128)} %get-tuple-element.334, bf16[2048,1024]{1,0:T(8,128)(2,1)} %all-gather.15.cloned.1.call-done, bf16[3,512,1024]{2,1,0:T(8,128)(2,1)} %all-gather.9.cloned.1.call-done), kind=kOutput, calls=%fused_computation.12 | convolution fusion | flops 2168455168 | bytes 11534336 | tf_op jit(solution)/shard_map/td,fd->tf/dot_general | solution.py:63
  271.9 5.6 fusion.63
  292.8 6.7 %fusion.252 = f32[512,1024]{1,0:T(8,128)} fusion(bf16[2048,512]{1,0:T(8,128)(2,1)} %copy-done.177, bf16[2048,1024]{1,0:T(8,128)(2,1)} %all-gather.11.cloned.1.call-done), kind=kOutput, calls=%fused_computation.494 | convolution fusion | flops 2147483648 | bytes 8388608 | tf_op jit(solution)/shard_map/tf,td->fd/dot_general | solution.py:63
  302.3 3.7 fusion.253
  330.3 5.8 fusion.59
  354.4 3.3 fusion.29.values
  366.4 3.6 collective-permute-done.61.refs_2_
  370.1 5.6 collective-permute-done.62.refs_3_
  386.5 28.0 %shard_map.291 = (bf16[2048,384]{1,0:T(8,128)(2,1)S(1)}, bf16[2048,384]{1,0:T(8,128)(2,1)S(1)}) custom-call(s32[8]{0:T(128)S(1)} %copy-done.30, bf16[2048,384]{1,0:T(8,128)(2,1)S(1)} %copy-done.3, bf16[2048,128]{1,0:T(8,128)(2,1)S(1)} %add_convert_fusion.refs_2_, f32[2,2048]{1,0:T(2,128)S(1)} %copy-done.24, f32[1,2048]{1,0:T(1,128)S(1)} %bitcast.284, ...), custom_call_target="tpu_custom_call" | custom-call | flops 2048 | bytes 2048 | tf_op jit(solution)/shard_map/pallas_call | solution.py:630
  414.6 3.3 convert_add_fusion
  437.0 4.0 collective-permute-start.70
  442.5 5.7 fusion.86
  448.7 5.5 collective-permute-start.72
  472.5 4.1 collective-permute-done.76
  488.1 18.2 %all-to-all-start.2 = ((f32[128,8,128]{2,1,0:T(8,128)}), f32[128,8,128]{2,1,0:T(8,128)S(1)}, u32[]{:S(2)}, u32[]{:S(2)}) async-start(f32[128,8,128]{2,1,0:T(8,128)} %bitcast.85), calls=%async_computation.5 | async-start | bytes 1048576 | tf_op jit(solution)/shard_map/all_to_all | solution.py:991
  530.3 3.6 add_add_fusion.5
  565.8 3.4 collective-permute-done.92.refs_1_
  (820 shorter events, 341.9 us)
Async XLA Ops:
  7.2 127.0 %all-gather.7.cloned.1.call-start = ((), (), s32[]{:S(2)}) async-start(), calls=%async_computation.6 | async-start | bytes 4227072 | tf_op jit(solution)/shard_map/all_gather | solution.py:744
  11.6 20.6 %collective-permute-start = (bf16[256,1024]{1,0:T(8,128)(2,1)S(1)}, bf16[256,1024]{1,0:T(8,128)(2,1)}, u32[]{:S(2)}, u32[]{:S(2)}) collective-permute-start(bf16[256,1024]{1,0:T(8,128)(2,1)S(1)} %multiply_convert_fusion.4), channel_id=1, source_target_pairs={{0,2},{2,4},{4,6},{6,0},{1,3},{3,5},{5,7},{7,1},{8,10},{10,12},{12... | collective-permute-start | bytes 1572872 | tf_op jit(solution)/shard_map/ppermute | solution.py:68
  14.2 18.1 %collective-permute-start.1 = (bf16[256,1024]{1,0:T(8,128)(2,1)S(1)}, bf16[256,1024]{1,0:T(8,128)(2,1)}, u32[]{:S(2)}, u32[]{:S(2)}) collective-permute-start(bf16[256,1024]{1,0:T(8,128)(2,1)S(1)} %multiply_convert_fusion.4), channel_id=1, source_target_pairs={{0,6},{2,0},{4,2},{6,4},{1,7},{3,1},{5,3},{7,5},{8,14},{10,8},{12,... | collective-permute-start | bytes 1572872 | tf_op jit(solution)/shard_map/ppermute | solution.py:68
  17.2 15.0 %all-to-all-start = ((bf16[8,32,512]{2,1,0:T(8,128)(2,1)}), bf16[8,32,512]{2,1,0:T(8,128)(2,1)S(1)}, u32[]{:S(2)}, u32[]{:S(2)}) async-start(bf16[8,32,512]{2,1,0:T(8,128)(2,1)} %pad_maximum_fusion.9), calls=%async_computation | async-start | bytes 524288 | tf_op jit(solution)/shard_map/all_to_all | solution.py:430
  21.5 115.5 %all-gather.9.cloned.1.call-start = ((), (), s32[]{:S(2)}) async-start(), calls=%async_computation.7 | async-start | bytes 3342336 | tf_op jit(solution)/shard_map/all_gather | solution.py:736
  37.0 179.5 %all-gather.13.cloned.1.call-start = ((), (), s32[]{:S(2)}) async-start(), calls=%async_computation.9 | async-start | bytes 2228224 | tf_op jit(solution)/shard_map/all_gather | solution.py:747
  56.2 16.3 %collective-permute-start.7 = (bf16[1024,1024]{1,0:T(8,128)(2,1)S(1)}, bf16[1024,1024]{1,0:T(8,128)(2,1)}, u32[]{:S(2)}, u32[]{:S(2)}) collective-permute-start(bf16[1024,1024]{1,0:T(8,128)(2,1)S(1)} %shard_map.278.refs_0_), channel_id=1, source_target_pairs={{0,1},{1,0},{2,3},{3,2},{4,5},{5,4},{6,7},{7,6},{8,9},{9,8},{10,11... | collective-permute-start | bytes 6291464 | tf_op jit(solution)/shard_map/ppermute | solution.py:68
  69.6 30.7 %collective-permute-start.13 = (f32[64,2048]{1,0:T(8,128)S(1)}, f32[64,2048]{1,0:T(8,128)S(1)}, u32[]{:S(2)}, u32[]{:S(2)}) collective-permute-start(f32[64,2048]{1,0:T(8,128)S(1)} %get-tuple-element.249.refs_5_), channel_id=1, source_target_pairs={{0,6},{2,4},{4,2},{6,0},{1,7},{3,5},{5,3},{7,1},{8,14},{10,12},{12... | collective-permute-start | bytes 1572872 | tf_op jit(solution)/shard_map/ppermute | solution.py:72
  72.5 27.9 %collective-permute-start.12 = (f32[64,2048]{1,0:T(8,128)S(1)}, f32[64,2048]{1,0:T(8,128)S(1)}, u32[]{:S(2)}, u32[]{:S(2)}) collective-permute-start(f32[64,2048]{1,0:T(8,128)S(1)} %get-tuple-element.250.refs_4_), channel_id=1, source_target_pairs={{0,2},{2,0},{4,6},{6,4},{1,3},{3,1},{5,7},{7,5},{8,10},{10,8},{12,... | collective-permute-start | bytes 1572872 | tf_op jit(solution)/shard_map/ppermute | solution.py:72
  100.6 14.1 %collective-permute-start.14 = (f32[64,2048]{1,0:T(8,128)S(1)}, f32[64,2048]{1,0:T(8,128)S(1)}, u32[]{:S(2)}, u32[]{:S(2)}) collective-permute-start(f32[64,2048]{1,0:T(8,128)S(1)} %get-tuple-element.247), channel_id=1, source_target_pairs={{0,6},{2,4},{4,2},{6,0},{1,7},{3,5},{5,3},{7,1},{8,14},{10,12},{12... | collective-permute-start | bytes 1572872 | tf_op jit(solution)/shard_map/ppermute | solution.py:72
  115.9 15.5 %collective-permute-start.17 = (f32[128,2048]{1,0:T(8,128)}, f32[128,2048]{1,0:T(8,128)}, u32[]{:S(2)}, u32[]{:S(2)}) collective-permute-start(f32[128,2048]{1,0:T(8,128)} %pad_maximum_fusion.4), channel_id=1, source_target_pairs={{0,1},{1,0},{2,3},{3,2},{4,5},{5,4},{6,7},{7,6},{8,9},{9,8},{10,11... | collective-permute-start | bytes 3145736 | tf_op jit(solution)/shard_map/ppermute | solution.py:68
  144.0 20.1 %all-to-all-start.1 = ((f32[128,8,128]{2,1,0:T(8,128)}), f32[128,8,128]{2,1,0:T(8,128)S(1)}, u32[]{:S(2)}, u32[]{:S(2)}) async-start(f32[128,8,128]{2,1,0:T(8,128)} %bitcast.306), calls=%async_computation.1 | async-start | bytes 1048576 | tf_op jit(solution)/shard_map/all_to_all | solution.py:769
  149.3 75.6 %all-gather.11.cloned.1.call-start = ((), (), s32[]{:S(2)}) async-start(), calls=%async_computation.8 | async-start | bytes 4718592 | tf_op jit(solution)/shard_map/all_gather | solution.py:818
  152.3 19.1 %collective-permute-start.27 = (bf16[64,1024]{1,0:T(8,128)(2,1)}, bf16[64,1024]{1,0:T(8,128)(2,1)}, u32[]{:S(2)}, u32[]{:S(2)}) collective-permute-start(bf16[64,1024]{1,0:T(8,128)(2,1)} %get-tuple-element.312), channel_id=1, source_target_pairs={{0,6},{2,4},{4,2},{6,0},{1,7},{3,5},{5,3},{7,1},{8,14},{10,12},{12... | collective-permute-start | bytes 393224 | tf_op jit(solution)/shard_map/ppermute | solution.py:72
  154.9 16.6 %collective-permute-start.26 = (bf16[64,1024]{1,0:T(8,128)(2,1)}, bf16[64,1024]{1,0:T(8,128)(2,1)}, u32[]{:S(2)}, u32[]{:S(2)}) collective-permute-start(bf16[64,1024]{1,0:T(8,128)(2,1)} %get-tuple-element.313), channel_id=1, source_target_pairs={{0,2},{2,0},{4,6},{6,4},{1,3},{3,1},{5,7},{7,5},{8,10},{10,8},{12,... | collective-permute-start | bytes 393224 | tf_op jit(solution)/shard_map/ppermute | solution.py:72
  176.1 84.2 %all-gather.15.cloned.1.call-start = ((), (), s32[]{:S(2)}) async-start(), calls=%async_computation.10 | async-start | bytes 4718592 | tf_op jit(solution)/shard_map/all_gather | solution.py:819
  189.9 160.5 %reduce-scatter.4.cloned.1.call-start = ((), (), s32[]{:S(2)}) async-start(), calls=%async_computation.11 | async-start | bytes 4718592 | tf_op jit(solution)/shard_map/reduce_scatter | solution.py:859
  251.7 17.2 %collective-permute-start.38 = (bf16[64,1024]{1,0:T(8,128)(2,1)S(1)}, bf16[64,1024]{1,0:T(8,128)(2,1)S(1)}, u32[]{:S(2)}, u32[]{:S(2)}) collective-permute-start(bf16[64,1024]{1,0:T(8,128)(2,1)S(1)} %get-tuple-element.304), channel_id=1, source_target_pairs={{0,6},{2,4},{4,2},{6,0},{1,7},{3,5},{5,3},{7,1},{8,14},{10,12},{12... | collective-permute-start | bytes 393224 | tf_op jit(solution)/shard_map/ppermute | solution.py:72
  253.0 15.9 %collective-permute-start.37 = (bf16[64,1024]{1,0:T(8,128)(2,1)S(1)}, bf16[64,1024]{1,0:T(8,128)(2,1)S(1)}, u32[]{:S(2)}, u32[]{:S(2)}) collective-permute-start(bf16[64,1024]{1,0:T(8,128)(2,1)S(1)} %get-tuple-element.305), channel_id=1, source_target_pairs={{0,2},{2,0},{4,6},{6,4},{1,3},{3,1},{5,7},{7,5},{8,10},{10,8},{12,... | collective-permute-start | bytes 393224 | tf_op jit(solution)/shard_map/ppermute | solution.py:72
  288.4 135.3 %all-gather.17.cloned.1.call-start = ((), (), s32[]{:S(2)}) async-start(), calls=%async_computation.13 | async-start | bytes 4718592 | tf_op jit(solution)/shard_map/all_gather | solution.py:922
  354.3 176.0 %reduce-scatter.6.cloned.1.call-start = ((), (), s32[]{:S(2)}) async-start(), calls=%async_computation.12 | async-start | bytes 9437184 | tf_op jit(solution)/shard_map/reduce_scatter | solution.py:929
  376.7 184.0 %reduce-scatter.8.cloned.1.call-start = ((), (), s32[]{:S(2)}) async-start(), calls=%async_computation.14 | async-start | bytes 9437184 | tf_op jit(solution)/shard_map/reduce_scatter | solution.py:975
  376.8 37.8 %collective-permute-start.63 = (bf16[512,1024]{1,0:T(8,128)(2,1)}, bf16[512,1024]{1,0:T(8,128)(2,1)}, u32[]{:S(2)}, u32[]{:S(2)}) collective-permute-start(bf16[512,1024]{1,0:T(8,128)(2,1)} %copy-done.33), channel_id=1, source_target_pairs={{0,8},{1,33},{8,16},{9,41},{16,24},{17,49},{24,0},{25,57},{32,40},... | collective-permute-start | bytes 3145736 | tf_op jit(solution)/shard_map/ppermute | solution.py:103
  378.4 36.1 %collective-permute-start.64 = (bf16[512,1024]{1,0:T(8,128)(2,1)}, bf16[512,1024]{1,0:T(8,128)(2,1)}, u32[]{:S(2)}, u32[]{:S(2)}) collective-permute-start(bf16[512,1024]{1,0:T(8,128)(2,1)} %copy-done.32), channel_id=1, source_target_pairs={{0,16},{1,65},{8,24},{9,73},{16,0},{17,81},{24,8},{25,89},{32,48},... | collective-permute-start | bytes 3145736 | tf_op jit(solution)/shard_map/ppermute | solution.py:103
  380.8 33.8 %collective-permute-start.65 = (bf16[512,1024]{1,0:T(8,128)(2,1)}, bf16[512,1024]{1,0:T(8,128)(2,1)}, u32[]{:S(2)}, u32[]{:S(2)}) collective-permute-start(bf16[512,1024]{1,0:T(8,128)(2,1)} %copy-done.31), channel_id=1, source_target_pairs={{0,24},{1,97},{8,0},{9,105},{16,8},{17,113},{24,16},{25,121},{32,5... | collective-permute-start | bytes 3145736 | tf_op jit(solution)/shard_map/ppermute | solution.py:103
  435.7 20.5 %collective-permute-start.73 = (bf16[320,1024]{1,0:T(8,128)(2,1)}, bf16[320,1024]{1,0:T(8,128)(2,1)}, u32[]{:S(2)}, u32[]{:S(2)}) collective-permute-start(bf16[320,1024]{1,0:T(8,128)(2,1)} %get-tuple-element.181), channel_id=1, source_target_pairs={{0,8},{1,33},{8,16},{9,41},{16,24},{17,49},{24,0},{25,57},{32,40},... | collective-permute-start | bytes 1966088 | tf_op jit(solution)/shard_map/ppermute | solution.py:103
  436.2 20.1 %collective-permute-start.74 = (bf16[320,1024]{1,0:T(8,128)(2,1)S(1)}, bf16[320,1024]{1,0:T(8,128)(2,1)}, u32[]{:S(2)}, u32[]{:S(2)}) collective-permute-start(bf16[320,1024]{1,0:T(8,128)(2,1)S(1)} %get-tuple-element.182), channel_id=1, source_target_pairs={{0,16},{1,65},{8,24},{9,73},{16,0},{17,81},{24,8},{25,89},{32,48},... | collective-permute-start | bytes 1966088 | tf_op jit(solution)/shard_map/ppermute | solution.py:103
  480.7 26.4 %collective-permute-start.81 = (bf16[32,1024]{1,0:T(8,128)(2,1)S(1)}, bf16[32,1024]{1,0:T(8,128)(2,1)S(1)}, u32[]{:S(2)}, u32[]{:S(2)}) collective-permute-start(bf16[32,1024]{1,0:T(8,128)(2,1)S(1)} %get-tuple-element.257), channel_id=1, source_target_pairs={{0,96},{1,25},{8,104},{9,1},{16,112},{17,9},{24,120},{25,17},{32,0... | collective-permute-start | bytes 196616 | tf_op jit(solution)/shard_map/ppermute | solution.py:103
  482.2 24.9 %collective-permute-start.80 = (bf16[32,1024]{1,0:T(8,128)(2,1)S(1)}, bf16[32,1024]{1,0:T(8,128)(2,1)S(1)}, u32[]{:S(2)}, u32[]{:S(2)}) collective-permute-start(bf16[32,1024]{1,0:T(8,128)(2,1)S(1)} %get-tuple-element.258), channel_id=1, source_target_pairs={{0,64},{1,17},{8,72},{9,25},{16,80},{17,1},{24,88},{25,9},{32,96},... | collective-permute-start | bytes 196616 | tf_op jit(solution)/shard_map/ppermute | solution.py:103
  482.6 24.5 %collective-permute-start.79 = (bf16[32,1024]{1,0:T(8,128)(2,1)S(1)}, bf16[32,1024]{1,0:T(8,128)(2,1)S(1)}, u32[]{:S(2)}, u32[]{:S(2)}) collective-permute-start(bf16[32,1024]{1,0:T(8,128)(2,1)S(1)} %get-tuple-element.259), channel_id=1, source_target_pairs={{0,32},{1,9},{8,40},{9,17},{16,48},{17,25},{24,56},{25,1},{32,64},... | collective-permute-start | bytes 196616 | tf_op jit(solution)/shard_map/ppermute | solution.py:103
  488.1 32.9 %all-to-all-start.2 = ((f32[128,8,128]{2,1,0:T(8,128)}), f32[128,8,128]{2,1,0:T(8,128)S(1)}, u32[]{:S(2)}, u32[]{:S(2)}) async-start(f32[128,8,128]{2,1,0:T(8,128)} %bitcast.85), calls=%async_computation.5 | async-start | bytes 1048576 | tf_op jit(solution)/shard_map/all_to_all | solution.py:991
  517.3 16.6 %collective-permute-start.90 = (bf16[128,1024]{1,0:T(8,128)(2,1)S(1)}, bf16[128,1024]{1,0:T(8,128)(2,1)S(1)}, u32[]{:S(2)}, u32[]{:S(2)}) collective-permute-start(bf16[128,1024]{1,0:T(8,128)(2,1)S(1)} %shard_map.294.refs_0_), channel_id=1, source_target_pairs={{0,24},{1,97},{8,0},{9,105},{16,8},{17,113},{24,16},{25,121},{32,5... | collective-permute-start | bytes 786440 | tf_op jit(solution)/shard_map/ppermute | solution.py:103
  (255 other events, 1674.5 us)
Sparse Core Ops, SparseCore 0:
  11.8 74.7 all-gather.6
  89.3 46.0 all-gather.8
  137.5 46.3 all-gather.12
  185.5 38.5 all-gather.10
  225.6 34.6 all-gather.14
  288.5 36.2 reduce-scatter.3
  354.4 36.0 all-gather.16
  392.9 55.4 reduce-scatter.5
  467.6 62.0 reduce-scatter.7

commit v4 on v3

--- a/solution.py
+++ b/solution.py
@@ -776,10 +776,10 @@
     def of_slots(values):
         return jnp.einsum("st,td->sd", pick_all, values, preferred_element_type=F32).astype(BF16)
 
-    start_rows = jnp.einsum(
-        "st,td->sd", pick, jnp.concatenate([inputs, cotangent], axis=1), precision=HIGHEST
-    )
-    start_round = sum_near(sum_core(after(start_rows, heads_dense), F32))
+    start_rows = dot_f32(
+        "st,td->sd", pick.astype(BF16), jnp.concatenate([inputs, cotangent], axis=1).astype(BF16)
+    )
+    start_round = sum_near(sum_core(after(start_rows, heads_dense)))
     projected = qkv_forward(normed_low, heads_dense)
     mixed_low, mixed_line, log_total = attend(
         projected, order, segments_all, *start_round[0]

time: 589 us -> 585 us (level)
  starting transfers between devices: 145 us -> 137 us
  local copies, waits for them, and re-layouts: 45.1 us -> 51.6 us
    unnamed x363 -> x393, local copies, waits for them, and re-layouts: 19.9 us -> 26.8 us
    ppermute x30, waiting for transfers between devices: 24.7 us -> 31 us  [turn(): return lax.ppermute(values, ('y', 'x', 'c'), pairs)]
    dot_general x34 -> x35, matrix products: 90.5 us -> 88.4 us  [dot_f32(): return jnp.einsum(pattern, left, right, preferred_element_type=F32)]
where the time goes in v4:
time: 585 us; the launch traced here: 574 us
  starting transfers between devices  137 us (23%)
  waiting for transfers between devices  116 us (20%)
  matrix products  114 us (19%)
  Pallas kernels  72 us (12%)
  other arithmetic  64 us (11%)
  local copies, waits for them, and re-layouts  51.6 us (9%)
  between operations  18.7 us (3%)
    dot_general x35, matrix products, dot_f32(): return jnp.einsum(pattern, left, right, preferred_element_type=F32)  88.4 us
    ppermute x41, starting transfers between devices, shift(): lax.ppermute(values, axis, [(i, (i + step) % size) for i in range(size)])  55 us
    ppermute x41, waiting for transfers between devices, shift(): lax.ppermute(values, axis, [(i, (i + step) % size) for i in range(size)])  44.8 us
    ppermute x30, starting transfers between devices, turn(): return lax.ppermute(values, ('y', 'x', 'c'), pairs)  31.4 us
    ppermute x30, waiting for transfers between devices, turn(): return lax.ppermute(values, ('y', 'x', 'c'), pairs)  31 us
    pallas_call x2, Pallas kernels, attend_back(): pl.pallas_call(functools.partial(skip_awaited, attend_back_kernel, 6, len...  29.7 us
    unnamed x393, local copies, waits for them, and re-layouts  26.8 us
    ppermute x24, starting transfers between devices, pair(): return lax.ppermute(values, axis, [(i, partner(i)) for i in range(4)])  25.1 us
  transfers between devices with their start and end apart: 107, of which 50 were waited for; matrix products, arithmetic and copies ran while one was open for 34% of the time, Pallas kernels for 12%

profile of v4, /device:TPU:1, one launch (start us, length us, event | category | flops | bytes accessed | tf_op | source)
XLA Modules:
  0.0 574.0 jit_solution(9959529353696720485)
XLA Ops:
  19.3 4.3 all-to-all-start
  27.4 7.1 %all-to-all-done = bf16[8,32,512]{2,1,0:T(8,128)(2,1)S(1)} async-done(((bf16[8,32,512]{2,1,0:T(8,128)(2,1)}), bf16[8,32,512]{2,1,0:T(8,128)(2,1)S(1)}, u32[]{:S(2)}, u32[]{:S(2)}) %all-to-all-start) | async-done | bytes 262176 | tf_op jit(solution)/shard_map/all_to_all | solution.py:430
  68.6 3.4 collective-permute-start.11
  83.0 22.6 %shard_map.282 = (bf16[2048,128]{1,0:T(8,128)(2,1)S(1)}, bf16[2048,128]{1,0:T(8,128)(2,1)S(1)}, f32[2,2048]{1,0:T(2,128)S(1)}) custom-call(s32[8]{0:T(128)S(1)} %fusion.201.refs_0_, bf16[2048,384]{1,0:T(8,128)(2,1)S(1)} %convolution_convert_fusion.refs_1_, f32[1,2048]{1,0:T(1,128)S(1)} %bitcast.284, f32[2048,1]{1,0:T(8,128)S(1)} %copy.61.refs_3_.refs_5_, ...), custom_call_target="tpu_custom_call" | custom-call | flops 2048 | bytes 2048 | tf_op jit(solution)/shard_map/pallas_call | solution.py:608
  110.1 3.7 collective-permute-done.15
  124.6 3.6 collective-permute-done.18.refs_1_
  142.3 3.8 all-to-all-start.1
  157.5 3.4 all-to-all-done.1
  195.0 5.9 %collective-permute-done.34.refs_3_ = bf16[256,256]{1,0:T(8,128)(2,1)S(1)} collective-permute-done((bf16[256,256]{1,0:T(8,128)(2,1)S(1)}, bf16[256,256]{1,0:T(8,128)(2,1)S(1)}, u32[]{:S(2)}, u32[]{:S(2)}) %collective-permute-start.34) | collective-permute-done | bytes 131104 | tf_op jit(solution)/shard_map/ppermute | solution.py:68
  203.1 3.7 collective-permute-done.32.refs_1_
  209.6 3.5 multiply_reduce_fusion.5
  222.6 8.5 %multiply_convert_fusion = (bf16[2048,512]{1,0:T(8,128)(2,1)}, f32[2048,512]{1,0:T(8,128)}) fusion(bf16[2048,1024]{1,0:T(8,128)(2,1)} %all-gather.11.cloned.1.call-done, bf16[3,512,1024]{2,1,0:T(8,128)(2,1)} %all-gather.9.cloned.1.call-done), kind=kOutput, calls=%fused_computation.14 | convolution fusion | flops 2156920832 | bytes 11534336 | tf_op jit(solution)/shard_map/td,fd->tf/dot_general | solution.py:63
  232.9 7.5 %collective-permute-done.44 = bf16[64,1024]{1,0:T(8,128)(2,1)S(1)} collective-permute-done((bf16[64,1024]{1,0:T(8,128)(2,1)S(1)}, bf16[64,1024]{1,0:T(8,128)(2,1)S(1)}, u32[]{:S(2)}, u32[]{:S(2)}) %collective-permute-start.44) | collective-permute-done | bytes 131104 | tf_op jit(solution)/shard_map/ppermute | solution.py:72
  251.3 6.3 %all-gather.15.cloned.1.call-done = bf16[2048,1024]{1,0:T(8,128)(2,1)} async-done(((bf16[256,1024]{1,0:T(8,128)(2,1)}), bf16[2048,1024]{1,0:T(8,128)(2,1)}) %all-gather.15.cloned.1.call-update) | async-done | bytes 4194320 | tf_op jit(solution)/shard_map/all_gather | solution.py:819
  257.6 8.7 %fusion.8 = bf16[2048,512]{1,0:T(8,128)(2,1)S(1)} fusion(f32[2048,512]{1,0:T(8,128)} %get-tuple-element.338, bf16[2048,1024]{1,0:T(8,128)(2,1)} %all-gather.15.cloned.1.call-done, bf16[3,512,1024]{2,1,0:T(8,128)(2,1)} %all-gather.9.cloned.1.call-done), kind=kOutput, calls=%fused_computation.12 | convolution fusion | flops 2168455168 | bytes 11534336 | tf_op jit(solution)/shard_map/td,fd->tf/dot_general | solution.py:63
  268.3 4.4 fusion.63
  288.5 6.7 %fusion.255 = f32[512,1024]{1,0:T(8,128)} fusion(bf16[2048,512]{1,0:T(8,128)(2,1)} %copy-done.192, bf16[2048,1024]{1,0:T(8,128)(2,1)} %all-gather.11.cloned.1.call-done), kind=kOutput, calls=%fused_computation.500 | convolution fusion | flops 2147483648 | bytes 8388608 | tf_op jit(solution)/shard_map/tf,td->fd/dot_general | solution.py:63
  298.6 3.7 fusion.256
  320.3 3.6 collective-permute-done.55
  326.5 5.8 %fusion.59 = f32[2048,1024]{1,0:T(8,128)} fusion(bf16[2048,512]{1,0:T(8,128)(2,1)S(1)} %copy-done.191, bf16[3,512,1024]{2,1,0:T(8,128)(2,1)S(1)} %copy-done.76), kind=kOutput, calls=%fused_computation.98 | convolution fusion | flops 2147483648 | bytes 11534336 | tf_op jit(solution)/shard_map/tf,fd->td/dot_general | solution.py:63
  350.7 3.3 fusion.25.values
  362.7 3.6 collective-permute-done.61.refs_2_
  366.3 5.6 collective-permute-done.62.refs_3_
  382.2 28.0 %shard_map.291 = (bf16[2048,384]{1,0:T(8,128)(2,1)S(1)}, bf16[2048,384]{1,0:T(8,128)(2,1)S(1)}) custom-call(s32[8]{0:T(128)S(1)} %copy-done.34, bf16[2048,384]{1,0:T(8,128)(2,1)S(1)} %copy-done.3, bf16[2048,128]{1,0:T(8,128)(2,1)S(1)} %add_convert_fusion.refs_2_, f32[2,2048]{1,0:T(2,128)S(1)} %copy-done.28, f32[1,2048]{1,0:T(1,128)S(1)} %bitcast.286, ...), custom_call_target="tpu_custom_call" | custom-call | flops 2048 | bytes 2048 | tf_op jit(solution)/shard_map/pallas_call | solution.py:630
  410.3 3.3 convert_add_fusion
  433.1 4.0 collective-permute-start.70
  438.9 5.6 fusion.87
  445.2 5.2 collective-permute-start.72
  468.6 4.1 collective-permute-done.76
  484.2 17.5 %all-to-all-start.2 = ((f32[128,8,128]{2,1,0:T(8,128)}), f32[128,8,128]{2,1,0:T(8,128)S(1)}, u32[]{:S(2)}, u32[]{:S(2)}) async-start(f32[128,8,128]{2,1,0:T(8,128)} %bitcast.85), calls=%async_computation.5 | async-start | bytes 1048576 | tf_op jit(solution)/shard_map/all_to_all | solution.py:991
  525.8 3.6 add_add_fusion.5
  561.3 3.5 collective-permute-done.92.refs_1_
  (851 shorter events, 347.8 us)
Async XLA Ops:
  7.2 126.4 %all-gather.7.cloned.1.call-start = ((), (), s32[]{:S(2)}) async-start(), calls=%async_computation.6 | async-start | bytes 4227072 | tf_op jit(solution)/shard_map/all_gather | solution.py:744
  13.9 20.6 %collective-permute-start = (bf16[256,1024]{1,0:T(8,128)(2,1)S(1)}, bf16[256,1024]{1,0:T(8,128)(2,1)S(1)}, u32[]{:S(2)}, u32[]{:S(2)}) collective-permute-start(bf16[256,1024]{1,0:T(8,128)(2,1)S(1)} %get-tuple-element.250), channel_id=1, source_target_pairs={{0,2},{2,4},{4,6},{6,0},{1,3},{3,5},{5,7},{7,1},{8,10},{10,12},{12... | collective-permute-start | bytes 1572872 | tf_op jit(solution)/shard_map/ppermute | solution.py:68
  16.3 18.1 %collective-permute-start.1 = (bf16[256,1024]{1,0:T(8,128)(2,1)S(1)}, bf16[256,1024]{1,0:T(8,128)(2,1)S(1)}, u32[]{:S(2)}, u32[]{:S(2)}) collective-permute-start(bf16[256,1024]{1,0:T(8,128)(2,1)S(1)} %get-tuple-element.250), channel_id=1, source_target_pairs={{0,6},{2,0},{4,2},{6,4},{1,7},{3,1},{5,3},{7,5},{8,14},{10,8},{12,... | collective-permute-start | bytes 1572872 | tf_op jit(solution)/shard_map/ppermute | solution.py:68
  19.3 15.1 %all-to-all-start = ((bf16[8,32,512]{2,1,0:T(8,128)(2,1)}), bf16[8,32,512]{2,1,0:T(8,128)(2,1)S(1)}, u32[]{:S(2)}, u32[]{:S(2)}) async-start(bf16[8,32,512]{2,1,0:T(8,128)(2,1)} %pad_maximum_fusion.9), calls=%async_computation | async-start | bytes 524288 | tf_op jit(solution)/shard_map/all_to_all | solution.py:430
  23.6 112.8 %all-gather.9.cloned.1.call-start = ((), (), s32[]{:S(2)}) async-start(), calls=%async_computation.7 | async-start | bytes 3342336 | tf_op jit(solution)/shard_map/all_gather | solution.py:736
  37.2 177.1 %all-gather.13.cloned.1.call-start = ((), (), s32[]{:S(2)}) async-start(), calls=%async_computation.9 | async-start | bytes 2228224 | tf_op jit(solution)/shard_map/all_gather | solution.py:747
  52.6 25.8 %collective-permute-start.7 = (bf16[1024,1024]{1,0:T(8,128)(2,1)S(1)}, bf16[1024,1024]{1,0:T(8,128)(2,1)}, u32[]{:S(2)}, u32[]{:S(2)}) collective-permute-start(bf16[1024,1024]{1,0:T(8,128)(2,1)S(1)} %shard_map.278.refs_0_), channel_id=1, source_target_pairs={{0,1},{1,0},{2,3},{3,2},{4,5},{5,4},{6,7},{7,6},{8,9},{9,8},{10,11... | collective-permute-start | bytes 6291464 | tf_op jit(solution)/shard_map/ppermute | solution.py:68
  75.6 30.6 %collective-permute-start.13 = (bf16[64,2048]{1,0:T(8,128)(2,1)S(1)}, bf16[64,2048]{1,0:T(8,128)(2,1)S(1)}, u32[]{:S(2)}, u32[]{:S(2)}) collective-permute-start(bf16[64,2048]{1,0:T(8,128)(2,1)S(1)} %get-tuple-element.282.refs_5_), channel_id=1, source_target_pairs={{0,6},{2,4},{4,2},{6,0},{1,7},{3,5},{5,3},{7,1},{8,14},{10,12},{12... | collective-permute-start | bytes 786440 | tf_op jit(solution)/shard_map/ppermute | solution.py:72
  78.4 27.8 %collective-permute-start.12 = (bf16[64,2048]{1,0:T(8,128)(2,1)S(1)}, bf16[64,2048]{1,0:T(8,128)(2,1)S(1)}, u32[]{:S(2)}, u32[]{:S(2)}) collective-permute-start(bf16[64,2048]{1,0:T(8,128)(2,1)S(1)} %get-tuple-element.283.refs_4_), channel_id=1, source_target_pairs={{0,2},{2,0},{4,6},{6,4},{1,3},{3,1},{5,7},{7,5},{8,10},{10,8},{12,... | collective-permute-start | bytes 786440 | tf_op jit(solution)/shard_map/ppermute | solution.py:72
  115.9 15.1 %collective-permute-start.17 = (bf16[128,2048]{1,0:T(8,128)(2,1)S(1)}, bf16[128,2048]{1,0:T(8,128)(2,1)}, u32[]{:S(2)}, u32[]{:S(2)}) collective-permute-start(bf16[128,2048]{1,0:T(8,128)(2,1)S(1)} %pad_maximum_fusion.6), channel_id=1, source_target_pairs={{0,1},{1,0},{2,3},{3,2},{4,5},{5,4},{6,7},{7,6},{8,9},{9,8},{10,11... | collective-permute-start | bytes 1572872 | tf_op jit(solution)/shard_map/ppermute | solution.py:68
  142.3 18.7 %all-to-all-start.1 = ((f32[128,8,128]{2,1,0:T(8,128)}), f32[128,8,128]{2,1,0:T(8,128)S(1)}, u32[]{:S(2)}, u32[]{:S(2)}) async-start(f32[128,8,128]{2,1,0:T(8,128)} %bitcast.308), calls=%async_computation.1 | async-start | bytes 1048576 | tf_op jit(solution)/shard_map/all_to_all | solution.py:769
  146.0 76.6 %all-gather.11.cloned.1.call-start = ((), (), s32[]{:S(2)}) async-start(), calls=%async_computation.8 | async-start | bytes 4718592 | tf_op jit(solution)/shard_map/all_gather | solution.py:818
  149.0 19.6 %collective-permute-start.27 = (bf16[64,1024]{1,0:T(8,128)(2,1)}, bf16[64,1024]{1,0:T(8,128)(2,1)}, u32[]{:S(2)}, u32[]{:S(2)}) collective-permute-start(bf16[64,1024]{1,0:T(8,128)(2,1)} %get-tuple-element.316), channel_id=1, source_target_pairs={{0,6},{2,4},{4,2},{6,0},{1,7},{3,5},{5,3},{7,1},{8,14},{10,12},{12... | collective-permute-start | bytes 393224 | tf_op jit(solution)/shard_map/ppermute | solution.py:72
  151.6 17.0 %collective-permute-start.26 = (bf16[64,1024]{1,0:T(8,128)(2,1)}, bf16[64,1024]{1,0:T(8,128)(2,1)}, u32[]{:S(2)}, u32[]{:S(2)}) collective-permute-start(bf16[64,1024]{1,0:T(8,128)(2,1)} %get-tuple-element.317), channel_id=1, source_target_pairs={{0,2},{2,0},{4,6},{6,4},{1,3},{3,1},{5,7},{7,5},{8,10},{10,8},{12,... | collective-permute-start | bytes 393224 | tf_op jit(solution)/shard_map/ppermute | solution.py:72
  173.9 83.7 %all-gather.15.cloned.1.call-start = ((), (), s32[]{:S(2)}) async-start(), calls=%async_computation.10 | async-start | bytes 4718592 | tf_op jit(solution)/shard_map/all_gather | solution.py:819
  187.5 159.2 %reduce-scatter.4.cloned.1.call-start = ((), (), s32[]{:S(2)}) async-start(), calls=%async_computation.11 | async-start | bytes 4718592 | tf_op jit(solution)/shard_map/reduce_scatter | solution.py:859
  249.1 17.2 %collective-permute-start.38 = (bf16[64,1024]{1,0:T(8,128)(2,1)S(1)}, bf16[64,1024]{1,0:T(8,128)(2,1)S(1)}, u32[]{:S(2)}, u32[]{:S(2)}) collective-permute-start(bf16[64,1024]{1,0:T(8,128)(2,1)S(1)} %get-tuple-element.308), channel_id=1, source_target_pairs={{0,6},{2,4},{4,2},{6,0},{1,7},{3,5},{5,3},{7,1},{8,14},{10,12},{12... | collective-permute-start | bytes 393224 | tf_op jit(solution)/shard_map/ppermute | solution.py:72
  250.7 15.6 %collective-permute-start.37 = (bf16[64,1024]{1,0:T(8,128)(2,1)S(1)}, bf16[64,1024]{1,0:T(8,128)(2,1)S(1)}, u32[]{:S(2)}, u32[]{:S(2)}) collective-permute-start(bf16[64,1024]{1,0:T(8,128)(2,1)S(1)} %get-tuple-element.309), channel_id=1, source_target_pairs={{0,2},{2,0},{4,6},{6,4},{1,3},{3,1},{5,7},{7,5},{8,10},{10,8},{12,... | collective-permute-start | bytes 393224 | tf_op jit(solution)/shard_map/ppermute | solution.py:72
  284.6 135.1 %all-gather.17.cloned.1.call-start = ((), (), s32[]{:S(2)}) async-start(), calls=%async_computation.13 | async-start | bytes 4718592 | tf_op jit(solution)/shard_map/all_gather | solution.py:922
  350.6 175.2 %reduce-scatter.6.cloned.1.call-start = ((), (), s32[]{:S(2)}) async-start(), calls=%async_computation.12 | async-start | bytes 9437184 | tf_op jit(solution)/shard_map/reduce_scatter | solution.py:929
  372.9 183.4 %reduce-scatter.8.cloned.1.call-start = ((), (), s32[]{:S(2)}) async-start(), calls=%async_computation.14 | async-start | bytes 9437184 | tf_op jit(solution)/shard_map/reduce_scatter | solution.py:975
  372.9 37.3 %collective-permute-start.63 = (bf16[512,1024]{1,0:T(8,128)(2,1)}, bf16[512,1024]{1,0:T(8,128)(2,1)}, u32[]{:S(2)}, u32[]{:S(2)}) collective-permute-start(bf16[512,1024]{1,0:T(8,128)(2,1)} %copy-done.37), channel_id=1, source_target_pairs={{0,8},{1,33},{8,16},{9,41},{16,24},{17,49},{24,0},{25,57},{32,40},... | collective-permute-start | bytes 3145736 | tf_op jit(solution)/shard_map/ppermute | solution.py:103
  374.0 36.3 %collective-permute-start.64 = (bf16[512,1024]{1,0:T(8,128)(2,1)}, bf16[512,1024]{1,0:T(8,128)(2,1)}, u32[]{:S(2)}, u32[]{:S(2)}) collective-permute-start(bf16[512,1024]{1,0:T(8,128)(2,1)} %copy-done.36), channel_id=1, source_target_pairs={{0,16},{1,65},{8,24},{9,73},{16,0},{17,81},{24,8},{25,89},{32,48},... | collective-permute-start | bytes 3145736 | tf_op jit(solution)/shard_map/ppermute | solution.py:103
  376.7 33.6 %collective-permute-start.65 = (bf16[512,1024]{1,0:T(8,128)(2,1)}, bf16[512,1024]{1,0:T(8,128)(2,1)}, u32[]{:S(2)}, u32[]{:S(2)}) collective-permute-start(bf16[512,1024]{1,0:T(8,128)(2,1)} %copy-done.35), channel_id=1, source_target_pairs={{0,24},{1,97},{8,0},{9,105},{16,8},{17,113},{24,16},{25,121},{32,5... | collective-permute-start | bytes 3145736 | tf_op jit(solution)/shard_map/ppermute | solution.py:103
  431.5 20.9 %collective-permute-start.73 = (bf16[320,1024]{1,0:T(8,128)(2,1)}, bf16[320,1024]{1,0:T(8,128)(2,1)}, u32[]{:S(2)}, u32[]{:S(2)}) collective-permute-start(bf16[320,1024]{1,0:T(8,128)(2,1)} %get-tuple-element.181), channel_id=1, source_target_pairs={{0,8},{1,33},{8,16},{9,41},{16,24},{17,49},{24,0},{25,57},{32,40},... | collective-permute-start | bytes 1966088 | tf_op jit(solution)/shard_map/ppermute | solution.py:103
  432.4 20.0 %collective-permute-start.74 = (bf16[320,1024]{1,0:T(8,128)(2,1)S(1)}, bf16[320,1024]{1,0:T(8,128)(2,1)}, u32[]{:S(2)}, u32[]{:S(2)}) collective-permute-start(bf16[320,1024]{1,0:T(8,128)(2,1)S(1)} %get-tuple-element.182), channel_id=1, source_target_pairs={{0,16},{1,65},{8,24},{9,73},{16,0},{17,81},{24,8},{25,89},{32,48},... | collective-permute-start | bytes 1966088 | tf_op jit(solution)/shard_map/ppermute | solution.py:103
  437.9 14.5 %collective-permute-start.75 = (bf16[320,1024]{1,0:T(8,128)(2,1)S(1)}, bf16[320,1024]{1,0:T(8,128)(2,1)}, u32[]{:S(2)}, u32[]{:S(2)}) collective-permute-start(bf16[320,1024]{1,0:T(8,128)(2,1)S(1)} %get-tuple-element.183), channel_id=1, source_target_pairs={{0,24},{1,97},{8,0},{9,105},{16,8},{17,113},{24,16},{25,121},{32,5... | collective-permute-start | bytes 1966088 | tf_op jit(solution)/shard_map/ppermute | solution.py:103
  476.9 25.6 %collective-permute-start.81 = (bf16[32,1024]{1,0:T(8,128)(2,1)S(1)}, bf16[32,1024]{1,0:T(8,128)(2,1)S(1)}, u32[]{:S(2)}, u32[]{:S(2)}) collective-permute-start(bf16[32,1024]{1,0:T(8,128)(2,1)S(1)} %get-tuple-element.257), channel_id=1, source_target_pairs={{0,96},{1,25},{8,104},{9,1},{16,112},{17,9},{24,120},{25,17},{32,0... | collective-permute-start | bytes 196616 | tf_op jit(solution)/shard_map/ppermute | solution.py:103
  478.4 24.2 %collective-permute-start.80 = (bf16[32,1024]{1,0:T(8,128)(2,1)S(1)}, bf16[32,1024]{1,0:T(8,128)(2,1)S(1)}, u32[]{:S(2)}, u32[]{:S(2)}) collective-permute-start(bf16[32,1024]{1,0:T(8,128)(2,1)S(1)} %get-tuple-element.258), channel_id=1, source_target_pairs={{0,64},{1,17},{8,72},{9,25},{16,80},{17,1},{24,88},{25,9},{32,96},... | collective-permute-start | bytes 196616 | tf_op jit(solution)/shard_map/ppermute | solution.py:103
  478.4 24.2 %collective-permute-start.79 = (bf16[32,1024]{1,0:T(8,128)(2,1)S(1)}, bf16[32,1024]{1,0:T(8,128)(2,1)S(1)}, u32[]{:S(2)}, u32[]{:S(2)}) collective-permute-start(bf16[32,1024]{1,0:T(8,128)(2,1)S(1)} %get-tuple-element.259), channel_id=1, source_target_pairs={{0,32},{1,9},{8,40},{9,17},{16,48},{17,25},{24,56},{25,1},{32,64},... | collective-permute-start | bytes 196616 | tf_op jit(solution)/shard_map/ppermute | solution.py:103
  484.2 32.3 %all-to-all-start.2 = ((f32[128,8,128]{2,1,0:T(8,128)}), f32[128,8,128]{2,1,0:T(8,128)S(1)}, u32[]{:S(2)}, u32[]{:S(2)}) async-start(f32[128,8,128]{2,1,0:T(8,128)} %bitcast.85), calls=%async_computation.5 | async-start | bytes 1048576 | tf_op jit(solution)/shard_map/all_to_all | solution.py:991
  512.8 16.6 %collective-permute-start.90 = (bf16[128,1024]{1,0:T(8,128)(2,1)S(1)}, bf16[128,1024]{1,0:T(8,128)(2,1)S(1)}, u32[]{:S(2)}, u32[]{:S(2)}) collective-permute-start(bf16[128,1024]{1,0:T(8,128)(2,1)S(1)} %shard_map.294.refs_0_), channel_id=1, source_target_pairs={{0,24},{1,97},{8,0},{9,105},{16,8},{17,113},{24,16},{25,121},{32,5... | collective-permute-start | bytes 786440 | tf_op jit(solution)/shard_map/ppermute | solution.py:103
  (271 other events, 1703.8 us)
Sparse Core Ops, SparseCore 0:
  11.8 72.1 all-gather.6
  86.7 45.0 all-gather.8
  134.0 46.3 all-gather.12
  181.9 38.5 all-gather.10
  222.1 35.4 all-gather.14
  284.8 36.9 reduce-scatter.3
  350.7 36.3 all-gather.16
  389.5 56.4 reduce-scatter.5
  463.8 61.4 reduce-scatter.7
